TPU v7x, 32 devices: a whole 2x2x4 slice. The times are simulated.
32 devices in a mesh: group: 2 (over y), col: 4 (over z), row: 2 (over x), section: 2 (over core).
Axes of the slice: x: 2, y: 2, z: 4, core: 2. Of those that a mesh axis runs over, the one named last changes fastest.
Arguments:
- tokens: bfloat16 [2, 256, 8192], P(None, ('group', 'col'), 'row'), parts along dimension 1, may hold values from -12 to 12, as said below
- norm_gain: float32 [2, 8192], P('section', 'row'), may hold values from 0.5 to 1.5
- w_gate: bfloat16 [2, 8192, 14336], P('section', 'row', 'col'), may hold values from -0.0625 to 0.0625
- w_up: bfloat16 [2, 8192, 14336], P('section', 'row', 'col'), may hold values from -0.0625 to 0.0625
- w_down: bfloat16 [2, 14336, 8192], P('section', 'col', 'row'), may hold values from -0.046875 to 0.046875
Outputs:
- block_out: bfloat16 [2, 2, 256, 8192], P('section', None, ('group', 'col'), 'row'), parts along dimension 2
There are 2 independent parts, one for each index of `group`. A program takes and returns all parts, laid end to end along the dimension named above; an argument that names none is the same for every part. Nothing has to cross between parts.
Inputs may be any that keep to these rules, and one draw needn't show every extreme that they name: `tokens`: dense real activations.
All inputs are finite; a program needn't handle non-finite values.
Results may differ from a plain program's by a relative error of at most 0.024.
Values may be sent and summed in bfloat16 or wider, within the bound.
No kernel may reach another device: no remote copies, remote signals or barrier semaphores. Data moves between devices by JAX's collectives and lax.ppermute only.
A program may use at most 128 MiB of HBM per device.

v0:
```python
import jax
import jax.numpy as jnp
from jax import lax
from jax.sharding import PartitionSpec as P

D = 8192


EPS = 1e-05


def from_behind(value, axis, steps):
    count = lax.axis_size(axis)
    initial, last = (max(0, -steps), min(count, count - steps))
    return lax.ppermute(value, axis, [(source, source + steps) for source in range(initial, last)])


def on_device(tokens, norm_gain, w_gate, w_up, w_down):
    section_index = lax.axis_index("section")
    is_first = section_index == 0
    gain = norm_gain[0]
    gate_tile = w_gate[0]
    up_tile = w_up[0]
    down_tile = w_down[0]
    micro, tok_col, width_row = tokens.shape
    hidden_cols = gate_tile.shape[1]
    results = []
    received = jnp.zeros((tok_col, width_row), jnp.bfloat16)
    for tick in range(micro + 1):
        fresh = tokens[tick] if tick < micro else jnp.zeros((tok_col, width_row), jnp.bfloat16)
        block_in = jnp.where(is_first, fresh, received)
        wide_in = block_in.astype(jnp.float32)
        sum_sq = lax.psum(jnp.sum(wide_in * wide_in, axis=1), "row")
        wide = block_in.astype(jnp.float32)
        scale = lax.rsqrt(sum_sq / D + EPS)
        normed = (wide * scale[:, None] * gain[None, :]).astype(jnp.bfloat16)
        normed_rows = lax.all_gather(normed, "col", axis=0, tiled=True)
        gate_part = jnp.dot(normed_rows, gate_tile, preferred_element_type=jnp.float32)
        up_part = jnp.dot(normed_rows, up_tile, preferred_element_type=jnp.float32)
        pair = jnp.concatenate([gate_part, up_part], axis=1)
        share = lax.psum_scatter(
            pair.astype(jnp.bfloat16), "row", scatter_dimension=0, tiled=True
        ).astype(jnp.float32)
        hidden_share = (jax.nn.silu(share[:, :hidden_cols]) * share[:, hidden_cols:]).astype(
            jnp.bfloat16
        )
        hidden = lax.all_gather(hidden_share, "row", axis=0, tiled=True)
        ffn = lax.psum_scatter(
            jnp.dot(hidden, down_tile, preferred_element_type=jnp.float32).astype(jnp.bfloat16),
            "col",
            scatter_dimension=0,
            tiled=True,
        ).astype(jnp.float32)
        result = (wide_in + ffn).astype(jnp.bfloat16)
        results.append(result)
        if tick < micro:
            received = from_behind(result, "section", 1)
    early = jnp.stack(results[:micro], axis=0)
    late = jnp.stack(results[1:], axis=0)
    return jnp.where(is_first, early, late)[None]


def solution(mesh):
    placed = (
        P(None, ("group", "col"), "row"),
        P("section", "row"),
        P("section", "row", "col"),
        P("section", "row", "col"),
        P("section", "col", "row"),
    )
    return jax.shard_map(
        on_device,
        mesh=mesh,
        in_specs=placed,
        out_specs=P("section", None, ("group", "col"), "row"),
        check_vma=False,
    )
```

profile of v0, /device:TPU:1, one launch (start us, length us, event | category | flops | bytes accessed | tf_op | source)
XLA Modules:
  0.0 455.6 jit_solution(14409287867418705781)
XLA Ops:
  6.5 1.1 fusion.56
  7.7 4.4 psum.21
  12.0 1.8 fusion.58
  13.9 30.6 %all-gather.4.cloned.1.call-done = bf16[128,4096]{1,0:T(8,128)(2,1)} async-done(((bf16[32,4096]{1,0:T(8,128)(2,1)}), bf16[128,4096]{1,0:T(8,128)(2,1)}) %all-gather.4.cloned.1.call-update) | async-done | bytes 1048592 | tf_op jit(solution)/shard_map/all_gather | solution.py:37
  44.5 13.7 %fusion.27 = bf16[128,3584]{1,0:T(8,128)(2,1)S(1)} fusion(bf16[128,4096]{1,0:T(8,128)(2,1)} %all-gather.4.cloned.1.call-done, bf16[1,4096,3584]{2,1,0:T(8,128)(2,1)} %param.8), kind=kOutput, calls=%fused_computation.21 | convolution fusion | flops 3758555136 | bytes 31326208 | tf_op jit(solution)/shard_map/dot_general | solution.py:39
  58.2 11.6 %fusion.18 = bf16[128,3584]{1,0:T(8,128)(2,1)S(1)} fusion(bf16[128,4096]{1,0:T(8,128)(2,1)S(1)} %copy-done, bf16[1,4096,3584]{2,1,0:T(8,128)(2,1)} %param.7), kind=kOutput, calls=%fused_computation.18 | convolution fusion | flops 3758555136 | bytes 31326208 | tf_op jit(solution)/shard_map/dot_general | solution.py:38
  69.8 1.4 pad_maximum_fusion
  71.3 28.7 %reduce-scatter.7.cloned.1.call-done = bf16[64,7168]{1,0:T(8,128)(2,1)} async-done(((bf16[128,7168]{1,0:T(8,128)(2,1)}), bf16[64,7168]{1,0:T(8,128)(2,1)}) %reduce-scatter.7.cloned.1.call-update) | async-done | bytes 917520 | tf_op jit(solution)/shard_map/reduce_scatter | solution.py:41
  100.0 1.3 convert_element_type.75
  101.3 0.2 fusion.47
  101.6 12.1 %all_gather.19 = bf16[128,3584]{1,0:T(8,128)(2,1)S(1)} all-gather(bf16[64,3584]{1,0:T(8,128)(2,1)S(1)} %fusion.47), channel_id=1, replica_groups=mesh['group'=2,'col'=4,'row'=2,'section'=2] {'row'}, dimensions={0}, use_global_device_ids=true | all-gather | bytes 1376256 | tf_op jit(solution)/shard_map/all_gather | solution.py:47
  113.6 12.6 %fusion.36 = bf16[128,4096]{1,0:T(8,128)(2,1)} fusion(bf16[128,3584]{1,0:T(8,128)(2,1)S(1)} %all_gather.19, bf16[1,3584,4096]{2,1,0:T(8,128)(2,1)} %param.9), kind=kOutput, calls=%fused_computation.24 | convolution fusion | flops 3758620672 | bytes 31326208 | tf_op jit(solution)/shard_map/dot_general | solution.py:49
  126.3 27.9 %reduce-scatter.9.cloned.1.call-done = bf16[32,4096]{1,0:T(8,128)(2,1)} async-done(((bf16[128,4096]{1,0:T(8,128)(2,1)}), bf16[32,4096]{1,0:T(8,128)(2,1)}) %reduce-scatter.9.cloned.1.call-update) | async-done | bytes 262160 | tf_op jit(solution)/shard_map/reduce_scatter | solution.py:48
  154.3 1.0 fusion.59
  155.3 1.3 collective-permute-start
  156.6 2.1 collective-permute-done
  158.7 0.2 fusion.48
  158.9 3.8 psum.22
  162.7 0.8 fusion.50
  163.6 0.2 reduce-scatter.11.cloned.1.call-start
  163.8 27.2 %all-gather.6.cloned.1.call-done = bf16[128,4096]{1,0:T(8,128)(2,1)} async-done(((bf16[32,4096]{1,0:T(8,128)(2,1)}), bf16[128,4096]{1,0:T(8,128)(2,1)}) %all-gather.6.cloned.1.call-update) | async-done | bytes 1048592 | tf_op jit(solution)/shard_map/all_gather | solution.py:37
  191.0 13.7 %fusion.30 = bf16[128,3584]{1,0:T(8,128)(2,1)S(1)} fusion(bf16[128,4096]{1,0:T(8,128)(2,1)} %all-gather.6.cloned.1.call-done, bf16[1,4096,3584]{2,1,0:T(8,128)(2,1)} %param.8), kind=kOutput, calls=%fused_computation.22 | convolution fusion | flops 3758555136 | bytes 31326208 | tf_op jit(solution)/shard_map/dot_general | solution.py:39
  204.8 11.6 %fusion.21 = bf16[128,3584]{1,0:T(8,128)(2,1)S(1)} fusion(bf16[128,4096]{1,0:T(8,128)(2,1)S(1)} %copy-done.1, bf16[1,4096,3584]{2,1,0:T(8,128)(2,1)} %param.7), kind=kOutput, calls=%fused_computation.19 | convolution fusion | flops 3758555136 | bytes 31326208 | tf_op jit(solution)/shard_map/dot_general | solution.py:38
  216.4 1.4 pad_maximum_fusion.1
  217.9 28.7 %reduce-scatter.11.cloned.1.call-done = bf16[64,7168]{1,0:T(8,128)(2,1)} async-done(((bf16[128,7168]{1,0:T(8,128)(2,1)}), bf16[64,7168]{1,0:T(8,128)(2,1)}) %reduce-scatter.11.cloned.1.call-update) | async-done | bytes 917520 | tf_op jit(solution)/shard_map/reduce_scatter | solution.py:41
  246.6 1.3 convert_element_type.82
  247.9 0.2 fusion.46
  248.1 12.1 %all_gather.21 = bf16[128,3584]{1,0:T(8,128)(2,1)S(1)} all-gather(bf16[64,3584]{1,0:T(8,128)(2,1)S(1)} %fusion.46), channel_id=1, replica_groups=mesh['group'=2,'col'=4,'row'=2,'section'=2] {'row'}, dimensions={0}, use_global_device_ids=true | all-gather | bytes 1376256 | tf_op jit(solution)/shard_map/all_gather | solution.py:47
  260.2 12.5 %fusion.39 = bf16[128,4096]{1,0:T(8,128)(2,1)} fusion(bf16[128,3584]{1,0:T(8,128)(2,1)S(1)} %all_gather.21, bf16[1,3584,4096]{2,1,0:T(8,128)(2,1)} %param.9), kind=kOutput, calls=%fused_computation.25 | convolution fusion | flops 3758620672 | bytes 31326208 | tf_op jit(solution)/shard_map/dot_general | solution.py:49
  272.8 27.9 %reduce-scatter.13.cloned.1.call-done = bf16[32,4096]{1,0:T(8,128)(2,1)} async-done(((bf16[128,4096]{1,0:T(8,128)(2,1)}), bf16[32,4096]{1,0:T(8,128)(2,1)}) %reduce-scatter.13.cloned.1.call-update) | async-done | bytes 262160 | tf_op jit(solution)/shard_map/reduce_scatter | solution.py:48
  300.7 1.0 fusion.51
  301.8 1.3 collective-permute-start.1
  303.1 2.1 collective-permute-done.1
  305.4 3.8 psum.23
  309.2 0.8 fusion.54
  310.0 0.3 reduce-scatter.15.cloned.1.call-start
  310.3 27.2 %all-gather.8.cloned.1.call-done = bf16[128,4096]{1,0:T(8,128)(2,1)} async-done(((bf16[32,4096]{1,0:T(8,128)(2,1)}), bf16[128,4096]{1,0:T(8,128)(2,1)}) %all-gather.8.cloned.1.call-update) | async-done | bytes 1048592 | tf_op jit(solution)/shard_map/all_gather | solution.py:37
  337.4 13.7 %fusion.33 = bf16[128,3584]{1,0:T(8,128)(2,1)S(1)} fusion(bf16[128,4096]{1,0:T(8,128)(2,1)} %all-gather.8.cloned.1.call-done, bf16[1,4096,3584]{2,1,0:T(8,128)(2,1)} %param.8), kind=kOutput, calls=%fused_computation.23 | convolution fusion | flops 3758555136 | bytes 31326208 | tf_op jit(solution)/shard_map/dot_general | solution.py:39
  351.2 11.6 %fusion.24 = bf16[128,3584]{1,0:T(8,128)(2,1)S(1)} fusion(bf16[128,4096]{1,0:T(8,128)(2,1)S(1)} %copy-done.2, bf16[1,4096,3584]{2,1,0:T(8,128)(2,1)} %param.7), kind=kOutput, calls=%fused_computation.20 | convolution fusion | flops 3758555136 | bytes 31326208 | tf_op jit(solution)/shard_map/dot_general | solution.py:38
  362.8 1.4 pad_maximum_fusion.2
  364.3 28.7 %reduce-scatter.15.cloned.1.call-done = bf16[64,7168]{1,0:T(8,128)(2,1)} async-done(((bf16[128,7168]{1,0:T(8,128)(2,1)}), bf16[64,7168]{1,0:T(8,128)(2,1)}) %reduce-scatter.15.cloned.1.call-update) | async-done | bytes 917520 | tf_op jit(solution)/shard_map/reduce_scatter | solution.py:41
  393.0 1.3 convert_element_type.89
  394.3 0.2 fusion.45
  394.5 12.1 %all_gather.23 = bf16[128,3584]{1,0:T(8,128)(2,1)S(1)} all-gather(bf16[64,3584]{1,0:T(8,128)(2,1)S(1)} %fusion.45), channel_id=1, replica_groups=mesh['group'=2,'col'=4,'row'=2,'section'=2] {'row'}, dimensions={0}, use_global_device_ids=true | all-gather | bytes 1376256 | tf_op jit(solution)/shard_map/all_gather | solution.py:47
  406.6 12.5 %fusion.42 = bf16[128,4096]{1,0:T(8,128)(2,1)} fusion(bf16[128,3584]{1,0:T(8,128)(2,1)S(1)} %all_gather.23, bf16[1,3584,4096]{2,1,0:T(8,128)(2,1)} %param.9), kind=kOutput, calls=%fused_computation.26 | convolution fusion | flops 3758620672 | bytes 31326208 | tf_op jit(solution)/shard_map/dot_general | solution.py:49
  419.2 28.0 %reduce-scatter.17.cloned.1.call-done = bf16[32,4096]{1,0:T(8,128)(2,1)} async-done(((bf16[128,4096]{1,0:T(8,128)(2,1)}), bf16[32,4096]{1,0:T(8,128)(2,1)}) %reduce-scatter.17.cloned.1.call-update) | async-done | bytes 262160 | tf_op jit(solution)/shard_map/reduce_scatter | solution.py:48
  447.2 1.0 fusion.60
  448.2 0.9 maximum_select_fusion
  (30 shorter events, 0.6 us)
Async XLA Ops:
  6.5 37.9 %all-gather.4.cloned.1.call-start = ((), (), s32[]{:S(2)}) async-start(), calls=%async_computation.6 | async-start | bytes 1310720 | tf_op jit(solution)/shard_map/all_gather | solution.py:37
  13.8 86.2 %reduce-scatter.7.cloned.1.call-start = ((), (), s32[]{:S(2)}) async-start(), calls=%async_computation.7 | async-start | bytes 2752512 | tf_op jit(solution)/shard_map/reduce_scatter | solution.py:41
  44.5 13.7 %copy-start = (bf16[128,4096]{1,0:T(8,128)(2,1)S(1)}, bf16[128,4096]{1,0:T(8,128)(2,1)}, u32[]{:S(2)}) copy-start(bf16[128,4096]{1,0:T(8,128)(2,1)} %all-gather.4.cloned.1.call-done) | copy-start | bytes 3145732
  71.3 83.0 %reduce-scatter.9.cloned.1.call-start = ((), (), s32[]{:S(2)}) async-start(), calls=%async_computation.8 | async-start | bytes 1310720 | tf_op jit(solution)/shard_map/reduce_scatter | solution.py:48
  113.6 40.6 %copy-start.3 = (bf16[2,32,4096]{2,1,0:T(8,128)(2,1)S(1)}, bf16[2,32,4096]{2,1,0:T(8,128)(2,1)}, u32[]{:S(2)}) copy-start(bf16[2,32,4096]{2,1,0:T(8,128)(2,1)} %param.5) | copy-start | bytes 1572868
  113.6 49.1 %copy-start.4 = (f32[1,4096]{1,0:T(1,128)S(1)}, f32[1,4096]{1,0:T(1,128)}, u32[]{:S(2)}) copy-start(f32[1,4096]{1,0:T(1,128)} %param.6) | copy-start | bytes 49156
  126.3 64.8 %all-gather.6.cloned.1.call-start = ((), (), s32[]{:S(2)}) async-start(), calls=%async_computation.9 | async-start | bytes 1310720 | tf_op jit(solution)/shard_map/all_gather | solution.py:37
  155.3 3.4 collective-permute-start
  163.6 83.0 %reduce-scatter.11.cloned.1.call-start = ((), (), s32[]{:S(2)}) async-start(), calls=%async_computation.10 | async-start | bytes 2752512 | tf_op jit(solution)/shard_map/reduce_scatter | solution.py:41
  191.0 13.7 %copy-start.1 = (bf16[128,4096]{1,0:T(8,128)(2,1)S(1)}, bf16[128,4096]{1,0:T(8,128)(2,1)}, u32[]{:S(2)}) copy-start(bf16[128,4096]{1,0:T(8,128)(2,1)} %all-gather.6.cloned.1.call-done) | copy-start | bytes 3145732
  217.8 82.9 %reduce-scatter.13.cloned.1.call-start = ((), (), s32[]{:S(2)}) async-start(), calls=%async_computation.11 | async-start | bytes 1310720 | tf_op jit(solution)/shard_map/reduce_scatter | solution.py:48
  272.8 64.7 %all-gather.8.cloned.1.call-start = ((), (), s32[]{:S(2)}) async-start(), calls=%async_computation.12 | async-start | bytes 1310720 | tf_op jit(solution)/shard_map/all_gather | solution.py:37
  301.8 3.4 collective-permute-start.1
  310.0 83.0 %reduce-scatter.15.cloned.1.call-start = ((), (), s32[]{:S(2)}) async-start(), calls=%async_computation.13 | async-start | bytes 2752512 | tf_op jit(solution)/shard_map/reduce_scatter | solution.py:41
  337.4 13.7 %copy-start.2 = (bf16[128,4096]{1,0:T(8,128)(2,1)S(1)}, bf16[128,4096]{1,0:T(8,128)(2,1)}, u32[]{:S(2)}) copy-start(bf16[128,4096]{1,0:T(8,128)(2,1)} %all-gather.8.cloned.1.call-done) | copy-start | bytes 3145732
  364.2 82.9 %reduce-scatter.17.cloned.1.call-start = ((), (), s32[]{:S(2)}) async-start(), calls=%async_computation.14 | async-start | bytes 1310720 | tf_op jit(solution)/shard_map/reduce_scatter | solution.py:48
Sparse Core Ops, SparseCore 0:
  14.0 30.4 all-gather.3
  71.4 28.5 reduce-scatter.6
  126.4 27.8 reduce-scatter.8
  163.7 27.2 all-gather.5
  217.9 28.5 reduce-scatter.10
  272.9 27.8 reduce-scatter.12
  310.1 27.2 all-gather.7
  364.4 28.5 reduce-scatter.14
  419.3 27.8 reduce-scatter.16
where the time goes:
time: 457 us; the launch traced here: 456 us
  waiting for transfers between devices  259 us (57%)
  matrix products  114 us (25%)
  blocking collectives  48.1 us (11%)
  other arithmetic  17.9 us (4%)
  between operations  13.4 us (3%)
    reduce_scatter x3, waiting for transfers between devices, on_device(): lax.psum_scatter(pair.astype(jnp.bfloat16), 'row', scatter_dimension=0, t...  86.1 us
    all_gather x3, waiting for transfers between devices, on_device(): normed_rows = lax.all_gather(normed, 'col', axis=0, tiled=True)  84.9 us
    reduce_scatter x3, waiting for transfers between devices, on_device(): lax.psum_scatter(jnp.dot(hidden, down_tile, preferred_element_type=jnp.fl...  83.9 us
    dot_general x3, matrix products, on_device(): up_part = jnp.dot(normed_rows, up_tile, preferred_element_type=jnp.float32)  41.2 us
    dot_general x3, matrix products, on_device(): jnp.dot(hidden, down_tile, preferred_element_type=jnp.float32)  37.7 us
    all_gather x3, blocking collectives, on_device(): hidden = lax.all_gather(hidden_share, 'row', axis=0, tiled=True)  36.2 us
    dot_general x3, matrix products, on_device(): jnp.dot(normed_rows, gate_tile, preferred_element_type=jnp.float32)  34.8 us
    psum x3, blocking collectives, on_device(): sum_sq = lax.psum(jnp.sum(wide_in * wide_in, axis=1), 'row')  11.9 us
  transfers between devices with their start and end apart: 11, of which 11 were waited for; matrix products, arithmetic and copies ran while one was open for 0% of the time, Pallas kernels for 0%

commit v1 on v0

v1 whole, which is shorter than its diff:
```python
import jax
import jax.numpy as jnp
from jax import lax
from jax.experimental import pallas as pl
from jax.experimental.pallas import tpu as pltpu
from jax.sharding import PartitionSpec as P

EPS = 1e-05
MIB = 1 << 20
LANES = 128
BUFFERS = 3
VMEM_MIB = 12
PIECES = 8
AXES = ("group", "col", "row", "section")

f32 = jnp.float32
bf16 = jnp.bfloat16


def tile_of(width):
    for tile in (512, 256, 128):
        if width % tile == 0:
            return tile
    return width


def in_vmem(value):
    return pltpu.with_memory_space_constraint(value, pltpu.VMEM)


def in_hbm(value):
    return pltpu.with_memory_space_constraint(value, pltpu.HBM)


VMEM_SPEC = pl.BlockSpec(memory_space=pltpu.VMEM)
HBM_SPEC = pl.BlockSpec(memory_space=pltpu.HBM)
ANY_SPEC = pl.BlockSpec(memory_space=pl.ANY)


class Routes:
    def __init__(self, sizes):
        self.sizes = sizes

    def index(self, place):
        index = 0
        for axis in AXES:
            index = index * self.sizes[axis] + place[axis]
        return index

    def places(self):
        for g in range(self.sizes["group"]):
            for c in range(self.sizes["col"]):
                for r in range(self.sizes["row"]):
                    for s in range(self.sizes["section"]):
                        yield dict(group=g, col=c, row=r, section=s)

    def shifted(self, place, axis, steps):
        return dict(place, **{axis: (place[axis] + steps) % self.sizes[axis]})

    def within(self, section, axis, steps):
        pairs = []
        for place in self.places():
            if place["section"] == section:
                target = self.shifted(place, axis, steps)
            else:
                target = self.shifted(place, "group", 1)
            pairs.append((self.index(place), self.index(target)))
        return pairs

    def onward(self, section, steps):
        pairs = []
        for place in self.places():
            if place["section"] == section:
                target = dict(self.shifted(place, "col", steps), section=section + 1)
            elif place["section"] == section + 1:
                target = dict(place, section=section)
            else:
                target = self.shifted(place, "group", 1)
            pairs.append((self.index(place), self.index(target)))
        return pairs


def streamed(count, parts, copy, body):
    def start(q):
        tile, part = (q // parts, q % parts) if isinstance(q, int) else (lax.div(q, parts), lax.rem(q, parts))
        copy(tile, part, q % BUFFERS if isinstance(q, int) else lax.rem(q, BUFFERS)).start()

    for q in range(min(BUFFERS, count * parts)):
        start(q)

    def step(i, carry):
        def use(part, f):
            q = i * parts + part
            slot = lax.rem(q, BUFFERS)
            copy(i, part, slot).wait()
            value = f(slot)

            @pl.when(q + BUFFERS < count * parts)
            def _():
                start(q + BUFFERS)

            return value

        body(i, use)
        return carry

    return lambda: lax.fori_loop(0, count, step, 0)


class Kernels:
    def __init__(self, n_row, n_col, w_gate, w_up, w_down):
        self.n_row, self.n_col = n_row, n_col
        self.w_up, self.w_down = w_up, w_down
        self.kept = []
        self.before = []
        self.depth, self.width = w_gate.shape[1:]
        self.half = self.depth // 2
        self.load(w_gate)

    def call(self, kernel, operands, specs, out_shape, scratch, vmem, flops, moved, name):
        extras = [in_vmem(v) for v in self.kept] + self.before
        n_kept, n = len(self.kept), len(extras)

        def wrapped(*refs):
            kernel(refs[:n_kept], *refs[n:])

        outs = pl.pallas_call(
            wrapped,
            out_shape=out_shape,
            in_specs=[VMEM_SPEC] * n_kept + [ANY_SPEC] * (n - n_kept) + specs,
            out_specs=[VMEM_SPEC] * len(out_shape),
            scratch_shapes=scratch,
            compiler_params=pltpu.CompilerParams(vmem_limit_bytes=vmem * MIB),
            cost_estimate=pl.CostEstimate(flops=flops, bytes_accessed=moved, transcendentals=0),
            name=name,
        )(*extras, *operands)
        self.before = [outs[-1]]
        return outs

    def load(self, w_gate):
        rows = self.depth // PIECES

        def kernel(_, gate_ref, *refs):
            outs, sem = refs[:-1], refs[-1]
            copies = [
                pltpu.make_async_copy(gate_ref.at[0, pl.ds(i * rows, rows)], out, sem.at[i])
                for i, out in enumerate(outs)
            ]
            for copy in copies:
                copy.start()
            for copy in copies:
                copy.wait()

        self.kept = self.call(
            kernel,
            [in_hbm(w_gate)],
            [HBM_SPEC],
            [pltpu.VMEM((rows, self.width), bf16)] * PIECES,
            [pltpu.SemaphoreType.DMA((PIECES,))],
            1,
            0,
            2 * self.depth * self.width,
            "load",
        )
        self.before = []

    def gate_up(self, blocks, scaled_in, gain, start, size, tile):
        n_row, depth, half = self.n_row, self.depth, self.half
        opens = scaled_in is None
        n = len(blocks) if opens else 1
        rows = sum(b.shape[0] for b in blocks) if opens else scaled_in.shape[0]
        keep_rows = rows // n_row
        extra = LANES if opens else 0
        piece = depth // PIECES

        def scale_rows(block_refs, gain_ref, scaled, ssq):
            row = lax.axis_index("row")
            tok = block_refs[0].shape[0]
            per_piece = n // n_row
            for d, block in enumerate(block_refs):
                away = lax.rem(d // per_piece - row + n_row, n_row)
                place = pl.ds(pl.multiple_of((away * per_piece + d % per_piece) * tok, tok), tok)
                wide = block[...].astype(f32)
                scaled[place, :] = (wide * gain_ref[...]).astype(bf16)
                total = jnp.sum(wide * wide, axis=1, keepdims=True)
                ssq[place, :] = jnp.broadcast_to(total, (tok, LANES))

        def kernel(kept, *refs):
            sources, gain_ref, up_w, refs = refs[:n], refs[n], refs[n + 1], refs[n + 2 :]
            refs, (buf, sem) = refs[:-2], refs[-2:]
            keep, sends = refs[0], refs[1:n_row]

            def copy(i, part, slot):
                columns = pl.ds(pl.multiple_of(start + i * tile, LANES), tile)
                return pltpu.make_async_copy(
                    up_w.at[0, pl.ds(part * half, half), columns], buf.at[slot], sem.at[slot]
                )

            def body(i, use):
                offset = pl.multiple_of(i * tile, tile)
                columns = pl.ds(pl.multiple_of(start + offset, LANES), tile)

                def product(first, weights):
                    return jnp.dot(
                        scaled[:, first : first + weights.shape[0]], weights, preferred_element_type=f32
                    )

                gate = product(0, kept[0][:, columns])
                for p in range(1, PIECES):
                    gate = gate + product(p * piece, kept[p][:, columns])
                up = use(0, lambda slot: product(0, buf[slot]))
                up = up + use(1, lambda slot: product(half, buf[slot]))
                for part, base in ((gate, 0), (up, size)):
                    part = part.astype(bf16)
                    place = pl.ds(pl.multiple_of(base + offset, tile), tile)
                    keep[:, place] = part[:keep_rows]
                    for e, send in enumerate(sends, 1):
                        send[:, place] = part[e * keep_rows : (e + 1) * keep_rows]

            run = streamed(size // tile, 2, copy, body)
            if opens:
                scaled, ssq = refs[n_row:]
                scale_rows(sources, gain_ref, scaled, ssq)
                lane = lax.broadcasted_iota(jnp.int32, (keep_rows, LANES), 1)
                for e, send in enumerate(sends, 1):
                    total = ssq[pl.ds(e * keep_rows, keep_rows), :]
                    high = total.astype(bf16).astype(f32)
                    send[:, pl.ds(2 * size, LANES)] = jnp.where(
                        lane < LANES // 2, high, total - high
                    ).astype(bf16)
            else:
                scaled = sources[0]
            run()

        out_shape = [pltpu.VMEM((keep_rows, 2 * size), bf16)]
        out_shape += [jax.ShapeDtypeStruct((keep_rows, 2 * size + extra), bf16)] * (n_row - 1)
        if opens:
            out_shape += [pltpu.VMEM((rows, depth), bf16), pltpu.VMEM((rows, LANES), f32)]
        sources = list(blocks) if opens else [in_vmem(scaled_in)]
        return self.call(
            kernel,
            sources + [gain, in_hbm(self.w_up)],
            [VMEM_SPEC] * (n + 1) + [HBM_SPEC],
            out_shape,
            [
                pltpu.VMEM((BUFFERS, half, tile), bf16),
                pltpu.SemaphoreType.DMA((BUFFERS,)),
            ],
            VMEM_MIB,
            4 * rows * depth * size,
            2 * depth * size,
            "gate_up",
        )

    def hidden(self, keep, received, own, opens):
        rows, size = keep.shape[0], keep.shape[1] // 2
        n = len(received)
        features = self.depth * self.n_row

        def kernel(_, keep_ref, *refs):
            arrived, own_ref, out, scale_out = refs[:n], refs[n], refs[n + 1], refs[n + 2]
            if opens:
                total = own_ref[pl.ds(0, rows), 0:1]
                for ref in arrived:
                    tail = ref[:, pl.ds(2 * size, LANES)].astype(f32)
                    total = total + (tail[:, 0:1] + tail[:, LANES // 2 : LANES // 2 + 1])
                scale = lax.rsqrt(total / features + EPS)
            else:
                scale = own_ref[:, 0:1]
            scale_out[...] = jnp.broadcast_to(scale, (rows, LANES))
            gate = keep_ref[:, pl.ds(0, size)].astype(f32)
            up = keep_ref[:, pl.ds(size, size)].astype(f32)
            for ref in arrived:
                gate = gate + ref[:, pl.ds(0, size)].astype(f32)
                up = up + ref[:, pl.ds(size, size)].astype(f32)
            gate = gate * scale
            out[...] = (gate / (1.0 + jnp.exp(-gate)) * (up * scale)).astype(bf16)

        return self.call(
            kernel,
            [in_vmem(keep), *received, in_vmem(own)],
            [VMEM_SPEC] * (n + 2),
            [jax.ShapeDtypeStruct((rows, size), bf16), pltpu.VMEM((rows, LANES), f32)],
            [],
            4,
            0,
            2 * MIB,
            "hidden",
        )

    def down(self, pieces, start, size, acc):
        n_row, n_col = self.n_row, self.n_col
        keep_rows = pieces[0].shape[0]
        rows = keep_rows * n_row
        tok = rows // n_col
        columns = self.w_down.shape[2]
        tile = tile_of(columns)
        last = acc is not None

        def kernel(_, *refs):
            piece_refs, w_ref, refs = refs[:n_row], refs[n_row], refs[n_row + 1 :]
            if last:
                acc_ref, refs = refs[0], refs[1:]
            outs, (held, buf, sem) = refs[:-3], refs[-3:]
            row = lax.axis_index("row")

            def copy(i, _, slot):
                place = pl.ds(pl.multiple_of(i * tile, tile), tile)
                return pltpu.make_async_copy(
                    w_ref.at[0, pl.ds(start, size), place], buf.at[slot], sem.at[slot]
                )

            def body(i, use):
                place = pl.ds(pl.multiple_of(i * tile, tile), tile)
                part = use(0, lambda slot: jnp.dot(held[...], buf[slot], preferred_element_type=f32))
                if last:
                    part = (part + acc_ref[:, place]).astype(bf16)
                    for d, out in enumerate(outs):
                        out[:, place] = part[d * tok : (d + 1) * tok]
                else:
                    outs[0][:, place] = part

            run = streamed(columns // tile, 1, copy, body)
            for e, piece in enumerate(piece_refs):
                place = pl.multiple_of(lax.rem(row - e + n_row, n_row) * keep_rows, keep_rows)
                held[pl.ds(place, keep_rows), :] = piece[...]
            run()

        if last:
            out_shape = [jax.ShapeDtypeStruct((tok, columns), bf16)] * n_col
        else:
            out_shape = [pltpu.VMEM((rows, columns), f32)]
        return self.call(
            kernel,
            list(pieces) + [in_hbm(self.w_down)] + ([in_vmem(acc)] if last else []),
            [VMEM_SPEC] * n_row + [HBM_SPEC] + [VMEM_SPEC] * last,
            out_shape,
            [
                pltpu.VMEM((rows, size), bf16),
                pltpu.VMEM((BUFFERS, size, tile), bf16),
                pltpu.SemaphoreType.DMA((BUFFERS,)),
            ],
            VMEM_MIB,
            2 * rows * size * columns,
            2 * size * columns,
            "down",
        )


def solution(mesh):
    sizes = dict(mesh.shape)
    routes = Routes(sizes)
    n_col, n_row, n_section = sizes["col"], sizes["row"], sizes["section"]

    def move(value, pairs):
        return lax.ppermute(value, AXES, pairs)

    def on_device(tokens, norm_gain, w_gate, w_up, w_down):
        section_index = lax.axis_index("section")
        micro, tok, depth = tokens.shape
        width = w_gate.shape[2]
        tile = tile_of(width)
        cut = (width // tile + 1) // 2 * tile
        chunks = ((0, cut), (cut, width - cut))
        k = Kernels(n_row, n_col, w_gate, w_up, w_down)

        def gathered(section, block):
            if section == 0:
                return [block] + [move(block, routes.within(0, "col", d)) for d in range(1, n_col)]
            return [move(block, routes.onward(section - 1, d)) for d in range(n_col)]

        def exchanged(section, sends):
            return [move(v, routes.within(section, "row", e)) for e, v in enumerate(sends, 1)]

        class Job:
            def __init__(self, section, block):
                self.section = section
                self.blocks = gathered(section, block)

            def gate_up(self, c):
                if c == 0:
                    self.keep0, *sends, self.scaled, self.ssq = k.gate_up(
                        self.blocks, None, norm_gain, *chunks[0], tile
                    )
                    self.in0 = exchanged(self.section, sends)
                else:
                    self.keep1, *sends = k.gate_up(None, self.scaled, norm_gain, *chunks[1], tile)
                    self.in1 = exchanged(self.section, sends)

            def hidden(self, c):
                if c == 0:
                    out, self.scale = k.hidden(self.keep0, self.in0, self.ssq, True)
                    self.pieces0 = [out] + exchanged(self.section, [out] * (n_row - 1))
                else:
                    out, _ = k.hidden(self.keep1, self.in1, self.scale, False)
                    self.pieces1 = [out] + exchanged(self.section, [out] * (n_row - 1))

            def down(self, c):
                if c == 0:
                    (self.acc,) = k.down(self.pieces0, *chunks[0], None)
                else:
                    parts = k.down(self.pieces1, *chunks[1], self.acc)
                    arrived = [
                        move(parts[d], routes.within(self.section, "col", -d)) for d in range(1, n_col)
                    ]
                    total = parts[0].astype(f32)
                    for value in arrived:
                        total = total + value.astype(f32)
                    self.result = (self.blocks[0].astype(f32) + total).astype(bf16)

        current = [tokens[m] for m in range(micro)]
        outs = []
        for section in range(n_section):
            jobs = []
            for m in range(micro):
                block = current[m]
                if m and section == 0:
                    block, _ = lax.optimization_barrier((block, jobs[m - 1].blocks))
                jobs.append(Job(section, block))
            steps = ORDER if micro == 2 else [(j, w, c) for j in range(micro) for w in "ghd" for c in (0, 1)]
            uses = [step for step in steps if step[1] == "g"]
            for step in steps:
                j, what, c = step
                getattr(jobs[j], dict(g="gate_up", h="hidden", d="down")[what])(c)
                if section == n_section - 1 and step == uses[-1]:
                    k.kept = []
            current = [job.result for job in jobs]
            outs.append(jnp.stack(current, axis=0))
        out = outs[0]
        for section in range(1, n_section):
            out = jnp.where(section_index == section, outs[section], out)
        return out[None]

    placed = (
        P(None, ("group", "col"), "row"),
        P("section", "row"),
        P("section", "row", "col"),
        P("section", "row", "col"),
        P("section", "col", "row"),
    )
    return jax.shard_map(
        on_device,
        mesh=mesh,
        in_specs=placed,
        out_specs=P("section", None, ("group", "col"), "row"),
        check_vma=False,
    )


ORDER = [
    (0, "g", 0), (0, "g", 1), (1, "g", 0), (0, "h", 0), (0, "h", 1), (1, "g", 1),
    (0, "d", 0), (1, "h", 0), (0, "d", 1), (1, "h", 1), (1, "d", 0), (1, "d", 1),
]
```

time: 457 us -> 205 us (0.45)
  waiting for transfers between devices: 259 us -> 22.1 us
  Pallas kernels: 0 us -> 126 us
  matrix products: 114 us -> 0 us
  starting transfers between devices: 3.32 us -> 53.6 us
  blocking collectives: 48.1 us -> 0 us
  other arithmetic: 17.9 us -> 1.56 us
  between operations: 13.4 us -> 0.38 us
    reduce_scatter x6 -> x0, waiting for transfers between devices: 170 us -> none  [the longest x3 86.1 us: on_device(): lax.psum_scatter(pair.astype(jnp.bfloat16), 'row', scatter_dimension=0, t...]
    pallas_call x0 -> x25, Pallas kernels: none -> 126 us  [call(): pl.pallas_call(wrapped, out_shape=out_shape, in_specs=[VMEM_SPEC] * n_kep...]
    dot_general x9 -> x0, matrix products: 114 us -> none  [the longest x3 41.2 us: on_device(): up_part = jnp.dot(normed_rows, up_tile, preferred_element_type=jnp.float32)]
    all_gather x3 -> x0, waiting for transfers between devices: 84.9 us -> none  [on_device(): normed_rows = lax.all_gather(normed, 'col', axis=0, tiled=True)]
    ppermute x2 -> x42, starting transfers between devices: 2.58 us -> 53.6 us  [move(): return lax.ppermute(value, AXES, pairs)]
    all_gather x3 -> x0, blocking collectives: 36.2 us -> none  [on_device(): hidden = lax.all_gather(hidden_share, 'row', axis=0, tiled=True)]
    ppermute x2 -> x42, waiting for transfers between devices: 4.26 us -> 22.1 us  [move(): return lax.ppermute(value, AXES, pairs)]
    psum x3 -> x0, blocking collectives: 11.9 us -> none  [on_device(): sum_sq = lax.psum(jnp.sum(wide_in * wide_in, axis=1), 'row')]
  transfers between devices with their start and end apart: 11 -> 42, of which waited for: 11 -> 8; matrix products, arithmetic and copies ran while one was open for 0% -> 0% of each run, Pallas kernels for 0% -> 62%
where the time goes in v1:
time: 205 us
  Pallas kernels  126 us (61%)
  starting transfers between devices  53.6 us (26%)
  waiting for transfers between devices  22.1 us (11%)
    pallas_call x25, Pallas kernels, call(): pl.pallas_call(wrapped, out_shape=out_shape, in_specs=[VMEM_SPEC] * n_kep...  126 us
    ppermute x42, starting transfers between devices, move(): return lax.ppermute(value, AXES, pairs)  53.6 us
    ppermute x42, waiting for transfers between devices, move(): return lax.ppermute(value, AXES, pairs)  22.1 us
  transfers between devices with their start and end apart: 42, of which 8 were waited for; matrix products, arithmetic and copies ran while one was open for 0% of the time, Pallas kernels for 62%

profile of v1, /device:TPU:1, one launch (start us, length us, event | category | flops | bytes accessed | tf_op | source)
XLA Modules:
  0.0 204.6 jit_solution(653667983542789433)
XLA Ops:
  0.0 1.1 slice_bitcast_fusion
  1.1 2.1 %collective-permute-start = (bf16[32,4096]{1,0:T(8,128)(2,1)S(1)}, bf16[32,4096]{1,0:T(8,128)(2,1)S(1)}, u32[]{:S(2)}, u32[]{:S(2)}) collective-permute-start(bf16[32,4096]{1,0:T(8,128)(2,1)S(1)} %get-tuple-element.136.refs_8_), channel_id=1, source_target_pairs={{0,4},{1,17},{2,6},{3,19},{4,8},{5,21},{6,10},{7,23},{8,12},{9,25}... | collective-permute-start | bytes 786440 | tf_op jit(solution)/shard_map/ppermute | solution.py:356
  3.3 1.4 collective-permute-start.2
  4.7 9.5 %load.1 = (bf16[512,3584]{1,0:T(8,128)(2,1)S(1)}, bf16[512,3584]{1,0:T(8,128)(2,1)S(1)}, bf16[512,3584]{1,0:T(8,128)(2,1)S(1)}, bf16[512,3584]{1,0:T(8,128)(2,1)...) custom-call(bf16[1,4096,3584]{2,1,0:T(8,128)(2,1)} %refs_0_.1), custom_call_target="tpu_custom_call" | custom-call | bytes 29360128 | tf_op jit(solution)/shard_map/load/pallas_call | solution.py:127
  14.3 1.4 collective-permute-start.4
  15.8 8.2 %gate_up.8 = (bf16[64,4096]{1,0:T(8,128)(2,1)S(1)}, bf16[64,4224]{1,0:T(8,128)(2,1)S(1)}, bf16[128,4096]{1,0:T(8,128)(2,1)S(1)}, f32[128,128]{1,0:T(8,128)S(1)}) custom-call(bf16[512,3584]{1,0:T(8,128)(2,1)S(1)} %get-tuple-element.70.refs_0_, bf16[512,3584]{1,0:T(8,128)(2,1)S(1)} %get-tuple-element.71.refs_1_, ...), custom_call_target="tpu_custom_call" | custom-call | flops 4294967296 | bytes 16777216 | tf_op jit(solution)/shard_map/gate_up/pallas_call | solution.py:127
  24.0 1.4 collective-permute-start.6
  25.4 6.3 %gate_up.9 = (bf16[64,3072]{1,0:T(8,128)(2,1)S(1)}, bf16[64,3072]{1,0:T(8,128)(2,1)S(1)}) custom-call(bf16[512,3584]{1,0:T(8,128)(2,1)S(1)} %get-tuple-element.70.refs_0_, bf16[512,3584]{1,0:T(8,128)(2,1)S(1)} %get-tuple-element.71.refs_1_, bf16[512,3584]{1,0:T(8,128)(2,1)S(1)} %get-tuple-element.72.refs_2_, ...), custom_call_target="tpu_custom_call" | custom-call | flops 3221225472 | bytes 12582912 | tf_op jit(solution)/shard_map/gate_up/pallas_call | solution.py:127
  31.9 8.2 %gate_up.10 = (bf16[64,4096]{1,0:T(8,128)(2,1)S(1)}, bf16[64,4224]{1,0:T(8,128)(2,1)S(1)}, bf16[128,4096]{1,0:T(8,128)(2,1)S(1)}, f32[128,128]{1,0:T(8,128)S(1)}) custom-call(bf16[512,3584]{1,0:T(8,128)(2,1)S(1)} %get-tuple-element.70.refs_0_, bf16[512,3584]{1,0:T(8,128)(2,1)S(1)} %get-tuple-element.71.refs_1_, ...), custom_call_target="tpu_custom_call" | custom-call | flops 4294967296 | bytes 16777216 | tf_op jit(solution)/shard_map/gate_up/pallas_call | solution.py:127
  40.1 1.4 collective-permute-start.9
  42.5 1.4 collective-permute-start.10
  43.9 6.3 %gate_up.11 = (bf16[64,3072]{1,0:T(8,128)(2,1)S(1)}, bf16[64,3072]{1,0:T(8,128)(2,1)S(1)}) custom-call(bf16[512,3584]{1,0:T(8,128)(2,1)S(1)} %get-tuple-element.70.refs_0_, bf16[512,3584]{1,0:T(8,128)(2,1)S(1)} %get-tuple-element.71.refs_1_, bf16[512,3584]{1,0:T(8,128)(2,1)S(1)} %get-tuple-element.72.refs_2_, ...), custom_call_target="tpu_custom_call" | custom-call | flops 3221225472 | bytes 12582912 | tf_op jit(solution)/shard_map/gate_up/pallas_call | solution.py:127
  50.4 1.1 collective-permute-done.8.refs_10_
  51.5 6.9 %down.8.refs_8_.refs_12_ = f32[128,4096]{1,0:T(8,128)S(1)} custom-call(bf16[512,3584]{1,0:T(8,128)(2,1)S(1)} %get-tuple-element.70.refs_0_, bf16[512,3584]{1,0:T(8,128)(2,1)S(1)} %get-tuple-element.71.refs_1_, bf16[512,3584]{1,0:T(8,128)(2,1)S(1)} %get-tuple-element.72.refs_2_, bf16[512,3584]{1,0:T(8,128)(2,1)S(1)} %get-tuple-element.73.refs_3_, ...), custom_call_target="tpu_custom_call" | custom-call | flops 2147483648 | bytes 16777216 | tf_op jit(solution)/shard_map/down/pallas_call | solution.py:127
  58.9 5.9 %down.9 = (bf16[32,4096]{1,0:T(8,128)(2,1)S(1)}, bf16[32,4096]{1,0:T(8,128)(2,1)S(1)}, bf16[32,4096]{1,0:T(8,128)(2,1)S(1)}, bf16[32,4096]{1,0:T(8,128)(2,1)S(1)}) custom-call(bf16[512,3584]{1,0:T(8,128)(2,1)S(1)} %get-tuple-element.70.refs_0_, bf16[512,3584]{1,0:T(8,128)(2,1)S(1)} %get-tuple-element.71.refs_1_, ...), custom_call_target="tpu_custom_call" | custom-call | flops 1610612736 | bytes 12582912 | tf_op jit(solution)/shard_map/down/pallas_call | solution.py:127
  64.8 1.4 collective-permute-start.11
  66.3 1.4 collective-permute-start.13
  68.0 1.4 collective-permute-start.17
  70.1 2.8 %collective-permute-done.12 = bf16[32,4096]{1,0:T(8,128)(2,1)S(1)} collective-permute-done((bf16[32,4096]{1,0:T(8,128)(2,1)S(1)}, bf16[32,4096]{1,0:T(8,128)(2,1)S(1)}, u32[]{:S(2)}, u32[]{:S(2)}) %collective-permute-start.12) | collective-permute-done | bytes 262176 | tf_op jit(solution)/shard_map/ppermute | solution.py:356
  72.9 3.1 %collective-permute-done.13 = bf16[32,4096]{1,0:T(8,128)(2,1)S(1)} collective-permute-done((bf16[32,4096]{1,0:T(8,128)(2,1)S(1)}, bf16[32,4096]{1,0:T(8,128)(2,1)S(1)}, u32[]{:S(2)}, u32[]{:S(2)}) %collective-permute-start.13) | collective-permute-done | bytes 262176 | tf_op jit(solution)/shard_map/ppermute | solution.py:356
  76.1 12.3 %collective-permute-start.14 = (bf16[32,4096]{1,0:T(8,128)(2,1)S(1)}, bf16[32,4096]{1,0:T(8,128)(2,1)S(1)}, u32[]{:S(2)}, u32[]{:S(2)}) collective-permute-start(bf16[32,4096]{1,0:T(8,128)(2,1)S(1)} %add_convert_fusion.3), channel_id=1, source_target_pairs={{0,1},{1,0},{2,3},{3,2},{4,5},{5,4},{6,7},{7,6},{8,9},{9,8},{10,11... | collective-permute-start | bytes 786440 | tf_op jit(solution)/shard_map/ppermute | solution.py:356
  88.6 2.0 collective-permute-start.20
  90.6 6.9 %down.10.refs_8_.refs_12_ = f32[128,4096]{1,0:T(8,128)S(1)} custom-call(bf16[512,3584]{1,0:T(8,128)(2,1)S(1)} %get-tuple-element.70.refs_0_, bf16[512,3584]{1,0:T(8,128)(2,1)S(1)} %get-tuple-element.71.refs_1_, bf16[512,3584]{1,0:T(8,128)(2,1)S(1)} %get-tuple-element.72.refs_2_, bf16[512,3584]{1,0:T(8,128)(2,1)S(1)} %get-tuple-element.73.refs_3_, ...), custom_call_target="tpu_custom_call" | custom-call | flops 2147483648 | bytes 16777216 | tf_op jit(solution)/shard_map/down/pallas_call | solution.py:127
  97.5 5.9 %down.11 = (bf16[32,4096]{1,0:T(8,128)(2,1)S(1)}, bf16[32,4096]{1,0:T(8,128)(2,1)S(1)}, bf16[32,4096]{1,0:T(8,128)(2,1)S(1)}, bf16[32,4096]{1,0:T(8,128)(2,1)S(1)}) custom-call(bf16[512,3584]{1,0:T(8,128)(2,1)S(1)} %get-tuple-element.70.refs_0_, bf16[512,3584]{1,0:T(8,128)(2,1)S(1)} %get-tuple-element.71.refs_1_, ...), custom_call_target="tpu_custom_call" | custom-call | flops 1610612736 | bytes 12582912 | tf_op jit(solution)/shard_map/down/pallas_call | solution.py:127
  103.4 1.5 collective-permute-start.21
  104.9 1.4 collective-permute-start.23
  106.3 8.2 %gate_up.12 = (bf16[64,4096]{1,0:T(8,128)(2,1)S(1)}, bf16[64,4224]{1,0:T(8,128)(2,1)S(1)}, bf16[128,4096]{1,0:T(8,128)(2,1)S(1)}, f32[128,128]{1,0:T(8,128)S(1)}) custom-call(bf16[512,3584]{1,0:T(8,128)(2,1)S(1)} %get-tuple-element.70.refs_0_, bf16[512,3584]{1,0:T(8,128)(2,1)S(1)} %get-tuple-element.71.refs_1_, ...), custom_call_target="tpu_custom_call" | custom-call | flops 4294967296 | bytes 16777216 | tf_op jit(solution)/shard_map/gate_up/pallas_call | solution.py:127
  114.5 1.3 collective-permute-start.28
  116.0 2.6 %collective-permute-start.24 = (bf16[32,4096]{1,0:T(8,128)(2,1)S(1)}, bf16[32,4096]{1,0:T(8,128)(2,1)S(1)}, u32[]{:S(2)}, u32[]{:S(2)}) collective-permute-start(bf16[32,4096]{1,0:T(8,128)(2,1)S(1)} %add_convert_fusion.2), channel_id=1, source_target_pairs={{0,1},{1,0},{2,3},{3,2},{4,5},{5,4},{6,7},{7,6},{8,9},{9,8},{10,11... | collective-permute-start | bytes 786440 | tf_op jit(solution)/shard_map/ppermute | solution.py:356
  119.5 2.0 collective-permute-start.27
  121.4 6.3 %gate_up.13 = (bf16[64,3072]{1,0:T(8,128)(2,1)S(1)}, bf16[64,3072]{1,0:T(8,128)(2,1)S(1)}) custom-call(bf16[512,3584]{1,0:T(8,128)(2,1)S(1)} %get-tuple-element.70.refs_0_, bf16[512,3584]{1,0:T(8,128)(2,1)S(1)} %get-tuple-element.71.refs_1_, bf16[512,3584]{1,0:T(8,128)(2,1)S(1)} %get-tuple-element.72.refs_2_, ...), custom_call_target="tpu_custom_call" | custom-call | flops 3221225472 | bytes 12582912 | tf_op jit(solution)/shard_map/gate_up/pallas_call | solution.py:127
  127.8 1.3 collective-permute-start.29
  129.1 1.9 collective-permute-done.26.refs_11_
  131.0 8.2 %gate_up.14 = (bf16[64,4096]{1,0:T(8,128)(2,1)S(1)}, bf16[64,4224]{1,0:T(8,128)(2,1)S(1)}, bf16[128,4096]{1,0:T(8,128)(2,1)S(1)}, f32[128,128]{1,0:T(8,128)S(1)}) custom-call(bf16[512,3584]{1,0:T(8,128)(2,1)S(1)} %get-tuple-element.70.refs_0_, bf16[512,3584]{1,0:T(8,128)(2,1)S(1)} %get-tuple-element.71.refs_1_, ...), custom_call_target="tpu_custom_call" | custom-call | flops 4294967296 | bytes 16777216 | tf_op jit(solution)/shard_map/gate_up/pallas_call | solution.py:127
  139.2 1.4 collective-permute-start.31
  142.2 1.3 collective-permute-start.32
  143.6 6.3 %gate_up.15 = (bf16[64,3072]{1,0:T(8,128)(2,1)S(1)}, bf16[64,3072]{1,0:T(8,128)(2,1)S(1)}) custom-call(bf16[512,3584]{1,0:T(8,128)(2,1)S(1)} %get-tuple-element.70.refs_0_, bf16[512,3584]{1,0:T(8,128)(2,1)S(1)} %get-tuple-element.71.refs_1_, bf16[512,3584]{1,0:T(8,128)(2,1)S(1)} %get-tuple-element.72.refs_2_, ...), custom_call_target="tpu_custom_call" | custom-call | flops 3221225472 | bytes 12582912 | tf_op jit(solution)/shard_map/gate_up/pallas_call | solution.py:127
  150.6 6.9 %down.12.refs_0_.refs_4_ = f32[128,4096]{1,0:T(8,128)S(1)} custom-call(bf16[64,3072]{1,0:T(8,128)(2,1)S(1)} %get-tuple-element.117.refs_0_, bf16[64,2048]{1,0:T(8,128)(2,1)S(1)} %get-tuple-element.118.refs_1_, bf16[64,2048]{1,0:T(8,128)(2,1)S(1)} %collective-permute-done.30.refs_2_, bf16[1,3584,4096]{2,1,0:T(8,128)(2,1)} %refs_3_.7), custom_call_target="tpu_custom_call" | custom-call | flops 2147483648 | bytes 16777216 | tf_op jit(solution)/shard_map/down/pallas_call | solution.py:127
  157.5 1.2 hidden.14
  158.7 1.3 collective-permute-start.37
  160.0 6.9 %down.13 = (bf16[32,4096]{1,0:T(8,128)(2,1)S(1)}, bf16[32,4096]{1,0:T(8,128)(2,1)S(1)}, bf16[32,4096]{1,0:T(8,128)(2,1)S(1)}, bf16[32,4096]{1,0:T(8,128)(2,1)S(1)}) custom-call(f32[64,128]{1,0:T(8,128)S(1)} %get-tuple-element.121.refs_0_.refs_3_, bf16[64,1536]{1,0:T(8,128)(2,1)} %get-tuple-element.122.refs_1_, ...), custom_call_target="tpu_custom_call" | custom-call | flops 1610612736 | bytes 12582912 | tf_op jit(solution)/shard_map/down/pallas_call | solution.py:127
  166.9 5.1 %collective-permute-start.33 = (bf16[32,4096]{1,0:T(8,128)(2,1)S(1)}, bf16[32,4096]{1,0:T(8,128)(2,1)S(1)}, u32[]{:S(2)}, u32[]{:S(2)}) collective-permute-start(bf16[32,4096]{1,0:T(8,128)(2,1)S(1)} %get-tuple-element.124), channel_id=1, source_target_pairs={{0,16},{1,13},{2,18},{3,15},{4,20},{5,1},{6,22},{7,3},{8,24},{9,5}... | collective-permute-start | bytes 786440 | tf_op jit(solution)/shard_map/ppermute | solution.py:356
  172.4 1.3 hidden.15
  174.0 7.9 %down.14.refs_0_.refs_4_ = f32[128,4096]{1,0:T(8,128)S(1)} custom-call(f32[64,128]{1,0:T(8,128)S(1)} %get-tuple-element.128.refs_0_, bf16[64,2048]{1,0:T(8,128)(2,1)} %get-tuple-element.129.refs_1_, bf16[64,2048]{1,0:T(8,128)(2,1)} %collective-permute-done.37.refs_2_, bf16[1,3584,4096]{2,1,0:T(8,128)(2,1)} %refs_3_.7), custom_call_target="tpu_custom_call" | custom-call | flops 2147483648 | bytes 16777216 | tf_op jit(solution)/shard_map/down/pallas_call | solution.py:127
  181.9 5.9 %down.15 = (bf16[32,4096]{1,0:T(8,128)(2,1)S(1)}, bf16[32,4096]{1,0:T(8,128)(2,1)S(1)}, bf16[32,4096]{1,0:T(8,128)(2,1)S(1)}, bf16[32,4096]{1,0:T(8,128)(2,1)S(1)}) custom-call(f32[128,4096]{1,0:T(8,128)S(1)} %down.14.refs_0_.refs_4_, bf16[64,1536]{1,0:T(8,128)(2,1)S(1)} %get-tuple-element.130.refs_1_, bf16[64,1536]{1,0:T(8,128)(2,1)S(1)} %collective-permute-done.38.refs_2_, ...), custom_call_target="tpu_custom_call" | custom-call | flops 1610612736 | bytes 12582912 | tf_op jit(solution)/shard_map/down/pallas_call | solution.py:127
  187.8 3.0 %collective-permute-start.39 = (bf16[32,4096]{1,0:T(8,128)(2,1)S(1)}, bf16[32,4096]{1,0:T(8,128)(2,1)S(1)}, u32[]{:S(2)}, u32[]{:S(2)}) collective-permute-start(bf16[32,4096]{1,0:T(8,128)(2,1)S(1)} %get-tuple-element.132), channel_id=1, source_target_pairs={{0,16},{1,13},{2,18},{3,15},{4,20},{5,1},{6,22},{7,3},{8,24},{9,5}... | collective-permute-start | bytes 786440 | tf_op jit(solution)/shard_map/ppermute | solution.py:356
  191.6 2.7 %collective-permute-done.39 = bf16[32,4096]{1,0:T(8,128)(2,1)S(1)} collective-permute-done((bf16[32,4096]{1,0:T(8,128)(2,1)S(1)}, bf16[32,4096]{1,0:T(8,128)(2,1)S(1)}, u32[]{:S(2)}, u32[]{:S(2)}) %collective-permute-start.39) | collective-permute-done | bytes 262176 | tf_op jit(solution)/shard_map/ppermute | solution.py:356
  194.2 9.3 %collective-permute-done.40 = bf16[32,4096]{1,0:T(8,128)(2,1)S(1)} collective-permute-done((bf16[32,4096]{1,0:T(8,128)(2,1)S(1)}, bf16[32,4096]{1,0:T(8,128)(2,1)S(1)}, u32[]{:S(2)}, u32[]{:S(2)}) %collective-permute-start.40) | collective-permute-done | bytes 262176 | tf_op jit(solution)/shard_map/ppermute | solution.py:356
  (79 shorter events, 9.3 us)
Async XLA Ops:
  1.1 14.7 %copy-start = (f32[1,4096]{1,0:T(1,128)S(1)}, f32[1,4096]{1,0:T(1,128)}, u32[]{:S(2)}) copy-start(f32[1,4096]{1,0:T(1,128)} %refs_10_.7) | copy-start | bytes 49156
  1.1 13.1 %collective-permute-start = (bf16[32,4096]{1,0:T(8,128)(2,1)S(1)}, bf16[32,4096]{1,0:T(8,128)(2,1)S(1)}, u32[]{:S(2)}, u32[]{:S(2)}) collective-permute-start(bf16[32,4096]{1,0:T(8,128)(2,1)S(1)} %get-tuple-element.136.refs_8_), channel_id=1, source_target_pairs={{0,4},{1,17},{2,6},{3,19},{4,8},{5,21},{6,10},{7,23},{8,12},{9,25}... | collective-permute-start | bytes 786440 | tf_op jit(solution)/shard_map/ppermute | solution.py:356
  3.2 11.0 %collective-permute-start.1 = (bf16[32,4096]{1,0:T(8,128)(2,1)S(1)}, bf16[32,4096]{1,0:T(8,128)(2,1)S(1)}, u32[]{:S(2)}, u32[]{:S(2)}) collective-permute-start(bf16[32,4096]{1,0:T(8,128)(2,1)S(1)} %get-tuple-element.136.refs_8_), channel_id=1, source_target_pairs={{0,8},{1,17},{2,10},{3,19},{4,12},{5,21},{6,14},{7,23},{8,0},{9,25... | collective-permute-start | bytes 786440 | tf_op jit(solution)/shard_map/ppermute | solution.py:356
  3.3 10.9 %collective-permute-start.2 = (bf16[32,4096]{1,0:T(8,128)(2,1)S(1)}, bf16[32,4096]{1,0:T(8,128)(2,1)S(1)}, u32[]{:S(2)}, u32[]{:S(2)}) collective-permute-start(bf16[32,4096]{1,0:T(8,128)(2,1)S(1)} %get-tuple-element.136.refs_8_), channel_id=1, source_target_pairs={{0,12},{1,17},{2,14},{3,19},{4,0},{5,21},{6,2},{7,23},{8,4},{9,25}... | collective-permute-start | bytes 786440 | tf_op jit(solution)/shard_map/ppermute | solution.py:356
  14.2 17.7 %collective-permute-start.3 = (bf16[32,4096]{1,0:T(8,128)(2,1)S(1)}, bf16[32,4096]{1,0:T(8,128)(2,1)S(1)}, u32[]{:S(2)}, u32[]{:S(2)}) collective-permute-start(bf16[32,4096]{1,0:T(8,128)(2,1)S(1)} %get-tuple-element.81.refs_9_), channel_id=1, source_target_pairs={{0,4},{1,17},{2,6},{3,19},{4,8},{5,21},{6,10},{7,23},{8,12},{9,25}... | collective-permute-start | bytes 786440 | tf_op jit(solution)/shard_map/ppermute | solution.py:356
  14.3 17.6 %collective-permute-start.4 = (bf16[32,4096]{1,0:T(8,128)(2,1)S(1)}, bf16[32,4096]{1,0:T(8,128)(2,1)S(1)}, u32[]{:S(2)}, u32[]{:S(2)}) collective-permute-start(bf16[32,4096]{1,0:T(8,128)(2,1)S(1)} %get-tuple-element.81.refs_9_), channel_id=1, source_target_pairs={{0,8},{1,17},{2,10},{3,19},{4,12},{5,21},{6,14},{7,23},{8,0},{9,25... | collective-permute-start | bytes 786440 | tf_op jit(solution)/shard_map/ppermute | solution.py:356
  15.7 16.2 %collective-permute-start.5 = (bf16[32,4096]{1,0:T(8,128)(2,1)S(1)}, bf16[32,4096]{1,0:T(8,128)(2,1)S(1)}, u32[]{:S(2)}, u32[]{:S(2)}) collective-permute-start(bf16[32,4096]{1,0:T(8,128)(2,1)S(1)} %get-tuple-element.81.refs_9_), channel_id=1, source_target_pairs={{0,12},{1,17},{2,14},{3,19},{4,0},{5,21},{6,2},{7,23},{8,4},{9,25}... | collective-permute-start | bytes 786440 | tf_op jit(solution)/shard_map/ppermute | solution.py:356
  24.0 17.6 %collective-permute-start.6 = (bf16[64,4224]{1,0:T(8,128)(2,1)S(1)}, bf16[64,4224]{1,0:T(8,128)(2,1)S(1)}, u32[]{:S(2)}, u32[]{:S(2)}) collective-permute-start(bf16[64,4224]{1,0:T(8,128)(2,1)S(1)} %get-tuple-element.84), channel_id=1, source_target_pairs={{0,2},{1,17},{2,0},{3,19},{4,6},{5,21},{6,4},{7,23},{8,10},{9,25},... | collective-permute-start | bytes 1622024 | tf_op jit(solution)/shard_map/ppermute | solution.py:356
  31.8 10.4 %collective-permute-start.7 = (bf16[64,3072]{1,0:T(8,128)(2,1)S(1)}, bf16[64,3072]{1,0:T(8,128)(2,1)S(1)}, u32[]{:S(2)}, u32[]{:S(2)}) collective-permute-start(bf16[64,3072]{1,0:T(8,128)(2,1)S(1)} %get-tuple-element.80.refs_8_), channel_id=1, source_target_pairs={{0,2},{1,17},{2,0},{3,19},{4,6},{5,21},{6,4},{7,23},{8,10},{9,25},... | collective-permute-start | bytes 1179656 | tf_op jit(solution)/shard_map/ppermute | solution.py:356
  40.1 18.3 %collective-permute-start.9 = (bf16[64,4224]{1,0:T(8,128)(2,1)S(1)}, bf16[64,4224]{1,0:T(8,128)(2,1)S(1)}, u32[]{:S(2)}, u32[]{:S(2)}) collective-permute-start(bf16[64,4224]{1,0:T(8,128)(2,1)S(1)} %get-tuple-element.92), channel_id=1, source_target_pairs={{0,2},{1,17},{2,0},{3,19},{4,6},{5,21},{6,4},{7,23},{8,10},{9,25},... | collective-permute-start | bytes 1622024 | tf_op jit(solution)/shard_map/ppermute | solution.py:356
  42.0 9.5 %collective-permute-start.8 = (bf16[64,2048]{1,0:T(8,128)(2,1)S(1)}, bf16[64,2048]{1,0:T(8,128)(2,1)S(1)}, u32[]{:S(2)}, u32[]{:S(2)}) collective-permute-start(bf16[64,2048]{1,0:T(8,128)(2,1)S(1)} %get-tuple-element.90.refs_9_), channel_id=1, source_target_pairs={{0,2},{1,17},{2,0},{3,19},{4,6},{5,21},{6,4},{7,23},{8,10},{9,25},... | collective-permute-start | bytes 786440 | tf_op jit(solution)/shard_map/ppermute | solution.py:356
  42.5 16.4 %collective-permute-start.10 = (bf16[64,1536]{1,0:T(8,128)(2,1)S(1)}, bf16[64,1536]{1,0:T(8,128)(2,1)S(1)}, u32[]{:S(2)}, u32[]{:S(2)}) collective-permute-start(bf16[64,1536]{1,0:T(8,128)(2,1)S(1)} %get-tuple-element.94.refs_9_), channel_id=1, source_target_pairs={{0,2},{1,17},{2,0},{3,19},{4,6},{5,21},{6,4},{7,23},{8,10},{9,25},... | collective-permute-start | bytes 589832 | tf_op jit(solution)/shard_map/ppermute | solution.py:356
  50.3 17.5 %collective-permute-start.15 = (bf16[64,3072]{1,0:T(8,128)(2,1)S(1)}, bf16[64,3072]{1,0:T(8,128)(2,1)S(1)}, u32[]{:S(2)}, u32[]{:S(2)}) collective-permute-start(bf16[64,3072]{1,0:T(8,128)(2,1)S(1)} %get-tuple-element.89.refs_8_), channel_id=1, source_target_pairs={{0,2},{1,17},{2,0},{3,19},{4,6},{5,21},{6,4},{7,23},{8,10},{9,25},... | collective-permute-start | bytes 1179656 | tf_op jit(solution)/shard_map/ppermute | solution.py:356
  64.8 5.3 %collective-permute-start.11 = (bf16[32,4096]{1,0:T(8,128)(2,1)S(1)}, bf16[32,4096]{1,0:T(8,128)(2,1)S(1)}, u32[]{:S(2)}, u32[]{:S(2)}) collective-permute-start(bf16[32,4096]{1,0:T(8,128)(2,1)S(1)} %get-tuple-element.96), channel_id=1, source_target_pairs={{0,12},{1,17},{2,14},{3,19},{4,0},{5,21},{6,2},{7,23},{8,4},{9,25}... | collective-permute-start | bytes 786440 | tf_op jit(solution)/shard_map/ppermute | solution.py:356
  66.2 6.7 %collective-permute-start.12 = (bf16[32,4096]{1,0:T(8,128)(2,1)S(1)}, bf16[32,4096]{1,0:T(8,128)(2,1)S(1)}, u32[]{:S(2)}, u32[]{:S(2)}) collective-permute-start(bf16[32,4096]{1,0:T(8,128)(2,1)S(1)} %get-tuple-element.97), channel_id=1, source_target_pairs={{0,8},{1,17},{2,10},{3,19},{4,12},{5,21},{6,14},{7,23},{8,0},{9,25... | collective-permute-start | bytes 786440 | tf_op jit(solution)/shard_map/ppermute | solution.py:356
  66.3 9.7 %collective-permute-start.13 = (bf16[32,4096]{1,0:T(8,128)(2,1)S(1)}, bf16[32,4096]{1,0:T(8,128)(2,1)S(1)}, u32[]{:S(2)}, u32[]{:S(2)}) collective-permute-start(bf16[32,4096]{1,0:T(8,128)(2,1)S(1)} %get-tuple-element.98.refs_8_), channel_id=1, source_target_pairs={{0,4},{1,17},{2,6},{3,19},{4,8},{5,21},{6,10},{7,23},{8,12},{9,25}... | collective-permute-start | bytes 786440 | tf_op jit(solution)/shard_map/ppermute | solution.py:356
  67.7 20.9 %collective-permute-start.16 = (bf16[64,2048]{1,0:T(8,128)(2,1)S(1)}, bf16[64,2048]{1,0:T(8,128)(2,1)S(1)}, u32[]{:S(2)}, u32[]{:S(2)}) collective-permute-start(bf16[64,2048]{1,0:T(8,128)(2,1)S(1)} %get-tuple-element.101.refs_9_), channel_id=1, source_target_pairs={{0,2},{1,17},{2,0},{3,19},{4,6},{5,21},{6,4},{7,23},{8,10},{9,25},... | collective-permute-start | bytes 786440 | tf_op jit(solution)/shard_map/ppermute | solution.py:356
  67.8 8.2 %copy-start.1 = (bf16[2,32,4096]{2,1,0:T(8,128)(2,1)S(1)}, bf16[2,32,4096]{2,1,0:T(8,128)(2,1)}, u32[]{:S(2)}) copy-start(bf16[2,32,4096]{2,1,0:T(8,128)(2,1)} %param.5) | copy-start | bytes 1572868
  68.0 29.4 %collective-permute-start.17 = (bf16[64,1536]{1,0:T(8,128)(2,1)S(1)}, bf16[64,1536]{1,0:T(8,128)(2,1)S(1)}, u32[]{:S(2)}, u32[]{:S(2)}) collective-permute-start(bf16[64,1536]{1,0:T(8,128)(2,1)S(1)} %get-tuple-element.102.refs_9_), channel_id=1, source_target_pairs={{0,2},{1,17},{2,0},{3,19},{4,6},{5,21},{6,4},{7,23},{8,10},{9,25},... | collective-permute-start | bytes 589832 | tf_op jit(solution)/shard_map/ppermute | solution.py:356
  76.1 21.3 %copy-start.2 = (bf16[32,4096]{1,0:T(8,128)(2,1)}, bf16[32,4096]{1,0:T(8,128)(2,1)S(1)}, u32[]{:S(2)}) copy-start(bf16[32,4096]{1,0:T(8,128)(2,1)S(1)} %add_convert_fusion.3) | copy-start | bytes 786436
  76.1 28.7 %collective-permute-start.14 = (bf16[32,4096]{1,0:T(8,128)(2,1)S(1)}, bf16[32,4096]{1,0:T(8,128)(2,1)S(1)}, u32[]{:S(2)}, u32[]{:S(2)}) collective-permute-start(bf16[32,4096]{1,0:T(8,128)(2,1)S(1)} %add_convert_fusion.3), channel_id=1, source_target_pairs={{0,1},{1,0},{2,3},{3,2},{4,5},{5,4},{6,7},{7,6},{8,9},{9,8},{10,11... | collective-permute-start | bytes 786440 | tf_op jit(solution)/shard_map/ppermute | solution.py:356
  88.4 16.5 %collective-permute-start.18 = (bf16[32,4096]{1,0:T(8,128)(2,1)S(1)}, bf16[32,4096]{1,0:T(8,128)(2,1)S(1)}, u32[]{:S(2)}, u32[]{:S(2)}) collective-permute-start(bf16[32,4096]{1,0:T(8,128)(2,1)S(1)} %add_convert_fusion.3), channel_id=1, source_target_pairs={{0,5},{1,0},{2,7},{3,2},{4,9},{5,4},{6,11},{7,6},{8,13},{9,8},{10,... | collective-permute-start | bytes 786440 | tf_op jit(solution)/shard_map/ppermute | solution.py:356
  88.5 17.8 %collective-permute-start.19 = (bf16[32,4096]{1,0:T(8,128)(2,1)S(1)}, bf16[32,4096]{1,0:T(8,128)(2,1)S(1)}, u32[]{:S(2)}, u32[]{:S(2)}) collective-permute-start(bf16[32,4096]{1,0:T(8,128)(2,1)S(1)} %add_convert_fusion.3), channel_id=1, source_target_pairs={{0,9},{1,0},{2,11},{3,2},{4,13},{5,4},{6,15},{7,6},{8,1},{9,8},{10... | collective-permute-start | bytes 786440 | tf_op jit(solution)/shard_map/ppermute | solution.py:356
  88.6 17.7 %collective-permute-start.20 = (bf16[32,4096]{1,0:T(8,128)(2,1)S(1)}, bf16[32,4096]{1,0:T(8,128)(2,1)S(1)}, u32[]{:S(2)}, u32[]{:S(2)}) collective-permute-start(bf16[32,4096]{1,0:T(8,128)(2,1)S(1)} %add_convert_fusion.3), channel_id=1, source_target_pairs={{0,13},{1,0},{2,15},{3,2},{4,1},{5,4},{6,3},{7,6},{8,5},{9,8},{10,... | collective-permute-start | bytes 786440 | tf_op jit(solution)/shard_map/ppermute | solution.py:356
  103.4 12.4 %collective-permute-start.21 = (bf16[32,4096]{1,0:T(8,128)(2,1)S(1)}, bf16[32,4096]{1,0:T(8,128)(2,1)S(1)}, u32[]{:S(2)}, u32[]{:S(2)}) collective-permute-start(bf16[32,4096]{1,0:T(8,128)(2,1)S(1)} %get-tuple-element.108), channel_id=1, source_target_pairs={{0,12},{1,17},{2,14},{3,19},{4,0},{5,21},{6,2},{7,23},{8,4},{9,25}... | collective-permute-start | bytes 786440 | tf_op jit(solution)/shard_map/ppermute | solution.py:356
  104.8 10.9 %collective-permute-start.22 = (bf16[32,4096]{1,0:T(8,128)(2,1)S(1)}, bf16[32,4096]{1,0:T(8,128)(2,1)S(1)}, u32[]{:S(2)}, u32[]{:S(2)}) collective-permute-start(bf16[32,4096]{1,0:T(8,128)(2,1)S(1)} %get-tuple-element.109), channel_id=1, source_target_pairs={{0,8},{1,17},{2,10},{3,19},{4,12},{5,21},{6,14},{7,23},{8,0},{9,25... | collective-permute-start | bytes 786440 | tf_op jit(solution)/shard_map/ppermute | solution.py:356
  104.9 10.9 %collective-permute-start.23 = (bf16[32,4096]{1,0:T(8,128)(2,1)S(1)}, bf16[32,4096]{1,0:T(8,128)(2,1)S(1)}, u32[]{:S(2)}, u32[]{:S(2)}) collective-permute-start(bf16[32,4096]{1,0:T(8,128)(2,1)S(1)} %get-tuple-element.103.refs_8_), channel_id=1, source_target_pairs={{0,4},{1,17},{2,6},{3,19},{4,8},{5,21},{6,10},{7,23},{8,12},{9,25}... | collective-permute-start | bytes 786440 | tf_op jit(solution)/shard_map/ppermute | solution.py:356
  114.5 26.1 %collective-permute-start.28 = (bf16[64,4224]{1,0:T(8,128)(2,1)S(1)}, bf16[64,4224]{1,0:T(8,128)(2,1)S(1)}, u32[]{:S(2)}, u32[]{:S(2)}) collective-permute-start(bf16[64,4224]{1,0:T(8,128)(2,1)S(1)} %get-tuple-element.112), channel_id=1, source_target_pairs={{0,16},{1,3},{2,18},{3,1},{4,20},{5,7},{6,22},{7,5},{8,24},{9,11},... | collective-permute-start | bytes 1622024 | tf_op jit(solution)/shard_map/ppermute | solution.py:356
  116.0 11.8 %copy-start.4 = (bf16[32,4096]{1,0:T(8,128)(2,1)}, bf16[32,4096]{1,0:T(8,128)(2,1)S(1)}, u32[]{:S(2)}) copy-start(bf16[32,4096]{1,0:T(8,128)(2,1)S(1)} %add_convert_fusion.2) | copy-start | bytes 786436
  116.0 11.8 %collective-permute-start.24 = (bf16[32,4096]{1,0:T(8,128)(2,1)S(1)}, bf16[32,4096]{1,0:T(8,128)(2,1)S(1)}, u32[]{:S(2)}, u32[]{:S(2)}) collective-permute-start(bf16[32,4096]{1,0:T(8,128)(2,1)S(1)} %add_convert_fusion.2), channel_id=1, source_target_pairs={{0,1},{1,0},{2,3},{3,2},{4,5},{5,4},{6,7},{7,6},{8,9},{9,8},{10,11... | collective-permute-start | bytes 786440 | tf_op jit(solution)/shard_map/ppermute | solution.py:356
  118.6 10.5 %collective-permute-start.25 = (bf16[32,4096]{1,0:T(8,128)(2,1)S(1)}, bf16[32,4096]{1,0:T(8,128)(2,1)S(1)}, u32[]{:S(2)}, u32[]{:S(2)}) collective-permute-start(bf16[32,4096]{1,0:T(8,128)(2,1)S(1)} %add_convert_fusion.2), channel_id=1, source_target_pairs={{0,5},{1,0},{2,7},{3,2},{4,9},{5,4},{6,11},{7,6},{8,13},{9,8},{10,... | collective-permute-start | bytes 786440 | tf_op jit(solution)/shard_map/ppermute | solution.py:356
  118.7 12.4 %collective-permute-start.26 = (bf16[32,4096]{1,0:T(8,128)(2,1)S(1)}, bf16[32,4096]{1,0:T(8,128)(2,1)S(1)}, u32[]{:S(2)}, u32[]{:S(2)}) collective-permute-start(bf16[32,4096]{1,0:T(8,128)(2,1)S(1)} %add_convert_fusion.2), channel_id=1, source_target_pairs={{0,9},{1,0},{2,11},{3,2},{4,13},{5,4},{6,15},{7,6},{8,1},{9,8},{10... | collective-permute-start | bytes 786440 | tf_op jit(solution)/shard_map/ppermute | solution.py:356
  119.5 11.6 %collective-permute-start.27 = (bf16[32,4096]{1,0:T(8,128)(2,1)S(1)}, bf16[32,4096]{1,0:T(8,128)(2,1)S(1)}, u32[]{:S(2)}, u32[]{:S(2)}) collective-permute-start(bf16[32,4096]{1,0:T(8,128)(2,1)S(1)} %add_convert_fusion.2), channel_id=1, source_target_pairs={{0,13},{1,0},{2,15},{3,2},{4,1},{5,4},{6,3},{7,6},{8,5},{9,8},{10,... | collective-permute-start | bytes 786440 | tf_op jit(solution)/shard_map/ppermute | solution.py:356
  127.8 13.5 %collective-permute-start.29 = (bf16[64,3072]{1,0:T(8,128)(2,1)S(1)}, bf16[64,3072]{1,0:T(8,128)(2,1)S(1)}, u32[]{:S(2)}, u32[]{:S(2)}) collective-permute-start(bf16[64,3072]{1,0:T(8,128)(2,1)S(1)} %get-tuple-element.106.refs_8_), channel_id=1, source_target_pairs={{0,16},{1,3},{2,18},{3,1},{4,20},{5,7},{6,22},{7,5},{8,24},{9,11},... | collective-permute-start | bytes 1179656 | tf_op jit(solution)/shard_map/ppermute | solution.py:356
  139.2 18.3 %collective-permute-start.31 = (bf16[64,4224]{1,0:T(8,128)(2,1)S(1)}, bf16[64,4224]{1,0:T(8,128)(2,1)S(1)}, u32[]{:S(2)}, u32[]{:S(2)}) collective-permute-start(bf16[64,4224]{1,0:T(8,128)(2,1)S(1)} %get-tuple-element.120), channel_id=1, source_target_pairs={{0,16},{1,3},{2,18},{3,1},{4,20},{5,7},{6,22},{7,5},{8,24},{9,11},... | collective-permute-start | bytes 1622024 | tf_op jit(solution)/shard_map/ppermute | solution.py:356
  141.1 9.5 %collective-permute-start.30 = (bf16[64,2048]{1,0:T(8,128)(2,1)S(1)}, bf16[64,2048]{1,0:T(8,128)(2,1)S(1)}, u32[]{:S(2)}, u32[]{:S(2)}) collective-permute-start(bf16[64,2048]{1,0:T(8,128)(2,1)S(1)} %get-tuple-element.118.refs_1_), channel_id=1, source_target_pairs={{0,16},{1,3},{2,18},{3,1},{4,20},{5,7},{6,22},{7,5},{8,24},{9,11},... | collective-permute-start | bytes 786440 | tf_op jit(solution)/shard_map/ppermute | solution.py:356
  142.2 17.8 %collective-permute-start.32 = (bf16[64,1536]{1,0:T(8,128)(2,1)}, bf16[64,1536]{1,0:T(8,128)(2,1)}, u32[]{:S(2)}, u32[]{:S(2)}) collective-permute-start(bf16[64,1536]{1,0:T(8,128)(2,1)} %get-tuple-element.122.refs_1_), channel_id=1, source_target_pairs={{0,16},{1,3},{2,18},{3,1},{4,20},{5,7},{6,22},{7,5},{8,24},{9,11},... | collective-permute-start | bytes 589832 | tf_op jit(solution)/shard_map/ppermute | solution.py:356
  149.9 22.5 %collective-permute-start.36 = (bf16[64,3072]{1,0:T(8,128)(2,1)S(1)}, bf16[64,3072]{1,0:T(8,128)(2,1)}, u32[]{:S(2)}, u32[]{:S(2)}) collective-permute-start(bf16[64,3072]{1,0:T(8,128)(2,1)S(1)} %get-tuple-element.117.refs_0_), channel_id=1, source_target_pairs={{0,16},{1,3},{2,18},{3,1},{4,20},{5,7},{6,22},{7,5},{8,24},{9,11},... | collective-permute-start | bytes 1179656 | tf_op jit(solution)/shard_map/ppermute | solution.py:356
  158.7 15.3 %collective-permute-start.37 = (bf16[64,2048]{1,0:T(8,128)(2,1)}, bf16[64,2048]{1,0:T(8,128)(2,1)}, u32[]{:S(2)}, u32[]{:S(2)}) collective-permute-start(bf16[64,2048]{1,0:T(8,128)(2,1)} %get-tuple-element.129.refs_1_), channel_id=1, source_target_pairs={{0,16},{1,3},{2,18},{3,1},{4,20},{5,7},{6,22},{7,5},{8,24},{9,11},... | collective-permute-start | bytes 786440 | tf_op jit(solution)/shard_map/ppermute | solution.py:356
  166.9 24.5 %collective-permute-start.33 = (bf16[32,4096]{1,0:T(8,128)(2,1)S(1)}, bf16[32,4096]{1,0:T(8,128)(2,1)S(1)}, u32[]{:S(2)}, u32[]{:S(2)}) collective-permute-start(bf16[32,4096]{1,0:T(8,128)(2,1)S(1)} %get-tuple-element.124), channel_id=1, source_target_pairs={{0,16},{1,13},{2,18},{3,15},{4,20},{5,1},{6,22},{7,3},{8,24},{9,5}... | collective-permute-start | bytes 786440 | tf_op jit(solution)/shard_map/ppermute | solution.py:356
  172.0 19.4 %collective-permute-start.34 = (bf16[32,4096]{1,0:T(8,128)(2,1)S(1)}, bf16[32,4096]{1,0:T(8,128)(2,1)S(1)}, u32[]{:S(2)}, u32[]{:S(2)}) collective-permute-start(bf16[32,4096]{1,0:T(8,128)(2,1)S(1)} %get-tuple-element.125), channel_id=1, source_target_pairs={{0,16},{1,9},{2,18},{3,11},{4,20},{5,13},{6,22},{7,15},{8,24},{9,1... | collective-permute-start | bytes 786440 | tf_op jit(solution)/shard_map/ppermute | solution.py:356
  172.0 19.4 %collective-permute-start.35 = (bf16[32,4096]{1,0:T(8,128)(2,1)S(1)}, bf16[32,4096]{1,0:T(8,128)(2,1)S(1)}, u32[]{:S(2)}, u32[]{:S(2)}) collective-permute-start(bf16[32,4096]{1,0:T(8,128)(2,1)S(1)} %get-tuple-element.126.refs_0_), channel_id=1, source_target_pairs={{0,16},{1,5},{2,18},{3,7},{4,20},{5,9},{6,22},{7,11},{8,24},{9,13}... | collective-permute-start | bytes 786440 | tf_op jit(solution)/shard_map/ppermute | solution.py:356
  173.7 8.3 %collective-permute-start.38 = (bf16[64,1536]{1,0:T(8,128)(2,1)S(1)}, bf16[64,1536]{1,0:T(8,128)(2,1)S(1)}, u32[]{:S(2)}, u32[]{:S(2)}) collective-permute-start(bf16[64,1536]{1,0:T(8,128)(2,1)S(1)} %get-tuple-element.130.refs_1_), channel_id=1, source_target_pairs={{0,16},{1,3},{2,18},{3,1},{4,20},{5,7},{6,22},{7,5},{8,24},{9,11},... | collective-permute-start | bytes 589832 | tf_op jit(solution)/shard_map/ppermute | solution.py:356
  181.9 21.8 %copy-start.3 = (bf16[32,4096]{1,0:T(8,128)(2,1)S(1)}, bf16[32,4096]{1,0:T(8,128)(2,1)}, u32[]{:S(2)}) copy-start(bf16[32,4096]{1,0:T(8,128)(2,1)} %copy-done.2) | copy-start | bytes 786436
  181.9 21.8 %copy-start.5 = (bf16[32,4096]{1,0:T(8,128)(2,1)S(1)}, bf16[32,4096]{1,0:T(8,128)(2,1)}, u32[]{:S(2)}) copy-start(bf16[32,4096]{1,0:T(8,128)(2,1)} %copy-done.4) | copy-start | bytes 786436
  187.8 6.4 %collective-permute-start.39 = (bf16[32,4096]{1,0:T(8,128)(2,1)S(1)}, bf16[32,4096]{1,0:T(8,128)(2,1)S(1)}, u32[]{:S(2)}, u32[]{:S(2)}) collective-permute-start(bf16[32,4096]{1,0:T(8,128)(2,1)S(1)} %get-tuple-element.132), channel_id=1, source_target_pairs={{0,16},{1,13},{2,18},{3,15},{4,20},{5,1},{6,22},{7,3},{8,24},{9,5}... | collective-permute-start | bytes 786440 | tf_op jit(solution)/shard_map/ppermute | solution.py:356
  190.8 12.8 %collective-permute-start.40 = (bf16[32,4096]{1,0:T(8,128)(2,1)S(1)}, bf16[32,4096]{1,0:T(8,128)(2,1)S(1)}, u32[]{:S(2)}, u32[]{:S(2)}) collective-permute-start(bf16[32,4096]{1,0:T(8,128)(2,1)S(1)} %get-tuple-element.133), channel_id=1, source_target_pairs={{0,16},{1,9},{2,18},{3,11},{4,20},{5,13},{6,22},{7,15},{8,24},{9,1... | collective-permute-start | bytes 786440 | tf_op jit(solution)/shard_map/ppermute | solution.py:356
  191.4 12.2 %collective-permute-start.41 = (bf16[32,4096]{1,0:T(8,128)(2,1)S(1)}, bf16[32,4096]{1,0:T(8,128)(2,1)S(1)}, u32[]{:S(2)}, u32[]{:S(2)}) collective-permute-start(bf16[32,4096]{1,0:T(8,128)(2,1)S(1)} %get-tuple-element.134), channel_id=1, source_target_pairs={{0,16},{1,5},{2,18},{3,7},{4,20},{5,9},{6,22},{7,11},{8,24},{9,13}... | collective-permute-start | bytes 786440 | tf_op jit(solution)/shard_map/ppermute | solution.py:356

commit v2 on v1

v2 whole, which is shorter than its diff:
```python
import jax
import jax.numpy as jnp
from jax import lax
from jax.experimental import pallas as pl
from jax.experimental.pallas import tpu as pltpu
from jax.sharding import PartitionSpec as P

EPS = 1e-05
MIB = 1 << 20
LANES = 128
BUFFERS = 3
VMEM_MIB = 12
PIECES = 8
PARTS = 2
WIDEST = 2048
AXES = ("group", "col", "row", "section")

f32 = jnp.float32
bf16 = jnp.bfloat16


def tile_of(width):
    for tile in (512, 256, 128):
        if width % tile == 0:
            return tile
    return width


def in_vmem(value):
    return pltpu.with_memory_space_constraint(value, pltpu.VMEM)


def in_hbm(value):
    return pltpu.with_memory_space_constraint(value, pltpu.HBM)


VMEM_SPEC = pl.BlockSpec(memory_space=pltpu.VMEM)
HBM_SPEC = pl.BlockSpec(memory_space=pltpu.HBM)
ANY_SPEC = pl.BlockSpec(memory_space=pl.ANY)


class Routes:
    def __init__(self, sizes):
        self.sizes = sizes

    def index(self, place):
        index = 0
        for axis in AXES:
            index = index * self.sizes[axis] + place[axis]
        return index

    def places(self):
        for g in range(self.sizes["group"]):
            for c in range(self.sizes["col"]):
                for r in range(self.sizes["row"]):
                    for s in range(self.sizes["section"]):
                        yield dict(group=g, col=c, row=r, section=s)

    def shifted(self, place, axis, steps):
        return dict(place, **{axis: (place[axis] + steps) % self.sizes[axis]})

    def within(self, section, axis, steps):
        pairs = []
        for place in self.places():
            if place["section"] == section:
                target = self.shifted(place, axis, steps)
            else:
                target = self.shifted(place, "group", 1)
            pairs.append((self.index(place), self.index(target)))
        return pairs

    def onward(self, section, steps):
        pairs = []
        for place in self.places():
            if place["section"] == section:
                target = dict(self.shifted(place, "col", steps), section=section + 1)
            elif place["section"] == section + 1:
                target = dict(place, section=section)
            else:
                target = self.shifted(place, "group", 1)
            pairs.append((self.index(place), self.index(target)))
        return pairs


def streamed(count, parts, copy, body):
    def start(q):
        tile, part = (q // parts, q % parts) if isinstance(q, int) else (lax.div(q, parts), lax.rem(q, parts))
        copy(tile, part, q % BUFFERS if isinstance(q, int) else lax.rem(q, BUFFERS)).start()

    for q in range(min(BUFFERS, count * parts)):
        start(q)

    def step(i, carry):
        def use(part, f):
            q = i * parts + part
            slot = lax.rem(q, BUFFERS)
            copy(i, part, slot).wait()
            value = f(slot)

            @pl.when(q + BUFFERS < count * parts)
            def _():
                start(q + BUFFERS)

            return value

        body(i, use)
        return carry

    return lambda: lax.fori_loop(0, count, step, 0)


class Kernels:
    def __init__(self, n_row, n_col, w_gate, w_up, w_down):
        self.n_row, self.n_col = n_row, n_col
        self.w_up, self.w_down = w_up, w_down
        self.kept = []
        self.before = []
        self.depth, self.width = w_gate.shape[1:]
        self.half = self.depth // PARTS
        self.load(w_gate)

    def call(self, section, kernel, operands, specs, out_shape, scratch, vmem, flops, moved, name):
        extras = [in_vmem(v) for v in self.kept] + self.before
        n_kept, n = len(self.kept), len(extras)

        def wrapped(*refs):
            if section is None:
                kernel(refs[:n_kept], *refs[n:])
            else:

                @pl.when(lax.axis_index("section") == section)
                def _():
                    kernel(refs[:n_kept], *refs[n:])

        outs = pl.pallas_call(
            wrapped,
            out_shape=out_shape,
            in_specs=[VMEM_SPEC] * n_kept + [ANY_SPEC] * (n - n_kept) + specs,
            out_specs=[VMEM_SPEC] * len(out_shape),
            scratch_shapes=scratch,
            compiler_params=pltpu.CompilerParams(vmem_limit_bytes=vmem * MIB),
            cost_estimate=pl.CostEstimate(flops=flops, bytes_accessed=moved, transcendentals=0),
            name=name,
        )(*extras, *operands)
        self.before = [outs[-1]]
        return outs

    def load(self, w_gate):
        rows = self.depth // PIECES
        n = PIECES

        def kernel(_, gate_ref, *refs):
            outs, sem = refs[:-1], refs[-1]
            copies = []
            for i, out in enumerate(outs):
                copies.append(pltpu.make_async_copy(gate_ref.at[0, pl.ds(i * rows, rows)], out, sem.at[i]))
            for copy in copies:
                copy.start()
            for copy in copies:
                copy.wait()

        self.kept = self.call(
            None,
            kernel,
            [in_hbm(w_gate)],
            [HBM_SPEC],
            [pltpu.VMEM((rows, self.width), bf16)] * n,
            [pltpu.SemaphoreType.DMA((n,))],
            1,
            0,
            2 * n * rows * self.width,
            "load",
        )
        self.before = []

    def gate_up(self, section, blocks, scaled_in, gain, start, size, tile):
        depth, half = self.depth, self.half
        opens = scaled_in is None
        n = len(blocks) if opens else 1
        rows = sum(b.shape[0] for b in blocks) if opens else scaled_in.shape[0]
        extra = LANES if opens else 0
        piece = depth // PIECES

        def scale_rows(block_refs, gain_ref, scaled, out):
            tok = block_refs[0].shape[0]
            lane = lax.broadcasted_iota(jnp.int32, (tok, LANES), 1)
            for d, block in enumerate(block_refs):
                place = slice(d * tok, (d + 1) * tok)
                total = jnp.zeros((tok, LANES), f32)
                for first in range(0, depth, tile):
                    wide = block[:, first : first + tile].astype(f32)
                    scaled[place, first : first + tile] = (
                        wide * gain_ref[:, first : first + tile]
                    ).astype(bf16)
                    wide = wide * wide
                    for lane_first in range(0, tile, LANES):
                        total = total + wide[:, lane_first : lane_first + LANES]
                total = jnp.broadcast_to(jnp.sum(total, axis=1, keepdims=True), (tok, LANES))
                high = total.astype(bf16).astype(f32)
                out[place, pl.ds(2 * size, LANES)] = jnp.where(
                    lane < LANES // 2, high, total - high
                ).astype(bf16)

        def kernel(kept, *refs):
            sources, gain_ref, up_w, refs = refs[:n], refs[n], refs[n + 1], refs[n + 2 :]
            out, buf, sem = refs[0], refs[-2], refs[-1]

            def copy(i, part, slot):
                columns = pl.ds(pl.multiple_of(start + i * tile, LANES), tile)
                return pltpu.make_async_copy(
                    up_w.at[0, pl.ds(part * half, half), columns], buf.at[slot], sem.at[slot]
                )

            def body(i, use):
                offset = pl.multiple_of(i * tile, tile)
                columns = pl.ds(pl.multiple_of(start + offset, LANES), tile)

                def product(first, weights):
                    return jnp.dot(
                        scaled[:, first : first + weights.shape[0]], weights, preferred_element_type=f32
                    )

                gate = product(0, kept[0][:, columns])
                for p in range(1, PIECES):
                    gate = gate + product(p * piece, kept[p][:, columns])
                out[:, pl.ds(offset, tile)] = gate.astype(bf16)
                up = use(0, lambda slot: product(0, buf[slot]))
                for part in range(1, PARTS):
                    up = up + use(part, lambda slot: product(part * half, buf[slot]))
                out[:, pl.ds(pl.multiple_of(size + offset, tile), tile)] = up.astype(bf16)

            run = streamed(size // tile, PARTS, copy, body)
            scaled = sources[0]
            if opens:
                scaled = refs[1]
                scale_rows(sources, gain_ref, scaled, out)
            run()

        out_shape = [pltpu.VMEM((rows, 2 * size + extra), bf16)]
        if opens:
            out_shape += [pltpu.VMEM((rows, depth), bf16)]
        sources = [in_vmem(v) for v in blocks] if opens else [in_vmem(scaled_in)]
        return self.call(
            section,
            kernel,
            sources + [gain, in_hbm(self.w_up)],
            [VMEM_SPEC] * (n + 1) + [HBM_SPEC],
            out_shape,
            [
                pltpu.VMEM((BUFFERS, half, tile), bf16),
                pltpu.SemaphoreType.DMA((BUFFERS,)),
            ],
            VMEM_MIB,
            4 * rows * depth * size,
            2 * depth * size,
            "gate_up",
        )

    def down(self, section, sums, chunks, scale_in, acc):
        n_row, n_col = self.n_row, self.n_col
        start, size = chunks[0][0], sum(chunk[1] for chunk in chunks)
        rows = sums[0][0].shape[0]
        tok = rows // n_col
        columns = self.w_down.shape[2]
        tile = tile_of(columns)
        opens, last = start == 0, start + size == self.width
        parts = -(-size // WIDEST)
        deep = size // parts
        features = self.depth * n_row
        flat = [in_vmem(v) for group in sums for v in group]
        n = len(flat)

        def kernel(_, *refs):
            sum_refs, w_ref, refs = refs[:n], refs[n], refs[n + 1 :]
            if not opens:
                scale_ref, acc_ref, refs = refs[0], refs[1], refs[2:]
            outs, (held, buf, sem) = refs[:-3], refs[-3:]

            def copy(i, part, slot):
                place = pl.ds(pl.multiple_of(i * tile, tile), tile)
                return pltpu.make_async_copy(
                    w_ref.at[0, pl.ds(start + part * deep, deep), place], buf.at[slot], sem.at[slot]
                )

            def body(i, use):
                place = pl.ds(pl.multiple_of(i * tile, tile), tile)
                total = None if opens else acc_ref[:, place]
                for p in range(parts):
                    left = held[:, p * deep : (p + 1) * deep]
                    part = use(p, lambda slot: jnp.dot(left, buf[slot], preferred_element_type=f32))
                    total = part if total is None else total + part
                if last:
                    total = total.astype(bf16)
                    for d, out in enumerate(outs):
                        out[:, place] = total[d * tok : (d + 1) * tok]
                else:
                    outs[0][:, place] = total

            run = streamed(columns // tile, parts, copy, body)
            for first in range(0, rows, tok):
                place = slice(first, first + tok)
                for c, (begin, width) in enumerate(chunks):
                    refs_here = sum_refs[c * n_row : (c + 1) * n_row]

                    def whole(columns):
                        total = refs_here[0][place, columns].astype(f32)
                        for ref in refs_here[1:]:
                            total = total + ref[place, columns].astype(f32)
                        return total

                    if c == 0 and opens:
                        squares = whole(pl.ds(2 * width, LANES))
                        squares = squares[:, 0:1] + squares[:, LANES // 2 : LANES // 2 + 1]
                        scale = lax.rsqrt(squares / features + EPS)
                    elif c == 0:
                        scale = scale_ref[place, 0:1]
                    step = tile_of(width)
                    for at in range(0, width, step):
                        gate = whole(pl.ds(at, step)) * scale
                        up = whole(pl.ds(width + at, step)) * scale
                        held[place, begin - start + at : begin - start + at + step] = (
                            gate / (1.0 + jnp.exp(-gate)) * up
                        ).astype(bf16)
                if not last:
                    outs[1][place, :] = jnp.broadcast_to(scale, (tok, LANES))
            run()

        if last:
            out_shape = [pltpu.VMEM((tok, columns), bf16)] * n_col
        else:
            out_shape = [pltpu.VMEM((rows, columns), f32), pltpu.VMEM((rows, LANES), f32)]
        extras = [] if opens else [in_vmem(scale_in), in_vmem(acc)]
        return self.call(
            section,
            kernel,
            flat + [in_hbm(self.w_down)] + extras,
            [VMEM_SPEC] * n + [HBM_SPEC] + [VMEM_SPEC] * len(extras),
            out_shape,
            [
                pltpu.VMEM((rows, size), bf16),
                pltpu.VMEM((BUFFERS, deep, tile), bf16),
                pltpu.SemaphoreType.DMA((BUFFERS,)),
            ],
            VMEM_MIB,
            2 * rows * size * columns,
            2 * size * columns,
            "down",
        )


def solution(mesh):
    sizes = dict(mesh.shape)
    routes = Routes(sizes)
    n_col, n_row, n_section = sizes["col"], sizes["row"], sizes["section"]

    def move(value, pairs):
        return lax.ppermute(value, AXES, pairs)

    def on_device(tokens, norm_gain, w_gate, w_up, w_down):
        section_index = lax.axis_index("section")
        micro, tok, depth = tokens.shape
        width = w_gate.shape[2]
        tile = tile_of(width)
        k = Kernels(n_row, n_col, w_gate, w_up, w_down)

        def gathered(section, block):
            if section:
                return [move(block, routes.onward(section - 1, d)) for d in range(n_col)]
            return [block] + [move(block, routes.within(section, "col", d)) for d in range(1, n_col)]

        def exchanged(section, value):
            return [value] + [move(value, routes.within(section, "row", e)) for e in range(1, n_row)]

        class Job:
            def __init__(self, section, block, chunks):
                self.section, self.chunks = section, chunks
                self.blocks = gathered(section, block)
                self.scaled = self.scale = self.acc = None
                self.sums = []

            def gate_up(self, c):
                outs = k.gate_up(self.section, self.blocks, self.scaled, norm_gain, *self.chunks[c], tile)
                if c == 0:
                    self.scaled = outs[1]
                self.sums.append(exchanged(self.section, outs[0]))

            def down(self, first, last):
                outs = k.down(
                    self.section, self.sums[first:last], self.chunks[first:last], self.scale, self.acc
                )
                if last < len(self.chunks):
                    self.acc, self.scale = outs
                    return
                arrived = [
                    move(outs[d], routes.within(self.section, "col", -d)) for d in range(1, n_col)
                ]
                total = outs[0].astype(f32)
                for value in arrived:
                    total = total + value.astype(f32)
                self.result = (self.blocks[0].astype(f32) + total).astype(bf16)

        jobs = {}
        steps = FLAT if (n_section, micro) == (2, 2) else in_turn(n_section, micro)
        for at, (what, section, m, *c) in enumerate(steps):
            if what == "n":
                block = jobs[section - 1, m].result if section else tokens[m]
                if jobs:
                    block, _ = lax.optimization_barrier((block, k.before[0]))
                jobs[section, m] = Job(section, block, chunked(width, tile, *c))
            elif what == "g":
                jobs[section, m].gate_up(*c)
                if not any(step[0] == "g" for step in steps[at + 1 :]):
                    k.kept = []
            else:
                jobs[section, m].down(*c)
        outs = [
            jnp.stack([jobs[section, m].result for m in range(micro)], axis=0)
            for section in range(n_section)
        ]
        out = outs[0]
        for section in range(1, n_section):
            out = jnp.where(section_index == section, outs[section], out)
        return out[None]

    placed = (
        P(None, ("group", "col"), "row"),
        P("section", "row"),
        P("section", "row", "col"),
        P("section", "row", "col"),
        P("section", "col", "row"),
    )
    return jax.shard_map(
        on_device,
        mesh=mesh,
        in_specs=placed,
        out_specs=P("section", None, ("group", "col"), "row"),
        check_vma=False,
    )


def chunked(width, tile, count):
    tiles = width // tile
    chunks, start = [], 0
    for c in range(count):
        size = -(-(tiles - start // tile) // (count - c)) * tile
        chunks.append((start, size))
        start += size
    return chunks


def in_turn(n_section, micro):
    steps = []
    for section in range(n_section):
        for m in range(micro):
            steps += [("n", section, m, 2), ("g", section, m, 0), ("g", section, m, 1)]
            steps += [("d", section, m, 0, 2)]
    return steps


FLAT = [("n", 0, 0, 2), ("g", 0, 0, 0), ("n", 0, 1, 2), ("g", 0, 0, 1), ("g", 0, 1, 0), ("d", 0, 0, 0, 1), ("d", 0, 0, 1, 2), ("g", 0, 1, 1), ("d", 0, 1, 0, 1), ("n", 1, 0, 2), ("d", 0, 1, 1, 2),("g", 1, 0, 0), ("g", 1, 0, 1), ("n", 1, 1, 2), ("d", 1, 0, 0, 1), ("d", 1, 0, 1, 2), ("g", 1, 1, 0), ("g", 1, 1, 1), ("d", 1, 1, 0, 1), ("d", 1, 1, 1, 2),]
```

time: 205 us -> 191 us (0.932)
  Pallas kernels: 126 us -> 65.4 us
  waiting for transfers between devices: 22.1 us -> 75.6 us
  starting transfers between devices: 53.6 us -> 46.8 us
    pallas_call x25 -> x17, Pallas kernels: 126 us -> 65.4 us  [call(): pl.pallas_call(wrapped, out_shape=out_shape, in_specs=[VMEM_SPEC] * n_kep...]
    ppermute x42 -> x34, waiting for transfers between devices: 22.1 us -> 75.6 us  [move(): return lax.ppermute(value, AXES, pairs)]
    ppermute x42 -> x34, starting transfers between devices: 53.6 us -> 46.8 us  [move(): return lax.ppermute(value, AXES, pairs)]
  transfers between devices with their start and end apart: 42 -> 34, of which waited for: 8 -> 17; matrix products, arithmetic and copies ran while one was open for 0% -> 0% of each run, Pallas kernels for 62% -> 30%
where the time goes in v2:
time: 191 us
  waiting for transfers between devices  75.6 us (40%)
  Pallas kernels  65.4 us (34%)
  starting transfers between devices  46.8 us (25%)
    ppermute x34, waiting for transfers between devices, move(): return lax.ppermute(value, AXES, pairs)  75.6 us
    pallas_call x17, Pallas kernels, call(): pl.pallas_call(wrapped, out_shape=out_shape, in_specs=[VMEM_SPEC] * n_kep...  65.4 us
    ppermute x34, starting transfers between devices, move(): return lax.ppermute(value, AXES, pairs)  46.8 us
  transfers between devices with their start and end apart: 34, of which 17 were waited for; matrix products, arithmetic and copies ran while one was open for 0% of the time, Pallas kernels for 30%

profile of v2, /device:TPU:1, one launch (start us, length us, event | category | flops | bytes accessed | tf_op | source)
XLA Modules:
  0.0 191.0 jit_solution(11198131511644743156)
XLA Ops:
  0.0 1.1 slice_bitcast_fusion
  1.1 2.1 %collective-permute-start = (bf16[32,4096]{1,0:T(8,128)(2,1)S(1)}, bf16[32,4096]{1,0:T(8,128)(2,1)S(1)}, u32[]{:S(2)}, u32[]{:S(2)}) collective-permute-start(bf16[32,4096]{1,0:T(8,128)(2,1)S(1)} %get-tuple-element.92.refs_8_), channel_id=1, source_target_pairs={{0,4},{1,17},{2,6},{3,19},{4,8},{5,21},{6,10},{7,23},{8,12},{9,25}... | collective-permute-start | bytes 786440 | tf_op jit(solution)/shard_map/ppermute | solution.py:357
  3.3 1.4 collective-permute-start.2
  4.7 9.5 %load.1 = (bf16[512,3584]{1,0:T(8,128)(2,1)S(1)}, bf16[512,3584]{1,0:T(8,128)(2,1)S(1)}, bf16[512,3584]{1,0:T(8,128)(2,1)S(1)}, bf16[512,3584]{1,0:T(8,128)(2,1)...) custom-call(bf16[1,4096,3584]{2,1,0:T(8,128)(2,1)} %refs_0_.1), custom_call_target="tpu_custom_call" | custom-call | bytes 29360128 | tf_op jit(solution)/shard_map/load/pallas_call | solution.py:135
  14.4 1.3 collective-permute-start.4
  15.9 1.3 collective-permute-start.6
  17.5 2.1 %collective-permute-done.3.refs_10_ = bf16[32,4096]{1,0:T(8,128)(2,1)S(1)} collective-permute-done((bf16[32,4096]{1,0:T(8,128)(2,1)S(1)}, bf16[32,4096]{1,0:T(8,128)(2,1)S(1)}, u32[]{:S(2)}, u32[]{:S(2)}) %collective-permute-start.3) | collective-permute-done | bytes 262176 | tf_op jit(solution)/shard_map/ppermute | solution.py:357
  19.5 2.8 %collective-permute-done.4.refs_11_ = bf16[32,4096]{1,0:T(8,128)(2,1)S(1)} collective-permute-done((bf16[32,4096]{1,0:T(8,128)(2,1)S(1)}, bf16[32,4096]{1,0:T(8,128)(2,1)S(1)}, u32[]{:S(2)}, u32[]{:S(2)}) %collective-permute-start.4) | collective-permute-done | bytes 262176 | tf_op jit(solution)/shard_map/ppermute | solution.py:357
  22.3 2.8 %collective-permute-done.5.refs_12_ = bf16[32,4096]{1,0:T(8,128)(2,1)S(1)} collective-permute-done((bf16[32,4096]{1,0:T(8,128)(2,1)S(1)}, bf16[32,4096]{1,0:T(8,128)(2,1)S(1)}, u32[]{:S(2)}, u32[]{:S(2)}) %collective-permute-start.5) | collective-permute-done | bytes 262176 | tf_op jit(solution)/shard_map/ppermute | solution.py:357
  25.4 11.7 %collective-permute-done.6.refs_10_ = bf16[128,4224]{1,0:T(8,128)(2,1)S(1)} collective-permute-done((bf16[128,4224]{1,0:T(8,128)(2,1)S(1)}, bf16[128,4224]{1,0:T(8,128)(2,1)S(1)}, u32[]{:S(2)}, u32[]{:S(2)}) %collective-permute-start.6) | collective-permute-done | bytes 1081376 | tf_op jit(solution)/shard_map/ppermute | solution.py:357
  37.1 8.4 %collective-permute-done.7.refs_10_ = bf16[128,3072]{1,0:T(8,128)(2,1)S(1)} collective-permute-done((bf16[128,3072]{1,0:T(8,128)(2,1)S(1)}, bf16[128,3072]{1,0:T(8,128)(2,1)S(1)}, u32[]{:S(2)}, u32[]{:S(2)}) %collective-permute-start.7) | collective-permute-done | bytes 786464 | tf_op jit(solution)/shard_map/ppermute | solution.py:357
  45.7 1.3 collective-permute-start.8
  47.2 1.4 collective-permute-start.13
  48.6 8.5 %collective-permute-done.11.refs_10_ = bf16[128,4224]{1,0:T(8,128)(2,1)S(1)} collective-permute-done((bf16[128,4224]{1,0:T(8,128)(2,1)S(1)}, bf16[128,4224]{1,0:T(8,128)(2,1)S(1)}, u32[]{:S(2)}, u32[]{:S(2)}) %collective-permute-start.11) | collective-permute-done | bytes 1081376 | tf_op jit(solution)/shard_map/ppermute | solution.py:357
  57.1 2.8 %collective-permute-done.10 = bf16[32,4096]{1,0:T(8,128)(2,1)S(1)} collective-permute-done((bf16[32,4096]{1,0:T(8,128)(2,1)S(1)}, bf16[32,4096]{1,0:T(8,128)(2,1)S(1)}, u32[]{:S(2)}, u32[]{:S(2)}) %collective-permute-start.10) | collective-permute-done | bytes 262176 | tf_op jit(solution)/shard_map/ppermute | solution.py:357
  59.9 2.8 %collective-permute-done.8 = bf16[32,4096]{1,0:T(8,128)(2,1)S(1)} collective-permute-done((bf16[32,4096]{1,0:T(8,128)(2,1)S(1)}, bf16[32,4096]{1,0:T(8,128)(2,1)S(1)}, u32[]{:S(2)}, u32[]{:S(2)}) %collective-permute-start.8) | collective-permute-done | bytes 262176 | tf_op jit(solution)/shard_map/ppermute | solution.py:357
  62.7 2.5 %collective-permute-done.9 = bf16[32,4096]{1,0:T(8,128)(2,1)S(1)} collective-permute-done((bf16[32,4096]{1,0:T(8,128)(2,1)S(1)}, bf16[32,4096]{1,0:T(8,128)(2,1)S(1)}, u32[]{:S(2)}, u32[]{:S(2)}) %collective-permute-start.9) | collective-permute-done | bytes 262176 | tf_op jit(solution)/shard_map/ppermute | solution.py:357
  65.4 16.0 %collective-permute-start.12 = (bf16[32,4096]{1,0:T(8,128)(2,1)S(1)}, bf16[32,4096]{1,0:T(8,128)(2,1)S(1)}, u32[]{:S(2)}, u32[]{:S(2)}) collective-permute-start(bf16[32,4096]{1,0:T(8,128)(2,1)S(1)} %add_convert_fusion.3), channel_id=1, source_target_pairs={{0,1},{1,0},{2,3},{3,2},{4,5},{5,4},{6,7},{7,6},{8,9},{9,8},{10,11... | collective-permute-start | bytes 786440 | tf_op jit(solution)/shard_map/ppermute | solution.py:357
  81.4 1.0 collective-permute-start.15
  82.4 1.0 collective-permute-start.16
  83.4 1.3 collective-permute-start.24
  84.7 4.4 %collective-permute-done.14.refs_10_ = bf16[32,4096]{1,0:T(8,128)(2,1)S(1)} collective-permute-done((bf16[32,4096]{1,0:T(8,128)(2,1)S(1)}, bf16[32,4096]{1,0:T(8,128)(2,1)S(1)}, u32[]{:S(2)}, u32[]{:S(2)}) %collective-permute-start.14) | collective-permute-done | bytes 262176 | tf_op jit(solution)/shard_map/ppermute | solution.py:357
  89.1 5.1 %collective-permute-done.15.refs_11_ = bf16[32,4096]{1,0:T(8,128)(2,1)S(1)} collective-permute-done((bf16[32,4096]{1,0:T(8,128)(2,1)S(1)}, bf16[32,4096]{1,0:T(8,128)(2,1)S(1)}, u32[]{:S(2)}, u32[]{:S(2)}) %collective-permute-start.15) | collective-permute-done | bytes 262176 | tf_op jit(solution)/shard_map/ppermute | solution.py:357
  94.2 8.2 %gate_up.12 = (bf16[128,4224]{1,0:T(8,128)(2,1)S(1)}, bf16[128,4096]{1,0:T(8,128)(2,1)S(1)}) custom-call(bf16[512,3584]{1,0:T(8,128)(2,1)S(1)} %get-tuple-element.48.refs_0_, bf16[512,3584]{1,0:T(8,128)(2,1)S(1)} %get-tuple-element.49.refs_1_, bf16[512,3584]{1,0:T(8,128)(2,1)S(1)} %get-tuple-element.50.refs_2_, ...), custom_call_target="tpu_custom_call" | custom-call | flops 4294967296 | bytes 16777216 | tf_op jit(solution)/shard_map/gate_up/pallas_call | solution.py:135
  102.4 1.3 collective-permute-start.17
  103.6 1.2 collective-permute-start.22
  105.1 6.3 %gate_up.13.refs_8_.refs_9_ = bf16[128,3072]{1,0:T(8,128)(2,1)S(1)} custom-call(bf16[512,3584]{1,0:T(8,128)(2,1)S(1)} %get-tuple-element.48.refs_0_, bf16[512,3584]{1,0:T(8,128)(2,1)S(1)} %get-tuple-element.49.refs_1_, bf16[512,3584]{1,0:T(8,128)(2,1)S(1)} %get-tuple-element.50.refs_2_, bf16[512,3584]{1,0:T(8,128)(2,1)S(1)} %get-tuple-element.51.refs_3_, ...), custom_call_target="tpu_custom_call" | custom-call | flops 3221225472 | bytes 12582912 | tf_op jit(solution)/shard_map/gate_up/pallas_call | solution.py:135
  111.4 0.3 collective-permute-start.18
  111.7 0.3 collective-permute-done.22
  112.0 5.6 %collective-permute-done.23 = bf16[32,4096]{1,0:T(8,128)(2,1)S(1)} collective-permute-done((bf16[32,4096]{1,0:T(8,128)(2,1)S(1)}, bf16[32,4096]{1,0:T(8,128)(2,1)S(1)}, u32[]{:S(2)}, u32[]{:S(2)}) %collective-permute-start.23) | collective-permute-done | bytes 262176 | tf_op jit(solution)/shard_map/ppermute | solution.py:357
  117.9 0.5 collective-permute-start.26
  118.4 6.2 %collective-permute-start.27 = (bf16[32,4096]{1,0:T(8,128)(2,1)S(1)}, bf16[32,4096]{1,0:T(8,128)(2,1)S(1)}, u32[]{:S(2)}, u32[]{:S(2)}) collective-permute-start(bf16[32,4096]{1,0:T(8,128)(2,1)S(1)} %add_convert_fusion.1), channel_id=1, source_target_pairs={{0,9},{1,0},{2,11},{3,2},{4,13},{5,4},{6,15},{7,6},{8,1},{9,8},{10... | collective-permute-start | bytes 786440 | tf_op jit(solution)/shard_map/ppermute | solution.py:357
  124.5 6.9 %down.12 = (f32[128,4096]{1,0:T(8,128)S(1)}, f32[128,128]{1,0:T(8,128)S(1)}) custom-call(bf16[512,3584]{1,0:T(8,128)(2,1)S(1)} %get-tuple-element.48.refs_0_, bf16[512,3584]{1,0:T(8,128)(2,1)S(1)} %get-tuple-element.49.refs_1_, bf16[512,3584]{1,0:T(8,128)(2,1)S(1)} %get-tuple-element.50.refs_2_, bf16[512,3584]{1,0:T(8,128)(2,1)S(1)} %get-tuple-element.51.refs_3_, ...), custom_call_target="tpu_custom_call" | custom-call | flops 2147483648 | bytes 16777216 | tf_op jit(solution)/shard_map/down/pallas_call | solution.py:135
  131.5 5.9 %down.13 = (bf16[32,4096]{1,0:T(8,128)(2,1)S(1)}, bf16[32,4096]{1,0:T(8,128)(2,1)S(1)}, bf16[32,4096]{1,0:T(8,128)(2,1)S(1)}, bf16[32,4096]{1,0:T(8,128)(2,1)S(1)}) custom-call(bf16[512,3584]{1,0:T(8,128)(2,1)S(1)} %get-tuple-element.48.refs_0_, bf16[512,3584]{1,0:T(8,128)(2,1)S(1)} %get-tuple-element.49.refs_1_, ...), custom_call_target="tpu_custom_call" | custom-call | flops 1610612736 | bytes 12582912 | tf_op jit(solution)/shard_map/down/pallas_call | solution.py:135
  137.4 8.3 %gate_up.14 = (bf16[128,4224]{1,0:T(8,128)(2,1)S(1)}, bf16[128,4096]{1,0:T(8,128)(2,1)S(1)}) custom-call(bf16[512,3584]{1,0:T(8,128)(2,1)S(1)} %get-tuple-element.48.refs_0_, bf16[512,3584]{1,0:T(8,128)(2,1)S(1)} %get-tuple-element.49.refs_1_, bf16[512,3584]{1,0:T(8,128)(2,1)S(1)} %get-tuple-element.50.refs_2_, ...), custom_call_target="tpu_custom_call" | custom-call | flops 4294967296 | bytes 16777216 | tf_op jit(solution)/shard_map/gate_up/pallas_call | solution.py:135
  145.7 0.3 collective-permute-start.29
  146.1 6.3 %gate_up.15.refs_0_.refs_1_ = bf16[128,3072]{1,0:T(8,128)(2,1)S(1)} custom-call(bf16[512,3584]{1,0:T(8,128)(2,1)S(1)} %get-tuple-element.48.refs_0_, bf16[512,3584]{1,0:T(8,128)(2,1)S(1)} %get-tuple-element.49.refs_1_, bf16[512,3584]{1,0:T(8,128)(2,1)S(1)} %get-tuple-element.50.refs_2_, bf16[512,3584]{1,0:T(8,128)(2,1)S(1)} %get-tuple-element.51.refs_3_, ...), custom_call_target="tpu_custom_call" | custom-call | flops 3221225472 | bytes 12582912 | tf_op jit(solution)/shard_map/gate_up/pallas_call | solution.py:135
  152.4 1.3 collective-permute-start.30
  153.7 3.2 %collective-permute-start.19 = (bf16[32,4096]{1,0:T(8,128)(2,1)}, bf16[32,4096]{1,0:T(8,128)(2,1)S(1)}, u32[]{:S(2)}, u32[]{:S(2)}) collective-permute-start(bf16[32,4096]{1,0:T(8,128)(2,1)} %copy-done.5), channel_id=1, source_target_pairs={{0,16},{1,13},{2,18},{3,15},{4,20},{5,1},{6,22},{7,3},{8,24},{9,5}... | collective-permute-start | bytes 786440 | tf_op jit(solution)/shard_map/ppermute | solution.py:357
  156.9 3.2 %collective-permute-done.29.refs_2_ = bf16[128,4224]{1,0:T(8,128)(2,1)S(1)} collective-permute-done((bf16[128,4224]{1,0:T(8,128)(2,1)S(1)}, bf16[128,4224]{1,0:T(8,128)(2,1)S(1)}, u32[]{:S(2)}, u32[]{:S(2)}) %collective-permute-start.29) | collective-permute-done | bytes 1081376 | tf_op jit(solution)/shard_map/ppermute | solution.py:357
  160.1 6.9 %down.14 = (f32[128,4096]{1,0:T(8,128)S(1)}, f32[128,128]{1,0:T(8,128)S(1)}) custom-call(bf16[128,3072]{1,0:T(8,128)(2,1)S(1)} %gate_up.15.refs_0_.refs_1_, bf16[128,4224]{1,0:T(8,128)(2,1)S(1)} %get-tuple-element.84.refs_1_, bf16[128,4224]{1,0:T(8,128)(2,1)S(1)} %collective-permute-done.29.refs_2_, bf16[1,3584,4096]{2,1,0:T(8,128)(2,1)} %refs_3_.3), custom_call_target="tpu_custom_call" | custom-call | flops 2147483648 | bytes 16777216 | tf_op jit(solution)/shard_map/down/pallas_call | solution.py:135
  167.0 1.5 collective-permute-done.30.refs_2_
  168.5 7.0 %down.15 = (bf16[32,4096]{1,0:T(8,128)(2,1)S(1)}, bf16[32,4096]{1,0:T(8,128)(2,1)S(1)}, bf16[32,4096]{1,0:T(8,128)(2,1)S(1)}, bf16[32,4096]{1,0:T(8,128)(2,1)S(1)}) custom-call(f32[128,128]{1,0:T(8,128)S(1)} %get-tuple-element.85.refs_0_.refs_4_, bf16[128,3072]{1,0:T(8,128)(2,1)S(1)} %gate_up.15.refs_0_.refs_1_, ...), custom_call_target="tpu_custom_call" | custom-call | flops 1610612736 | bytes 12582912 | tf_op jit(solution)/shard_map/down/pallas_call | solution.py:135
  175.6 2.6 %collective-permute-start.31 = (bf16[32,4096]{1,0:T(8,128)(2,1)S(1)}, bf16[32,4096]{1,0:T(8,128)(2,1)S(1)}, u32[]{:S(2)}, u32[]{:S(2)}) collective-permute-start(bf16[32,4096]{1,0:T(8,128)(2,1)S(1)} %get-tuple-element.88), channel_id=1, source_target_pairs={{0,16},{1,13},{2,18},{3,15},{4,20},{5,1},{6,22},{7,3},{8,24},{9,5}... | collective-permute-start | bytes 786440 | tf_op jit(solution)/shard_map/ppermute | solution.py:357
  178.2 0.4 collective-permute-start.33
  178.7 2.8 %collective-permute-done.31 = bf16[32,4096]{1,0:T(8,128)(2,1)S(1)} collective-permute-done((bf16[32,4096]{1,0:T(8,128)(2,1)S(1)}, bf16[32,4096]{1,0:T(8,128)(2,1)S(1)}, u32[]{:S(2)}, u32[]{:S(2)}) %collective-permute-start.31) | collective-permute-done | bytes 262176 | tf_op jit(solution)/shard_map/ppermute | solution.py:357
  181.5 8.4 %collective-permute-done.32 = bf16[32,4096]{1,0:T(8,128)(2,1)S(1)} collective-permute-done((bf16[32,4096]{1,0:T(8,128)(2,1)S(1)}, bf16[32,4096]{1,0:T(8,128)(2,1)S(1)}, u32[]{:S(2)}, u32[]{:S(2)}) %collective-permute-start.32) | collective-permute-done | bytes 262176 | tf_op jit(solution)/shard_map/ppermute | solution.py:357
  190.1 0.9 maximum_select_fusion
  (65 shorter events, 2.5 us)
Async XLA Ops:
  1.1 13.1 %copy-start = (f32[1,4096]{1,0:T(1,128)S(1)}, f32[1,4096]{1,0:T(1,128)}, u32[]{:S(2)}) copy-start(f32[1,4096]{1,0:T(1,128)} %refs_10_.7) | copy-start | bytes 49156
  1.1 13.1 %collective-permute-start = (bf16[32,4096]{1,0:T(8,128)(2,1)S(1)}, bf16[32,4096]{1,0:T(8,128)(2,1)S(1)}, u32[]{:S(2)}, u32[]{:S(2)}) collective-permute-start(bf16[32,4096]{1,0:T(8,128)(2,1)S(1)} %get-tuple-element.92.refs_8_), channel_id=1, source_target_pairs={{0,4},{1,17},{2,6},{3,19},{4,8},{5,21},{6,10},{7,23},{8,12},{9,25}... | collective-permute-start | bytes 786440 | tf_op jit(solution)/shard_map/ppermute | solution.py:357
  3.2 11.0 %collective-permute-start.1 = (bf16[32,4096]{1,0:T(8,128)(2,1)S(1)}, bf16[32,4096]{1,0:T(8,128)(2,1)S(1)}, u32[]{:S(2)}, u32[]{:S(2)}) collective-permute-start(bf16[32,4096]{1,0:T(8,128)(2,1)S(1)} %get-tuple-element.92.refs_8_), channel_id=1, source_target_pairs={{0,8},{1,17},{2,10},{3,19},{4,12},{5,21},{6,14},{7,23},{8,0},{9,25... | collective-permute-start | bytes 786440 | tf_op jit(solution)/shard_map/ppermute | solution.py:357
  3.3 10.9 %collective-permute-start.2 = (bf16[32,4096]{1,0:T(8,128)(2,1)S(1)}, bf16[32,4096]{1,0:T(8,128)(2,1)S(1)}, u32[]{:S(2)}, u32[]{:S(2)}) collective-permute-start(bf16[32,4096]{1,0:T(8,128)(2,1)S(1)} %get-tuple-element.92.refs_8_), channel_id=1, source_target_pairs={{0,12},{1,17},{2,14},{3,19},{4,0},{5,21},{6,2},{7,23},{8,4},{9,25}... | collective-permute-start | bytes 786440 | tf_op jit(solution)/shard_map/ppermute | solution.py:357
  14.3 5.3 %collective-permute-start.3 = (bf16[32,4096]{1,0:T(8,128)(2,1)S(1)}, bf16[32,4096]{1,0:T(8,128)(2,1)S(1)}, u32[]{:S(2)}, u32[]{:S(2)}) collective-permute-start(bf16[32,4096]{1,0:T(8,128)(2,1)S(1)} %get-tuple-element.57.refs_9_), channel_id=1, source_target_pairs={{0,4},{1,17},{2,6},{3,19},{4,8},{5,21},{6,10},{7,23},{8,12},{9,25}... | collective-permute-start | bytes 786440 | tf_op jit(solution)/shard_map/ppermute | solution.py:357
  14.4 7.9 %collective-permute-start.4 = (bf16[32,4096]{1,0:T(8,128)(2,1)S(1)}, bf16[32,4096]{1,0:T(8,128)(2,1)S(1)}, u32[]{:S(2)}, u32[]{:S(2)}) collective-permute-start(bf16[32,4096]{1,0:T(8,128)(2,1)S(1)} %get-tuple-element.57.refs_9_), channel_id=1, source_target_pairs={{0,8},{1,17},{2,10},{3,19},{4,12},{5,21},{6,14},{7,23},{8,0},{9,25... | collective-permute-start | bytes 786440 | tf_op jit(solution)/shard_map/ppermute | solution.py:357
  15.8 9.4 %collective-permute-start.5 = (bf16[32,4096]{1,0:T(8,128)(2,1)S(1)}, bf16[32,4096]{1,0:T(8,128)(2,1)S(1)}, u32[]{:S(2)}, u32[]{:S(2)}) collective-permute-start(bf16[32,4096]{1,0:T(8,128)(2,1)S(1)} %get-tuple-element.57.refs_9_), channel_id=1, source_target_pairs={{0,12},{1,17},{2,14},{3,19},{4,0},{5,21},{6,2},{7,23},{8,4},{9,25}... | collective-permute-start | bytes 786440 | tf_op jit(solution)/shard_map/ppermute | solution.py:357
  15.9 21.1 %collective-permute-start.6 = (bf16[128,4224]{1,0:T(8,128)(2,1)S(1)}, bf16[128,4224]{1,0:T(8,128)(2,1)S(1)}, u32[]{:S(2)}, u32[]{:S(2)}) collective-permute-start(bf16[128,4224]{1,0:T(8,128)(2,1)S(1)} %get-tuple-element.59.refs_9_), channel_id=1, source_target_pairs={{0,2},{1,17},{2,0},{3,19},{4,6},{5,21},{6,4},{7,23},{8,10},{9,25},... | collective-permute-start | bytes 3244040 | tf_op jit(solution)/shard_map/ppermute | solution.py:357
  17.3 28.2 %collective-permute-start.7 = (bf16[128,3072]{1,0:T(8,128)(2,1)S(1)}, bf16[128,3072]{1,0:T(8,128)(2,1)S(1)}, u32[]{:S(2)}, u32[]{:S(2)}) collective-permute-start(bf16[128,3072]{1,0:T(8,128)(2,1)S(1)} %gate_up.9.refs_8_.refs_9_), channel_id=1, source_target_pairs={{0,2},{1,17},{2,0},{3,19},{4,6},{5,21},{6,4},{7,23},{8,10},{9,25},... | collective-permute-start | bytes 2359304 | tf_op jit(solution)/shard_map/ppermute | solution.py:357
  25.2 31.9 %collective-permute-start.11 = (bf16[128,4224]{1,0:T(8,128)(2,1)S(1)}, bf16[128,4224]{1,0:T(8,128)(2,1)S(1)}, u32[]{:S(2)}, u32[]{:S(2)}) collective-permute-start(bf16[128,4224]{1,0:T(8,128)(2,1)S(1)} %get-tuple-element.66.refs_9_), channel_id=1, source_target_pairs={{0,2},{1,17},{2,0},{3,19},{4,6},{5,21},{6,4},{7,23},{8,10},{9,25},... | collective-permute-start | bytes 3244040 | tf_op jit(solution)/shard_map/ppermute | solution.py:357
  45.5 14.4 %collective-permute-start.10 = (bf16[32,4096]{1,0:T(8,128)(2,1)S(1)}, bf16[32,4096]{1,0:T(8,128)(2,1)S(1)}, u32[]{:S(2)}, u32[]{:S(2)}) collective-permute-start(bf16[32,4096]{1,0:T(8,128)(2,1)S(1)} %get-tuple-element.65.refs_8_), channel_id=1, source_target_pairs={{0,4},{1,17},{2,6},{3,19},{4,8},{5,21},{6,10},{7,23},{8,12},{9,25}... | collective-permute-start | bytes 786440 | tf_op jit(solution)/shard_map/ppermute | solution.py:357
  45.7 17.0 %collective-permute-start.8 = (bf16[32,4096]{1,0:T(8,128)(2,1)S(1)}, bf16[32,4096]{1,0:T(8,128)(2,1)S(1)}, u32[]{:S(2)}, u32[]{:S(2)}) collective-permute-start(bf16[32,4096]{1,0:T(8,128)(2,1)S(1)} %get-tuple-element.63), channel_id=1, source_target_pairs={{0,12},{1,17},{2,14},{3,19},{4,0},{5,21},{6,2},{7,23},{8,4},{9,25}... | collective-permute-start | bytes 786440 | tf_op jit(solution)/shard_map/ppermute | solution.py:357
  47.0 18.2 %collective-permute-start.9 = (bf16[32,4096]{1,0:T(8,128)(2,1)S(1)}, bf16[32,4096]{1,0:T(8,128)(2,1)S(1)}, u32[]{:S(2)}, u32[]{:S(2)}) collective-permute-start(bf16[32,4096]{1,0:T(8,128)(2,1)S(1)} %get-tuple-element.64), channel_id=1, source_target_pairs={{0,8},{1,17},{2,10},{3,19},{4,12},{5,21},{6,14},{7,23},{8,0},{9,25... | collective-permute-start | bytes 786440 | tf_op jit(solution)/shard_map/ppermute | solution.py:357
  47.2 18.0 %copy-start.6 = (bf16[2,32,4096]{2,1,0:T(8,128)(2,1)S(1)}, bf16[2,32,4096]{2,1,0:T(8,128)(2,1)}, u32[]{:S(2)}) copy-start(bf16[2,32,4096]{2,1,0:T(8,128)(2,1)} %param.5) | copy-start | bytes 1572868
  47.2 36.2 %collective-permute-start.13 = (bf16[128,3072]{1,0:T(8,128)(2,1)S(1)}, bf16[128,3072]{1,0:T(8,128)(2,1)S(1)}, u32[]{:S(2)}, u32[]{:S(2)}) collective-permute-start(bf16[128,3072]{1,0:T(8,128)(2,1)S(1)} %gate_up.11.refs_8_.refs_9_), channel_id=1, source_target_pairs={{0,2},{1,17},{2,0},{3,19},{4,6},{5,21},{6,4},{7,23},{8,10},{9,25},... | collective-permute-start | bytes 2359304 | tf_op jit(solution)/shard_map/ppermute | solution.py:357
  65.4 18.0 %copy-start.7 = (bf16[32,4096]{1,0:T(8,128)(2,1)}, bf16[32,4096]{1,0:T(8,128)(2,1)S(1)}, u32[]{:S(2)}) copy-start(bf16[32,4096]{1,0:T(8,128)(2,1)S(1)} %add_convert_fusion.3) | copy-start | bytes 786436
  65.4 19.3 %collective-permute-start.12 = (bf16[32,4096]{1,0:T(8,128)(2,1)S(1)}, bf16[32,4096]{1,0:T(8,128)(2,1)S(1)}, u32[]{:S(2)}, u32[]{:S(2)}) collective-permute-start(bf16[32,4096]{1,0:T(8,128)(2,1)S(1)} %add_convert_fusion.3), channel_id=1, source_target_pairs={{0,1},{1,0},{2,3},{3,2},{4,5},{5,4},{6,7},{7,6},{8,9},{9,8},{10,11... | collective-permute-start | bytes 786440 | tf_op jit(solution)/shard_map/ppermute | solution.py:357
  81.3 7.8 %collective-permute-start.14 = (bf16[32,4096]{1,0:T(8,128)(2,1)S(1)}, bf16[32,4096]{1,0:T(8,128)(2,1)S(1)}, u32[]{:S(2)}, u32[]{:S(2)}) collective-permute-start(bf16[32,4096]{1,0:T(8,128)(2,1)S(1)} %add_convert_fusion.3), channel_id=1, source_target_pairs={{0,5},{1,0},{2,7},{3,2},{4,9},{5,4},{6,11},{7,6},{8,13},{9,8},{10,... | collective-permute-start | bytes 786440 | tf_op jit(solution)/shard_map/ppermute | solution.py:357
  81.4 12.8 %collective-permute-start.15 = (bf16[32,4096]{1,0:T(8,128)(2,1)S(1)}, bf16[32,4096]{1,0:T(8,128)(2,1)S(1)}, u32[]{:S(2)}, u32[]{:S(2)}) collective-permute-start(bf16[32,4096]{1,0:T(8,128)(2,1)S(1)} %add_convert_fusion.3), channel_id=1, source_target_pairs={{0,9},{1,0},{2,11},{3,2},{4,13},{5,4},{6,15},{7,6},{8,1},{9,8},{10... | collective-permute-start | bytes 786440 | tf_op jit(solution)/shard_map/ppermute | solution.py:357
  82.4 11.8 %collective-permute-start.16 = (bf16[32,4096]{1,0:T(8,128)(2,1)S(1)}, bf16[32,4096]{1,0:T(8,128)(2,1)S(1)}, u32[]{:S(2)}, u32[]{:S(2)}) collective-permute-start(bf16[32,4096]{1,0:T(8,128)(2,1)S(1)} %add_convert_fusion.3), channel_id=1, source_target_pairs={{0,13},{1,0},{2,15},{3,2},{4,1},{5,4},{6,3},{7,6},{8,5},{9,8},{10,... | collective-permute-start | bytes 786440 | tf_op jit(solution)/shard_map/ppermute | solution.py:357
  83.4 34.2 %collective-permute-start.24 = (bf16[32,4096]{1,0:T(8,128)(2,1)S(1)}, bf16[32,4096]{1,0:T(8,128)(2,1)S(1)}, u32[]{:S(2)}, u32[]{:S(2)}) collective-permute-start(bf16[32,4096]{1,0:T(8,128)(2,1)S(1)} %get-tuple-element.70.refs_8_), channel_id=1, source_target_pairs={{0,4},{1,17},{2,6},{3,19},{4,8},{5,21},{6,10},{7,23},{8,12},{9,25}... | collective-permute-start | bytes 786440 | tf_op jit(solution)/shard_map/ppermute | solution.py:357
  102.4 22.2 %collective-permute-start.17 = (bf16[128,4224]{1,0:T(8,128)(2,1)S(1)}, bf16[128,4224]{1,0:T(8,128)(2,1)S(1)}, u32[]{:S(2)}, u32[]{:S(2)}) collective-permute-start(bf16[128,4224]{1,0:T(8,128)(2,1)S(1)} %get-tuple-element.72.refs_9_), channel_id=1, source_target_pairs={{0,16},{1,3},{2,18},{3,1},{4,20},{5,7},{6,22},{7,5},{8,24},{9,11},... | collective-permute-start | bytes 3244040 | tf_op jit(solution)/shard_map/ppermute | solution.py:357
  103.6 8.4 %collective-permute-start.22 = (bf16[32,4096]{1,0:T(8,128)(2,1)S(1)}, bf16[32,4096]{1,0:T(8,128)(2,1)S(1)}, u32[]{:S(2)}, u32[]{:S(2)}) collective-permute-start(bf16[32,4096]{1,0:T(8,128)(2,1)S(1)} %get-tuple-element.80), channel_id=1, source_target_pairs={{0,12},{1,17},{2,14},{3,19},{4,0},{5,21},{6,2},{7,23},{8,4},{9,25}... | collective-permute-start | bytes 786440 | tf_op jit(solution)/shard_map/ppermute | solution.py:357
  104.9 12.8 %collective-permute-start.23 = (bf16[32,4096]{1,0:T(8,128)(2,1)S(1)}, bf16[32,4096]{1,0:T(8,128)(2,1)S(1)}, u32[]{:S(2)}, u32[]{:S(2)}) collective-permute-start(bf16[32,4096]{1,0:T(8,128)(2,1)S(1)} %get-tuple-element.81), channel_id=1, source_target_pairs={{0,8},{1,17},{2,10},{3,19},{4,12},{5,21},{6,14},{7,23},{8,0},{9,25... | collective-permute-start | bytes 786440 | tf_op jit(solution)/shard_map/ppermute | solution.py:357
  111.4 20.1 %collective-permute-start.18 = (bf16[128,3072]{1,0:T(8,128)(2,1)S(1)}, bf16[128,3072]{1,0:T(8,128)(2,1)S(1)}, u32[]{:S(2)}, u32[]{:S(2)}) collective-permute-start(bf16[128,3072]{1,0:T(8,128)(2,1)S(1)} %gate_up.13.refs_8_.refs_9_), channel_id=1, source_target_pairs={{0,16},{1,3},{2,18},{3,1},{4,20},{5,7},{6,22},{7,5},{8,24},{9,11},... | collective-permute-start | bytes 2359304 | tf_op jit(solution)/shard_map/ppermute | solution.py:357
  117.8 13.6 %copy-start.9 = (bf16[32,4096]{1,0:T(8,128)(2,1)}, bf16[32,4096]{1,0:T(8,128)(2,1)S(1)}, u32[]{:S(2)}) copy-start(bf16[32,4096]{1,0:T(8,128)(2,1)S(1)} %add_convert_fusion.1) | copy-start | bytes 786436
  117.8 19.6 %collective-permute-start.25 = (bf16[32,4096]{1,0:T(8,128)(2,1)S(1)}, bf16[32,4096]{1,0:T(8,128)(2,1)S(1)}, u32[]{:S(2)}, u32[]{:S(2)}) collective-permute-start(bf16[32,4096]{1,0:T(8,128)(2,1)S(1)} %add_convert_fusion.1), channel_id=1, source_target_pairs={{0,1},{1,0},{2,3},{3,2},{4,5},{5,4},{6,7},{7,6},{8,9},{9,8},{10,11... | collective-permute-start | bytes 786440 | tf_op jit(solution)/shard_map/ppermute | solution.py:357
  117.9 19.5 %collective-permute-start.26 = (bf16[32,4096]{1,0:T(8,128)(2,1)S(1)}, bf16[32,4096]{1,0:T(8,128)(2,1)S(1)}, u32[]{:S(2)}, u32[]{:S(2)}) collective-permute-start(bf16[32,4096]{1,0:T(8,128)(2,1)S(1)} %add_convert_fusion.1), channel_id=1, source_target_pairs={{0,5},{1,0},{2,7},{3,2},{4,9},{5,4},{6,11},{7,6},{8,13},{9,8},{10,... | collective-permute-start | bytes 786440 | tf_op jit(solution)/shard_map/ppermute | solution.py:357
  118.4 19.0 %collective-permute-start.27 = (bf16[32,4096]{1,0:T(8,128)(2,1)S(1)}, bf16[32,4096]{1,0:T(8,128)(2,1)S(1)}, u32[]{:S(2)}, u32[]{:S(2)}) collective-permute-start(bf16[32,4096]{1,0:T(8,128)(2,1)S(1)} %add_convert_fusion.1), channel_id=1, source_target_pairs={{0,9},{1,0},{2,11},{3,2},{4,13},{5,4},{6,15},{7,6},{8,1},{9,8},{10... | collective-permute-start | bytes 786440 | tf_op jit(solution)/shard_map/ppermute | solution.py:357
  124.5 12.9 %collective-permute-start.28 = (bf16[32,4096]{1,0:T(8,128)(2,1)S(1)}, bf16[32,4096]{1,0:T(8,128)(2,1)S(1)}, u32[]{:S(2)}, u32[]{:S(2)}) collective-permute-start(bf16[32,4096]{1,0:T(8,128)(2,1)S(1)} %add_convert_fusion.1), channel_id=1, source_target_pairs={{0,13},{1,0},{2,15},{3,2},{4,1},{5,4},{6,3},{7,6},{8,5},{9,8},{10,... | collective-permute-start | bytes 786440 | tf_op jit(solution)/shard_map/ppermute | solution.py:357
  137.3 8.3 %copy-start.1 = (bf16[32,4096]{1,0:T(8,128)(2,1)}, bf16[32,4096]{1,0:T(8,128)(2,1)S(1)}, u32[]{:S(2)}) copy-start(bf16[32,4096]{1,0:T(8,128)(2,1)S(1)} %get-tuple-element.78.refs_8_) | copy-start | bytes 786436
  137.4 8.3 %copy-start.2 = (bf16[32,4096]{1,0:T(8,128)(2,1)}, bf16[32,4096]{1,0:T(8,128)(2,1)S(1)}, u32[]{:S(2)}) copy-start(bf16[32,4096]{1,0:T(8,128)(2,1)S(1)} %get-tuple-element.75) | copy-start | bytes 786436
  137.4 8.3 %copy-start.4 = (bf16[32,4096]{1,0:T(8,128)(2,1)}, bf16[32,4096]{1,0:T(8,128)(2,1)S(1)}, u32[]{:S(2)}) copy-start(bf16[32,4096]{1,0:T(8,128)(2,1)S(1)} %get-tuple-element.77) | copy-start | bytes 786436
  137.4 8.3 %copy-start.5 = (bf16[32,4096]{1,0:T(8,128)(2,1)}, bf16[32,4096]{1,0:T(8,128)(2,1)S(1)}, u32[]{:S(2)}) copy-start(bf16[32,4096]{1,0:T(8,128)(2,1)S(1)} %get-tuple-element.76) | copy-start | bytes 786436
  145.7 14.4 %collective-permute-start.29 = (bf16[128,4224]{1,0:T(8,128)(2,1)S(1)}, bf16[128,4224]{1,0:T(8,128)(2,1)S(1)}, u32[]{:S(2)}, u32[]{:S(2)}) collective-permute-start(bf16[128,4224]{1,0:T(8,128)(2,1)S(1)} %get-tuple-element.84.refs_1_), channel_id=1, source_target_pairs={{0,16},{1,3},{2,18},{3,1},{4,20},{5,7},{6,22},{7,5},{8,24},{9,11},... | collective-permute-start | bytes 3244040 | tf_op jit(solution)/shard_map/ppermute | solution.py:357
  152.4 16.1 %collective-permute-start.30 = (bf16[128,3072]{1,0:T(8,128)(2,1)S(1)}, bf16[128,3072]{1,0:T(8,128)(2,1)}, u32[]{:S(2)}, u32[]{:S(2)}) collective-permute-start(bf16[128,3072]{1,0:T(8,128)(2,1)S(1)} %gate_up.15.refs_0_.refs_1_), channel_id=1, source_target_pairs={{0,16},{1,3},{2,18},{3,1},{4,20},{5,7},{6,22},{7,5},{8,24},{9,11},... | collective-permute-start | bytes 2359304 | tf_op jit(solution)/shard_map/ppermute | solution.py:357
  153.6 24.9 %collective-permute-start.21 = (bf16[32,4096]{1,0:T(8,128)(2,1)}, bf16[32,4096]{1,0:T(8,128)(2,1)S(1)}, u32[]{:S(2)}, u32[]{:S(2)}) collective-permute-start(bf16[32,4096]{1,0:T(8,128)(2,1)} %copy-done.1), channel_id=1, source_target_pairs={{0,16},{1,5},{2,18},{3,7},{4,20},{5,9},{6,22},{7,11},{8,24},{9,13}... | collective-permute-start | bytes 786440 | tf_op jit(solution)/shard_map/ppermute | solution.py:357
  153.7 24.4 %collective-permute-start.19 = (bf16[32,4096]{1,0:T(8,128)(2,1)}, bf16[32,4096]{1,0:T(8,128)(2,1)S(1)}, u32[]{:S(2)}, u32[]{:S(2)}) collective-permute-start(bf16[32,4096]{1,0:T(8,128)(2,1)} %copy-done.5), channel_id=1, source_target_pairs={{0,16},{1,13},{2,18},{3,15},{4,20},{5,1},{6,22},{7,3},{8,24},{9,5}... | collective-permute-start | bytes 786440 | tf_op jit(solution)/shard_map/ppermute | solution.py:357
  156.9 21.6 %collective-permute-start.20 = (bf16[32,4096]{1,0:T(8,128)(2,1)}, bf16[32,4096]{1,0:T(8,128)(2,1)S(1)}, u32[]{:S(2)}, u32[]{:S(2)}) collective-permute-start(bf16[32,4096]{1,0:T(8,128)(2,1)} %copy-done.4), channel_id=1, source_target_pairs={{0,16},{1,9},{2,18},{3,11},{4,20},{5,13},{6,22},{7,15},{8,24},{9,1... | collective-permute-start | bytes 786440 | tf_op jit(solution)/shard_map/ppermute | solution.py:357
  168.5 10.0 %copy-start.3 = (bf16[32,4096]{1,0:T(8,128)(2,1)S(1)}, bf16[32,4096]{1,0:T(8,128)(2,1)}, u32[]{:S(2)}) copy-start(bf16[32,4096]{1,0:T(8,128)(2,1)} %copy-done.2) | copy-start | bytes 786436
  175.6 14.5 %copy-start.8 = (bf16[32,4096]{1,0:T(8,128)(2,1)S(1)}, bf16[32,4096]{1,0:T(8,128)(2,1)}, u32[]{:S(2)}) copy-start(bf16[32,4096]{1,0:T(8,128)(2,1)} %copy-done.7) | copy-start | bytes 786436
  175.6 14.5 %copy-start.10 = (bf16[32,4096]{1,0:T(8,128)(2,1)S(1)}, bf16[32,4096]{1,0:T(8,128)(2,1)}, u32[]{:S(2)}) copy-start(bf16[32,4096]{1,0:T(8,128)(2,1)} %copy-done.9) | copy-start | bytes 786436
  175.6 5.9 %collective-permute-start.31 = (bf16[32,4096]{1,0:T(8,128)(2,1)S(1)}, bf16[32,4096]{1,0:T(8,128)(2,1)S(1)}, u32[]{:S(2)}, u32[]{:S(2)}) collective-permute-start(bf16[32,4096]{1,0:T(8,128)(2,1)S(1)} %get-tuple-element.88), channel_id=1, source_target_pairs={{0,16},{1,13},{2,18},{3,15},{4,20},{5,1},{6,22},{7,3},{8,24},{9,5}... | collective-permute-start | bytes 786440 | tf_op jit(solution)/shard_map/ppermute | solution.py:357
  178.2 11.7 %collective-permute-start.32 = (bf16[32,4096]{1,0:T(8,128)(2,1)S(1)}, bf16[32,4096]{1,0:T(8,128)(2,1)S(1)}, u32[]{:S(2)}, u32[]{:S(2)}) collective-permute-start(bf16[32,4096]{1,0:T(8,128)(2,1)S(1)} %get-tuple-element.89), channel_id=1, source_target_pairs={{0,16},{1,9},{2,18},{3,11},{4,20},{5,13},{6,22},{7,15},{8,24},{9,1... | collective-permute-start | bytes 786440 | tf_op jit(solution)/shard_map/ppermute | solution.py:357
  178.2 11.7 %collective-permute-start.33 = (bf16[32,4096]{1,0:T(8,128)(2,1)S(1)}, bf16[32,4096]{1,0:T(8,128)(2,1)S(1)}, u32[]{:S(2)}, u32[]{:S(2)}) collective-permute-start(bf16[32,4096]{1,0:T(8,128)(2,1)S(1)} %get-tuple-element.90), channel_id=1, source_target_pairs={{0,16},{1,5},{2,18},{3,7},{4,20},{5,9},{6,22},{7,11},{8,24},{9,13}... | collective-permute-start | bytes 786440 | tf_op jit(solution)/shard_map/ppermute | solution.py:357

commit v3 on v2

--- a/solution.py
+++ b/solution.py
@@ -115,9 +115,10 @@
         self.w_up, self.w_down = w_up, w_down
         self.kept = []
         self.before = []
+        self.share = 1
         self.depth, self.width = w_gate.shape[1:]
         self.half = self.depth // PARTS
-        self.load(w_gate)
+        self.w_gate = w_gate
 
     def call(self, section, kernel, operands, specs, out_shape, scratch, vmem, flops, moved, name):
         extras = [in_vmem(v) for v in self.kept] + self.before
@@ -139,13 +140,14 @@
             out_specs=[VMEM_SPEC] * len(out_shape),
             scratch_shapes=scratch,
             compiler_params=pltpu.CompilerParams(vmem_limit_bytes=vmem * MIB),
-            cost_estimate=pl.CostEstimate(flops=flops, bytes_accessed=moved, transcendentals=0),
+            cost_estimate=pl.CostEstimate(flops=flops // self.share, bytes_accessed=moved // self.share, transcendentals=0),
             name=name,
         )(*extras, *operands)
         self.before = [outs[-1]]
         return outs
 
-    def load(self, w_gate):
+    def load(self, section):
+        self.kept = []
         rows = self.depth // PIECES
         n = PIECES
 
@@ -160,9 +162,9 @@
                 copy.wait()
 
         self.kept = self.call(
-            None,
+            section,
             kernel,
-            [in_hbm(w_gate)],
+            [in_hbm(self.w_gate)],
             [HBM_SPEC],
             [pltpu.VMEM((rows, self.width), bf16)] * n,
             [pltpu.SemaphoreType.DMA((n,))],
@@ -171,7 +173,6 @@
             2 * n * rows * self.width,
             "load",
         )
-        self.before = []
 
     def gate_up(self, section, blocks, scaled_in, gain, start, size, tile):
         depth, half = self.depth, self.half
@@ -364,8 +365,6 @@
         k = Kernels(n_row, n_col, w_gate, w_up, w_down)
 
         def gathered(section, block):
-            if section:
-                return [move(block, routes.onward(section - 1, d)) for d in range(n_col)]
             return [block] + [move(block, routes.within(section, "col", d)) for d in range(1, n_col)]
 
         def exchanged(section, value):
@@ -391,25 +390,35 @@
                 if last < len(self.chunks):
                     self.acc, self.scale = outs
                     return
-                arrived = [
-                    move(outs[d], routes.within(self.section, "col", -d)) for d in range(1, n_col)
-                ]
-                total = outs[0].astype(f32)
+                block = self.blocks[0]
+                if self.section + 1 < n_section:
+                    arrived = [move(outs[d], routes.onward(self.section, -d)) for d in range(n_col)]
+                    if self.section:
+                        block = move(block, routes.onward(self.section, 0))
+                else:
+                    arrived = [outs[0]] + [
+                        move(outs[d], routes.within(self.section, "col", -d)) for d in range(1, n_col)
+                    ]
+                total = block.astype(f32)
                 for value in arrived:
                     total = total + value.astype(f32)
-                self.result = (self.blocks[0].astype(f32) + total).astype(bf16)
+                self.result = total.astype(bf16)
 
         jobs = {}
         steps = FLAT if (n_section, micro) == (2, 2) else in_turn(n_section, micro)
         for at, (what, section, m, *c) in enumerate(steps):
+            k.share = SHARES.get((what, section, m, *c), 1)
             if what == "n":
                 block = jobs[section - 1, m].result if section else tokens[m]
-                if jobs:
+                if k.before and jobs:
                     block, _ = lax.optimization_barrier((block, k.before[0]))
                 jobs[section, m] = Job(section, block, chunked(width, tile, *c))
+            elif what == "l":
+                k.load(section)
             elif what == "g":
                 jobs[section, m].gate_up(*c)
-                if not any(step[0] == "g" for step in steps[at + 1 :]):
+                later = [step[0] for step in steps[at + 1 :] if step[0] in "gl"]
+                if later[:1] != ["g"]:
                     k.kept = []
             else:
                 jobs[section, m].down(*c)
@@ -417,6 +426,7 @@
             jnp.stack([jobs[section, m].result for m in range(micro)], axis=0)
             for section in range(n_section)
         ]
+        outs = [move(v, routes.onward(s, 0)) for s, v in enumerate(outs[:-1])] + outs[-1:]
         out = outs[0]
         for section in range(1, n_section):
             out = jnp.where(section_index == section, outs[section], out)
@@ -451,10 +461,19 @@
 def in_turn(n_section, micro):
     steps = []
     for section in range(n_section):
+        steps += [("l", section, 0)]
         for m in range(micro):
             steps += [("n", section, m, 2), ("g", section, m, 0), ("g", section, m, 1)]
             steps += [("d", section, m, 0, 2)]
     return steps
 
 
-FLAT = [("n", 0, 0, 2), ("g", 0, 0, 0), ("n", 0, 1, 2), ("g", 0, 0, 1), ("g", 0, 1, 0), ("d", 0, 0, 0, 1), ("d", 0, 0, 1, 2), ("g", 0, 1, 1), ("d", 0, 1, 0, 1), ("n", 1, 0, 2), ("d", 0, 1, 1, 2),("g", 1, 0, 0), ("g", 1, 0, 1), ("n", 1, 1, 2), ("d", 1, 0, 0, 1), ("d", 1, 0, 1, 2), ("g", 1, 1, 0), ("g", 1, 1, 1), ("d", 1, 1, 0, 1), ("d", 1, 1, 1, 2),]
+SHARES = {("g", 1, 0, 0): 3, ("g", 1, 0, 1): 3, ("d", 1, 1, 0, 1): 10, ("d", 1, 1, 1, 2): 10}
+
+FLAT = [
+    ("l", None, 0),
+    ("n", 0, 0, 2), ("g", 0, 0, 0), ("n", 0, 1, 2), ("g", 0, 0, 1), ("g", 0, 1, 0), ("d", 0, 0, 0, 1),
+    ("d", 0, 0, 1, 2), ("g", 0, 1, 1), ("d", 0, 1, 0, 1), ("n", 1, 0, 2), ("d", 0, 1, 1, 2),
+    ("g", 1, 0, 0), ("g", 1, 0, 1), ("n", 1, 1, 2), ("d", 1, 0, 0, 1), ("g", 1, 1, 0), ("g", 1, 1, 1),
+    ("d", 1, 0, 1, 2), ("d", 1, 1, 0, 1), ("d", 1, 1, 1, 2),
+]

time: 191 us -> 182 us (0.953)
  waiting for transfers between devices: 75.6 us -> 51.7 us
  starting transfers between devices: 46.8 us -> 57 us
  Pallas kernels: 65.4 us -> 68.3 us
    ppermute x34 -> x35, waiting for transfers between devices: 75.6 us -> 51.7 us  [move(): return lax.ppermute(value, AXES, pairs)]
    ppermute x34 -> x35, starting transfers between devices: 46.8 us -> 57 us  [move(): return lax.ppermute(value, AXES, pairs)]
    pallas_call x17, Pallas kernels: 65.4 us -> 68.3 us  [call(): pl.pallas_call(wrapped, out_shape=out_shape, in_specs=[VMEM_SPEC] * n_kep...]
  transfers between devices with their start and end apart: 34 -> 35, of which waited for: 17 -> 10; matrix products, arithmetic and copies ran while one was open for 0% -> 0% of each run, Pallas kernels for 30% -> 38%
where the time goes in v3:
time: 182 us
  Pallas kernels  68.3 us (38%)
  starting transfers between devices  57 us (31%)
  waiting for transfers between devices  51.7 us (28%)
  local copies, waits for them, and re-layouts  2.67 us (1%)
    pallas_call x17, Pallas kernels, call(): pl.pallas_call(wrapped, out_shape=out_shape, in_specs=[VMEM_SPEC] * n_kep...  68.3 us
    ppermute x35, starting transfers between devices, move(): return lax.ppermute(value, AXES, pairs)  57 us
    ppermute x35, waiting for transfers between devices, move(): return lax.ppermute(value, AXES, pairs)  51.7 us
  transfers between devices with their start and end apart: 35, of which 10 were waited for; matrix products, arithmetic and copies ran while one was open for 0% of the time, Pallas kernels for 38%

profile of v3, /device:TPU:1, one launch (start us, length us, event | category | flops | bytes accessed | tf_op | source)
XLA Modules:
  0.0 181.6 jit_solution(8747819662200301327)
XLA Ops:
  0.0 1.1 slice_bitcast_fusion
  1.1 2.1 %collective-permute-start = (bf16[32,4096]{1,0:T(8,128)(2,1)S(1)}, bf16[32,4096]{1,0:T(8,128)(2,1)S(1)}, u32[]{:S(2)}, u32[]{:S(2)}) collective-permute-start(bf16[32,4096]{1,0:T(8,128)(2,1)S(1)} %get-tuple-element.92.refs_9_), channel_id=1, source_target_pairs={{0,4},{1,17},{2,6},{3,19},{4,8},{5,21},{6,10},{7,23},{8,12},{9,25}... | collective-permute-start | bytes 786440 | tf_op jit(solution)/shard_map/ppermute | solution.py:358
  3.3 1.4 collective-permute-start.2
  4.7 9.5 %load.1 = (bf16[512,3584]{1,0:T(8,128)(2,1)S(1)}, bf16[512,3584]{1,0:T(8,128)(2,1)S(1)}, bf16[512,3584]{1,0:T(8,128)(2,1)S(1)}, bf16[512,3584]{1,0:T(8,128)(2,1)...) custom-call(bf16[1,4096,3584]{2,1,0:T(8,128)(2,1)} %refs_0_.1), custom_call_target="tpu_custom_call" | custom-call | bytes 29360128 | tf_op jit(solution)/shard_map/load/pallas_call | solution.py:136
  14.3 0.2 collective-permute-start.3
  14.4 1.4 collective-permute-start.4
  15.9 1.4 collective-permute-start.6
  17.3 0.2 collective-permute-start.7
  17.5 2.1 %collective-permute-done.3.refs_10_ = bf16[32,4096]{1,0:T(8,128)(2,1)S(1)} collective-permute-done((bf16[32,4096]{1,0:T(8,128)(2,1)S(1)}, bf16[32,4096]{1,0:T(8,128)(2,1)S(1)}, u32[]{:S(2)}, u32[]{:S(2)}) %collective-permute-start.3) | collective-permute-done | bytes 262176 | tf_op jit(solution)/shard_map/ppermute | solution.py:358
  19.5 2.8 %collective-permute-done.4.refs_11_ = bf16[32,4096]{1,0:T(8,128)(2,1)S(1)} collective-permute-done((bf16[32,4096]{1,0:T(8,128)(2,1)S(1)}, bf16[32,4096]{1,0:T(8,128)(2,1)S(1)}, u32[]{:S(2)}, u32[]{:S(2)}) %collective-permute-start.4) | collective-permute-done | bytes 262176 | tf_op jit(solution)/shard_map/ppermute | solution.py:358
  22.3 2.8 %collective-permute-done.5.refs_12_ = bf16[32,4096]{1,0:T(8,128)(2,1)S(1)} collective-permute-done((bf16[32,4096]{1,0:T(8,128)(2,1)S(1)}, bf16[32,4096]{1,0:T(8,128)(2,1)S(1)}, u32[]{:S(2)}, u32[]{:S(2)}) %collective-permute-start.5) | collective-permute-done | bytes 262176 | tf_op jit(solution)/shard_map/ppermute | solution.py:358
  25.2 0.2 collective-permute-start.12
  25.4 11.7 %collective-permute-done.6.refs_10_ = bf16[128,4224]{1,0:T(8,128)(2,1)S(1)} collective-permute-done((bf16[128,4224]{1,0:T(8,128)(2,1)S(1)}, bf16[128,4224]{1,0:T(8,128)(2,1)S(1)}, u32[]{:S(2)}, u32[]{:S(2)}) %collective-permute-start.6) | collective-permute-done | bytes 1081376 | tf_op jit(solution)/shard_map/ppermute | solution.py:358
  37.1 8.4 %collective-permute-done.7.refs_10_ = bf16[128,3072]{1,0:T(8,128)(2,1)S(1)} collective-permute-done((bf16[128,3072]{1,0:T(8,128)(2,1)S(1)}, bf16[128,3072]{1,0:T(8,128)(2,1)S(1)}, u32[]{:S(2)}, u32[]{:S(2)}) %collective-permute-start.7) | collective-permute-done | bytes 786464 | tf_op jit(solution)/shard_map/ppermute | solution.py:358
  45.5 16.8 %collective-permute-start.10 = (bf16[32,4096]{1,0:T(8,128)(2,1)S(1)}, bf16[32,4096]{1,0:T(8,128)(2,1)S(1)}, u32[]{:S(2)}, u32[]{:S(2)}) collective-permute-start(bf16[32,4096]{1,0:T(8,128)(2,1)S(1)} %get-tuple-element.64), channel_id=1, source_target_pairs={{0,9},{1,0},{2,11},{3,2},{4,13},{5,4},{6,15},{7,6},{8,1},{9,8},{10... | collective-permute-start | bytes 786440 | tf_op jit(solution)/shard_map/ppermute | solution.py:358
  62.4 3.4 %collective-permute-start.8 = (bf16[32,4096]{1,0:T(8,128)(2,1)S(1)}, bf16[32,4096]{1,0:T(8,128)(2,1)S(1)}, u32[]{:S(2)}, u32[]{:S(2)}) collective-permute-start(bf16[32,4096]{1,0:T(8,128)(2,1)S(1)} %get-tuple-element.62), channel_id=1, source_target_pairs={{0,1},{1,0},{2,3},{3,2},{4,5},{5,4},{6,7},{7,6},{8,9},{9,8},{10,11... | collective-permute-start | bytes 786440 | tf_op jit(solution)/shard_map/ppermute | solution.py:358
  65.8 1.3 collective-permute-start.13
  67.2 6.9 %collective-permute-done.10 = bf16[32,4096]{1,0:T(8,128)(2,1)S(1)} collective-permute-done((bf16[32,4096]{1,0:T(8,128)(2,1)S(1)}, bf16[32,4096]{1,0:T(8,128)(2,1)S(1)}, u32[]{:S(2)}, u32[]{:S(2)}) %collective-permute-start.10) | collective-permute-done | bytes 262176 | tf_op jit(solution)/shard_map/ppermute | solution.py:358
  74.0 2.2 %collective-permute-done.9 = bf16[32,4096]{1,0:T(8,128)(2,1)S(1)} collective-permute-done((bf16[32,4096]{1,0:T(8,128)(2,1)S(1)}, bf16[32,4096]{1,0:T(8,128)(2,1)S(1)}, u32[]{:S(2)}, u32[]{:S(2)}) %collective-permute-start.9) | collective-permute-done | bytes 262176 | tf_op jit(solution)/shard_map/ppermute | solution.py:358
  76.4 1.2 collective-permute-start.14
  77.7 2.3 %collective-permute-start.16 = (bf16[32,4096]{1,0:T(8,128)(2,1)S(1)}, bf16[32,4096]{1,0:T(8,128)(2,1)S(1)}, u32[]{:S(2)}, u32[]{:S(2)}) collective-permute-start(bf16[32,4096]{1,0:T(8,128)(2,1)S(1)} %add_convert_fusion.3.refs_9_), channel_id=1, source_target_pairs={{0,16},{1,13},{2,18},{3,15},{4,20},{5,1},{6,22},{7,3},{8,24},{9,5}... | collective-permute-start | bytes 786440 | tf_op jit(solution)/shard_map/ppermute | solution.py:358
  80.0 10.6 %collective-permute-start.18 = (bf16[32,4096]{1,0:T(8,128)(2,1)S(1)}, bf16[32,4096]{1,0:T(8,128)(2,1)S(1)}, u32[]{:S(2)}, u32[]{:S(2)}) collective-permute-start(bf16[32,4096]{1,0:T(8,128)(2,1)S(1)} %get-tuple-element.74), channel_id=1, source_target_pairs={{0,1},{1,0},{2,3},{3,2},{4,5},{5,4},{6,7},{7,6},{8,9},{9,8},{10,11... | collective-permute-start | bytes 786440 | tf_op jit(solution)/shard_map/ppermute | solution.py:358
  90.7 1.7 collective-permute-start.20
  92.6 8.3 %gate_up.12 = (bf16[128,4224]{1,0:T(8,128)(2,1)S(1)}, bf16[128,4096]{1,0:T(8,128)(2,1)S(1)}) custom-call(bf16[512,3584]{1,0:T(8,128)(2,1)S(1)} %get-tuple-element.48.refs_0_, bf16[512,3584]{1,0:T(8,128)(2,1)S(1)} %get-tuple-element.49.refs_1_, bf16[512,3584]{1,0:T(8,128)(2,1)S(1)} %get-tuple-element.50.refs_2_, ...), custom_call_target="tpu_custom_call" | custom-call | flops 1431655808 | bytes 5592405 | tf_op jit(solution)/shard_map/gate_up/pallas_call | solution.py:136
  100.9 0.5 collective-permute-start.17
  101.4 6.3 %gate_up.13.refs_8_.refs_1_ = bf16[128,3072]{1,0:T(8,128)(2,1)S(1)} custom-call(bf16[512,3584]{1,0:T(8,128)(2,1)S(1)} %get-tuple-element.48.refs_0_, bf16[512,3584]{1,0:T(8,128)(2,1)S(1)} %get-tuple-element.49.refs_1_, bf16[512,3584]{1,0:T(8,128)(2,1)S(1)} %get-tuple-element.50.refs_2_, bf16[512,3584]{1,0:T(8,128)(2,1)S(1)} %get-tuple-element.51.refs_3_, ...), custom_call_target="tpu_custom_call" | custom-call | flops 1073741824 | bytes 4194304 | tf_op jit(solution)/shard_map/gate_up/pallas_call | solution.py:136
  107.8 0.2 add_convert_fusion.2.refs_9_
  107.9 0.2 collective-permute-start.22
  108.1 1.9 %collective-permute-start.23 = (bf16[32,4096]{1,0:T(8,128)(2,1)S(1)}, bf16[32,4096]{1,0:T(8,128)(2,1)S(1)}, u32[]{:S(2)}, u32[]{:S(2)}) collective-permute-start(bf16[32,4096]{1,0:T(8,128)(2,1)S(1)} %add_convert_fusion.2.refs_9_), channel_id=1, source_target_pairs={{0,16},{1,9},{2,18},{3,11},{4,20},{5,13},{6,22},{7,15},{8,24},{9,1... | collective-permute-start | bytes 786440 | tf_op jit(solution)/shard_map/ppermute | solution.py:358
  110.1 1.3 collective-permute-start.24
  111.4 1.0 collective-permute-start.25
  112.4 2.8 %collective-permute-done.17.refs_10_ = bf16[128,4224]{1,0:T(8,128)(2,1)S(1)} collective-permute-done((bf16[128,4224]{1,0:T(8,128)(2,1)S(1)}, bf16[128,4224]{1,0:T(8,128)(2,1)S(1)}, u32[]{:S(2)}, u32[]{:S(2)}) %collective-permute-start.17) | collective-permute-done | bytes 1081376 | tf_op jit(solution)/shard_map/ppermute | solution.py:358
  115.2 6.9 %down.12 = (f32[128,4096]{1,0:T(8,128)S(1)}, f32[128,128]{1,0:T(8,128)S(1)}) custom-call(bf16[512,3584]{1,0:T(8,128)(2,1)S(1)} %get-tuple-element.48.refs_0_, bf16[512,3584]{1,0:T(8,128)(2,1)S(1)} %get-tuple-element.49.refs_1_, bf16[512,3584]{1,0:T(8,128)(2,1)S(1)} %get-tuple-element.50.refs_2_, bf16[512,3584]{1,0:T(8,128)(2,1)S(1)} %get-tuple-element.51.refs_3_, ...), custom_call_target="tpu_custom_call" | custom-call | flops 2147483648 | bytes 16777216 | tf_op jit(solution)/shard_map/down/pallas_call | solution.py:136
  122.2 8.7 %gate_up.14 = (bf16[128,4224]{1,0:T(8,128)(2,1)S(1)}, bf16[128,4096]{1,0:T(8,128)(2,1)S(1)}) custom-call(bf16[512,3584]{1,0:T(8,128)(2,1)S(1)} %get-tuple-element.48.refs_0_, bf16[512,3584]{1,0:T(8,128)(2,1)S(1)} %get-tuple-element.49.refs_1_, bf16[512,3584]{1,0:T(8,128)(2,1)S(1)} %get-tuple-element.50.refs_2_, ...), custom_call_target="tpu_custom_call" | custom-call | flops 4294967296 | bytes 16777216 | tf_op jit(solution)/shard_map/gate_up/pallas_call | solution.py:136
  130.9 0.5 collective-permute-start.29
  131.4 6.3 %gate_up.15.refs_0_.refs_1_ = bf16[128,3072]{1,0:T(8,128)(2,1)S(1)} custom-call(bf16[512,3584]{1,0:T(8,128)(2,1)S(1)} %get-tuple-element.48.refs_0_, bf16[512,3584]{1,0:T(8,128)(2,1)S(1)} %get-tuple-element.49.refs_1_, bf16[512,3584]{1,0:T(8,128)(2,1)S(1)} %get-tuple-element.50.refs_2_, bf16[512,3584]{1,0:T(8,128)(2,1)S(1)} %get-tuple-element.51.refs_3_, ...), custom_call_target="tpu_custom_call" | custom-call | flops 3221225472 | bytes 12582912 | tf_op jit(solution)/shard_map/gate_up/pallas_call | solution.py:136
  137.7 1.1 collective-permute-start.30
  138.8 1.6 copy-done.1
  140.3 7.0 %down.13 = (bf16[32,4096]{1,0:T(8,128)(2,1)S(1)}, bf16[32,4096]{1,0:T(8,128)(2,1)S(1)}, bf16[32,4096]{1,0:T(8,128)(2,1)S(1)}, bf16[32,4096]{1,0:T(8,128)(2,1)S(1)}) custom-call(bf16[128,3072]{1,0:T(8,128)(2,1)S(1)} %gate_up.15.refs_0_.refs_1_, bf16[128,3072]{1,0:T(8,128)(2,1)S(1)} %gate_up.13.refs_8_.refs_1_, ...), custom_call_target="tpu_custom_call" | custom-call | flops 1610612736 | bytes 12582912 | tf_op jit(solution)/shard_map/down/pallas_call | solution.py:136
  147.4 1.9 %collective-permute-start.26 = (bf16[32,4096]{1,0:T(8,128)(2,1)S(1)}, bf16[32,4096]{1,0:T(8,128)(2,1)S(1)}, u32[]{:S(2)}, u32[]{:S(2)}) collective-permute-start(bf16[32,4096]{1,0:T(8,128)(2,1)S(1)} %get-tuple-element.81), channel_id=1, source_target_pairs={{0,16},{1,13},{2,18},{3,15},{4,20},{5,1},{6,22},{7,3},{8,24},{9,5}... | collective-permute-start | bytes 786440 | tf_op jit(solution)/shard_map/ppermute | solution.py:358
  149.3 0.6 collective-permute-start.28
  150.1 8.1 %down.14 = (f32[128,4096]{1,0:T(8,128)S(1)}, f32[128,128]{1,0:T(8,128)S(1)}) custom-call(bf16[32,4096]{1,0:T(8,128)(2,1)S(1)} %get-tuple-element.83.refs_0_, bf16[128,4224]{1,0:T(8,128)(2,1)S(1)} %get-tuple-element.84.refs_1_, bf16[128,4224]{1,0:T(8,128)(2,1)} %collective-permute-done.29.refs_2_, bf16[1,3584,4096]{2,1,0:T(8,128)(2,1)} %refs_3_.5), custom_call_target="tpu_custom_call" | custom-call | flops 214748368 | bytes 1677721 | tf_op jit(solution)/shard_map/down/pallas_call | solution.py:136
  158.2 7.0 %down.15 = (bf16[32,4096]{1,0:T(8,128)(2,1)S(1)}, bf16[32,4096]{1,0:T(8,128)(2,1)S(1)}, bf16[32,4096]{1,0:T(8,128)(2,1)S(1)}, bf16[32,4096]{1,0:T(8,128)(2,1)S(1)}) custom-call(f32[128,128]{1,0:T(8,128)S(1)} %get-tuple-element.85.refs_0_.refs_4_, bf16[128,3072]{1,0:T(8,128)(2,1)S(1)} %gate_up.15.refs_0_.refs_1_, ...), custom_call_target="tpu_custom_call" | custom-call | flops 161061280 | bytes 1258291 | tf_op jit(solution)/shard_map/down/pallas_call | solution.py:136
  165.2 2.7 %collective-permute-start.31 = (bf16[32,4096]{1,0:T(8,128)(2,1)S(1)}, bf16[32,4096]{1,0:T(8,128)(2,1)S(1)}, u32[]{:S(2)}, u32[]{:S(2)}) collective-permute-start(bf16[32,4096]{1,0:T(8,128)(2,1)S(1)} %get-tuple-element.88), channel_id=1, source_target_pairs={{0,16},{1,13},{2,18},{3,15},{4,20},{5,1},{6,22},{7,3},{8,24},{9,5}... | collective-permute-start | bytes 786440 | tf_op jit(solution)/shard_map/ppermute | solution.py:358
  167.9 0.5 collective-permute-start.32
  168.6 2.7 %collective-permute-done.31 = bf16[32,4096]{1,0:T(8,128)(2,1)S(1)} collective-permute-done((bf16[32,4096]{1,0:T(8,128)(2,1)S(1)}, bf16[32,4096]{1,0:T(8,128)(2,1)S(1)}, u32[]{:S(2)}, u32[]{:S(2)}) %collective-permute-start.31) | collective-permute-done | bytes 262176 | tf_op jit(solution)/shard_map/ppermute | solution.py:358
  171.3 9.3 %collective-permute-done.32 = bf16[32,4096]{1,0:T(8,128)(2,1)S(1)} collective-permute-done((bf16[32,4096]{1,0:T(8,128)(2,1)S(1)}, bf16[32,4096]{1,0:T(8,128)(2,1)S(1)}, u32[]{:S(2)}, u32[]{:S(2)}) %collective-permute-start.32) | collective-permute-done | bytes 262176 | tf_op jit(solution)/shard_map/ppermute | solution.py:358
  180.8 0.9 fusion
  (54 shorter events, 1.5 us)
Async XLA Ops:
  1.1 13.1 %copy-start.2 = (f32[1,4096]{1,0:T(1,128)S(1)}, f32[1,4096]{1,0:T(1,128)}, u32[]{:S(2)}) copy-start(f32[1,4096]{1,0:T(1,128)} %refs_10_.7) | copy-start | bytes 49156
  1.1 13.1 %collective-permute-start = (bf16[32,4096]{1,0:T(8,128)(2,1)S(1)}, bf16[32,4096]{1,0:T(8,128)(2,1)S(1)}, u32[]{:S(2)}, u32[]{:S(2)}) collective-permute-start(bf16[32,4096]{1,0:T(8,128)(2,1)S(1)} %get-tuple-element.92.refs_9_), channel_id=1, source_target_pairs={{0,4},{1,17},{2,6},{3,19},{4,8},{5,21},{6,10},{7,23},{8,12},{9,25}... | collective-permute-start | bytes 786440 | tf_op jit(solution)/shard_map/ppermute | solution.py:358
  3.2 11.0 %collective-permute-start.1 = (bf16[32,4096]{1,0:T(8,128)(2,1)S(1)}, bf16[32,4096]{1,0:T(8,128)(2,1)S(1)}, u32[]{:S(2)}, u32[]{:S(2)}) collective-permute-start(bf16[32,4096]{1,0:T(8,128)(2,1)S(1)} %get-tuple-element.92.refs_9_), channel_id=1, source_target_pairs={{0,8},{1,17},{2,10},{3,19},{4,12},{5,21},{6,14},{7,23},{8,0},{9,25... | collective-permute-start | bytes 786440 | tf_op jit(solution)/shard_map/ppermute | solution.py:358
  3.3 10.9 %collective-permute-start.2 = (bf16[32,4096]{1,0:T(8,128)(2,1)S(1)}, bf16[32,4096]{1,0:T(8,128)(2,1)S(1)}, u32[]{:S(2)}, u32[]{:S(2)}) collective-permute-start(bf16[32,4096]{1,0:T(8,128)(2,1)S(1)} %get-tuple-element.92.refs_9_), channel_id=1, source_target_pairs={{0,12},{1,17},{2,14},{3,19},{4,0},{5,21},{6,2},{7,23},{8,4},{9,25}... | collective-permute-start | bytes 786440 | tf_op jit(solution)/shard_map/ppermute | solution.py:358
  14.3 5.3 %collective-permute-start.3 = (bf16[32,4096]{1,0:T(8,128)(2,1)S(1)}, bf16[32,4096]{1,0:T(8,128)(2,1)S(1)}, u32[]{:S(2)}, u32[]{:S(2)}) collective-permute-start(bf16[32,4096]{1,0:T(8,128)(2,1)S(1)} %get-tuple-element.57.refs_9_), channel_id=1, source_target_pairs={{0,4},{1,17},{2,6},{3,19},{4,8},{5,21},{6,10},{7,23},{8,12},{9,25}... | collective-permute-start | bytes 786440 | tf_op jit(solution)/shard_map/ppermute | solution.py:358
  14.4 7.9 %collective-permute-start.4 = (bf16[32,4096]{1,0:T(8,128)(2,1)S(1)}, bf16[32,4096]{1,0:T(8,128)(2,1)S(1)}, u32[]{:S(2)}, u32[]{:S(2)}) collective-permute-start(bf16[32,4096]{1,0:T(8,128)(2,1)S(1)} %get-tuple-element.57.refs_9_), channel_id=1, source_target_pairs={{0,8},{1,17},{2,10},{3,19},{4,12},{5,21},{6,14},{7,23},{8,0},{9,25... | collective-permute-start | bytes 786440 | tf_op jit(solution)/shard_map/ppermute | solution.py:358
  15.8 9.4 %collective-permute-start.5 = (bf16[32,4096]{1,0:T(8,128)(2,1)S(1)}, bf16[32,4096]{1,0:T(8,128)(2,1)S(1)}, u32[]{:S(2)}, u32[]{:S(2)}) collective-permute-start(bf16[32,4096]{1,0:T(8,128)(2,1)S(1)} %get-tuple-element.57.refs_9_), channel_id=1, source_target_pairs={{0,12},{1,17},{2,14},{3,19},{4,0},{5,21},{6,2},{7,23},{8,4},{9,25}... | collective-permute-start | bytes 786440 | tf_op jit(solution)/shard_map/ppermute | solution.py:358
  15.9 21.1 %collective-permute-start.6 = (bf16[128,4224]{1,0:T(8,128)(2,1)S(1)}, bf16[128,4224]{1,0:T(8,128)(2,1)S(1)}, u32[]{:S(2)}, u32[]{:S(2)}) collective-permute-start(bf16[128,4224]{1,0:T(8,128)(2,1)S(1)} %get-tuple-element.59.refs_9_), channel_id=1, source_target_pairs={{0,2},{1,17},{2,0},{3,19},{4,6},{5,21},{6,4},{7,23},{8,10},{9,25},... | collective-permute-start | bytes 3244040 | tf_op jit(solution)/shard_map/ppermute | solution.py:358
  17.3 28.2 %collective-permute-start.7 = (bf16[128,3072]{1,0:T(8,128)(2,1)S(1)}, bf16[128,3072]{1,0:T(8,128)(2,1)S(1)}, u32[]{:S(2)}, u32[]{:S(2)}) collective-permute-start(bf16[128,3072]{1,0:T(8,128)(2,1)S(1)} %gate_up.9.refs_8_.refs_9_), channel_id=1, source_target_pairs={{0,2},{1,17},{2,0},{3,19},{4,6},{5,21},{6,4},{7,23},{8,10},{9,25},... | collective-permute-start | bytes 2359304 | tf_op jit(solution)/shard_map/ppermute | solution.py:358
  25.2 40.6 %collective-permute-start.12 = (bf16[128,4224]{1,0:T(8,128)(2,1)S(1)}, bf16[128,4224]{1,0:T(8,128)(2,1)S(1)}, u32[]{:S(2)}, u32[]{:S(2)}) collective-permute-start(bf16[128,4224]{1,0:T(8,128)(2,1)S(1)} %get-tuple-element.66.refs_9_), channel_id=1, source_target_pairs={{0,2},{1,17},{2,0},{3,19},{4,6},{5,21},{6,4},{7,23},{8,10},{9,25},... | collective-permute-start | bytes 3244040 | tf_op jit(solution)/shard_map/ppermute | solution.py:358
  45.5 28.5 %collective-permute-start.10 = (bf16[32,4096]{1,0:T(8,128)(2,1)S(1)}, bf16[32,4096]{1,0:T(8,128)(2,1)S(1)}, u32[]{:S(2)}, u32[]{:S(2)}) collective-permute-start(bf16[32,4096]{1,0:T(8,128)(2,1)S(1)} %get-tuple-element.64), channel_id=1, source_target_pairs={{0,9},{1,0},{2,11},{3,2},{4,13},{5,4},{6,15},{7,6},{8,1},{9,8},{10... | collective-permute-start | bytes 786440 | tf_op jit(solution)/shard_map/ppermute | solution.py:358
  62.3 11.7 %collective-permute-start.11 = (bf16[32,4096]{1,0:T(8,128)(2,1)S(1)}, bf16[32,4096]{1,0:T(8,128)(2,1)S(1)}, u32[]{:S(2)}, u32[]{:S(2)}) collective-permute-start(bf16[32,4096]{1,0:T(8,128)(2,1)S(1)} %get-tuple-element.65.refs_8_), channel_id=1, source_target_pairs={{0,5},{1,0},{2,7},{3,2},{4,9},{5,4},{6,11},{7,6},{8,13},{9,8},{10,... | collective-permute-start | bytes 786440 | tf_op jit(solution)/shard_map/ppermute | solution.py:358
  62.4 11.7 %collective-permute-start.8 = (bf16[32,4096]{1,0:T(8,128)(2,1)S(1)}, bf16[32,4096]{1,0:T(8,128)(2,1)S(1)}, u32[]{:S(2)}, u32[]{:S(2)}) collective-permute-start(bf16[32,4096]{1,0:T(8,128)(2,1)S(1)} %get-tuple-element.62), channel_id=1, source_target_pairs={{0,1},{1,0},{2,3},{3,2},{4,5},{5,4},{6,7},{7,6},{8,9},{9,8},{10,11... | collective-permute-start | bytes 786440 | tf_op jit(solution)/shard_map/ppermute | solution.py:358
  65.8 10.5 %collective-permute-start.9 = (bf16[32,4096]{1,0:T(8,128)(2,1)S(1)}, bf16[32,4096]{1,0:T(8,128)(2,1)S(1)}, u32[]{:S(2)}, u32[]{:S(2)}) collective-permute-start(bf16[32,4096]{1,0:T(8,128)(2,1)S(1)} %get-tuple-element.63), channel_id=1, source_target_pairs={{0,13},{1,0},{2,15},{3,2},{4,1},{5,4},{6,3},{7,6},{8,5},{9,8},{10,... | collective-permute-start | bytes 786440 | tf_op jit(solution)/shard_map/ppermute | solution.py:358
  65.8 10.4 %copy-start.3 = (bf16[2,32,4096]{2,1,0:T(8,128)(2,1)S(1)}, bf16[2,32,4096]{2,1,0:T(8,128)(2,1)}, u32[]{:S(2)}) copy-start(bf16[2,32,4096]{2,1,0:T(8,128)(2,1)} %param.5) | copy-start | bytes 1572868
  65.8 14.1 %collective-permute-start.13 = (bf16[128,3072]{1,0:T(8,128)(2,1)S(1)}, bf16[128,3072]{1,0:T(8,128)(2,1)S(1)}, u32[]{:S(2)}, u32[]{:S(2)}) collective-permute-start(bf16[128,3072]{1,0:T(8,128)(2,1)S(1)} %gate_up.11.refs_8_.refs_9_), channel_id=1, source_target_pairs={{0,2},{1,17},{2,0},{3,19},{4,6},{5,21},{6,4},{7,23},{8,10},{9,25},... | collective-permute-start | bytes 2359304 | tf_op jit(solution)/shard_map/ppermute | solution.py:358
  76.4 14.3 %collective-permute-start.14 = (bf16[32,4096]{1,0:T(8,128)(2,1)S(1)}, bf16[32,4096]{1,0:T(8,128)(2,1)S(1)}, u32[]{:S(2)}, u32[]{:S(2)}) collective-permute-start(bf16[32,4096]{1,0:T(8,128)(2,1)S(1)} %add_convert_fusion.3.refs_9_), channel_id=1, source_target_pairs={{0,16},{1,5},{2,18},{3,7},{4,20},{5,9},{6,22},{7,11},{8,24},{9,13}... | collective-permute-start | bytes 786440 | tf_op jit(solution)/shard_map/ppermute | solution.py:358
  77.6 14.9 %collective-permute-start.15 = (bf16[32,4096]{1,0:T(8,128)(2,1)S(1)}, bf16[32,4096]{1,0:T(8,128)(2,1)S(1)}, u32[]{:S(2)}, u32[]{:S(2)}) collective-permute-start(bf16[32,4096]{1,0:T(8,128)(2,1)S(1)} %add_convert_fusion.3.refs_9_), channel_id=1, source_target_pairs={{0,16},{1,9},{2,18},{3,11},{4,20},{5,13},{6,22},{7,15},{8,24},{9,1... | collective-permute-start | bytes 786440 | tf_op jit(solution)/shard_map/ppermute | solution.py:358
  77.7 14.9 %collective-permute-start.16 = (bf16[32,4096]{1,0:T(8,128)(2,1)S(1)}, bf16[32,4096]{1,0:T(8,128)(2,1)S(1)}, u32[]{:S(2)}, u32[]{:S(2)}) collective-permute-start(bf16[32,4096]{1,0:T(8,128)(2,1)S(1)} %add_convert_fusion.3.refs_9_), channel_id=1, source_target_pairs={{0,16},{1,13},{2,18},{3,15},{4,20},{5,1},{6,22},{7,3},{8,24},{9,5}... | collective-permute-start | bytes 786440 | tf_op jit(solution)/shard_map/ppermute | solution.py:358
  80.0 27.7 %collective-permute-start.18 = (bf16[32,4096]{1,0:T(8,128)(2,1)S(1)}, bf16[32,4096]{1,0:T(8,128)(2,1)S(1)}, u32[]{:S(2)}, u32[]{:S(2)}) collective-permute-start(bf16[32,4096]{1,0:T(8,128)(2,1)S(1)} %get-tuple-element.74), channel_id=1, source_target_pairs={{0,1},{1,0},{2,3},{3,2},{4,5},{5,4},{6,7},{7,6},{8,9},{9,8},{10,11... | collective-permute-start | bytes 786440 | tf_op jit(solution)/shard_map/ppermute | solution.py:358
  90.7 17.1 %collective-permute-start.19 = (bf16[32,4096]{1,0:T(8,128)(2,1)S(1)}, bf16[32,4096]{1,0:T(8,128)(2,1)S(1)}, u32[]{:S(2)}, u32[]{:S(2)}) collective-permute-start(bf16[32,4096]{1,0:T(8,128)(2,1)S(1)} %get-tuple-element.75), channel_id=1, source_target_pairs={{0,13},{1,0},{2,15},{3,2},{4,1},{5,4},{6,3},{7,6},{8,5},{9,8},{10,... | collective-permute-start | bytes 786440 | tf_op jit(solution)/shard_map/ppermute | solution.py:358
  90.7 17.0 %collective-permute-start.20 = (bf16[32,4096]{1,0:T(8,128)(2,1)S(1)}, bf16[32,4096]{1,0:T(8,128)(2,1)S(1)}, u32[]{:S(2)}, u32[]{:S(2)}) collective-permute-start(bf16[32,4096]{1,0:T(8,128)(2,1)S(1)} %get-tuple-element.76), channel_id=1, source_target_pairs={{0,9},{1,0},{2,11},{3,2},{4,13},{5,4},{6,15},{7,6},{8,1},{9,8},{10... | collective-permute-start | bytes 786440 | tf_op jit(solution)/shard_map/ppermute | solution.py:358
  92.5 15.3 %collective-permute-start.21 = (bf16[32,4096]{1,0:T(8,128)(2,1)S(1)}, bf16[32,4096]{1,0:T(8,128)(2,1)S(1)}, u32[]{:S(2)}, u32[]{:S(2)}) collective-permute-start(bf16[32,4096]{1,0:T(8,128)(2,1)S(1)} %get-tuple-element.70.refs_8_), channel_id=1, source_target_pairs={{0,5},{1,0},{2,7},{3,2},{4,9},{5,4},{6,11},{7,6},{8,13},{9,8},{10,... | collective-permute-start | bytes 786440 | tf_op jit(solution)/shard_map/ppermute | solution.py:358
  100.9 14.4 %collective-permute-start.17 = (bf16[128,4224]{1,0:T(8,128)(2,1)S(1)}, bf16[128,4224]{1,0:T(8,128)(2,1)S(1)}, u32[]{:S(2)}, u32[]{:S(2)}) collective-permute-start(bf16[128,4224]{1,0:T(8,128)(2,1)S(1)} %get-tuple-element.72.refs_9_), channel_id=1, source_target_pairs={{0,16},{1,3},{2,18},{3,1},{4,20},{5,7},{6,22},{7,5},{8,24},{9,11},... | collective-permute-start | bytes 3244040 | tf_op jit(solution)/shard_map/ppermute | solution.py:358
  107.9 14.2 %collective-permute-start.22 = (bf16[32,4096]{1,0:T(8,128)(2,1)S(1)}, bf16[32,4096]{1,0:T(8,128)(2,1)S(1)}, u32[]{:S(2)}, u32[]{:S(2)}) collective-permute-start(bf16[32,4096]{1,0:T(8,128)(2,1)S(1)} %add_convert_fusion.2.refs_9_), channel_id=1, source_target_pairs={{0,16},{1,5},{2,18},{3,7},{4,20},{5,9},{6,22},{7,11},{8,24},{9,13}... | collective-permute-start | bytes 786440 | tf_op jit(solution)/shard_map/ppermute | solution.py:358
  108.1 14.0 %collective-permute-start.23 = (bf16[32,4096]{1,0:T(8,128)(2,1)S(1)}, bf16[32,4096]{1,0:T(8,128)(2,1)S(1)}, u32[]{:S(2)}, u32[]{:S(2)}) collective-permute-start(bf16[32,4096]{1,0:T(8,128)(2,1)S(1)} %add_convert_fusion.2.refs_9_), channel_id=1, source_target_pairs={{0,16},{1,9},{2,18},{3,11},{4,20},{5,13},{6,22},{7,15},{8,24},{9,1... | collective-permute-start | bytes 786440 | tf_op jit(solution)/shard_map/ppermute | solution.py:358
  110.1 12.1 %collective-permute-start.24 = (bf16[32,4096]{1,0:T(8,128)(2,1)S(1)}, bf16[32,4096]{1,0:T(8,128)(2,1)S(1)}, u32[]{:S(2)}, u32[]{:S(2)}) collective-permute-start(bf16[32,4096]{1,0:T(8,128)(2,1)S(1)} %add_convert_fusion.2.refs_9_), channel_id=1, source_target_pairs={{0,16},{1,13},{2,18},{3,15},{4,20},{5,1},{6,22},{7,3},{8,24},{9,5}... | collective-permute-start | bytes 786440 | tf_op jit(solution)/shard_map/ppermute | solution.py:358
  111.4 27.4 %collective-permute-start.25 = (bf16[128,3072]{1,0:T(8,128)(2,1)S(1)}, bf16[128,3072]{1,0:T(8,128)(2,1)}, u32[]{:S(2)}, u32[]{:S(2)}) collective-permute-start(bf16[128,3072]{1,0:T(8,128)(2,1)S(1)} %gate_up.13.refs_8_.refs_1_), channel_id=1, source_target_pairs={{0,16},{1,3},{2,18},{3,1},{4,20},{5,7},{6,22},{7,5},{8,24},{9,11},... | collective-permute-start | bytes 2359304 | tf_op jit(solution)/shard_map/ppermute | solution.py:358
  122.1 8.7 %copy-start = (f32[128,4096]{1,0:T(8,128)}, f32[128,4096]{1,0:T(8,128)S(1)}, u32[]{:S(2)}) copy-start(f32[128,4096]{1,0:T(8,128)S(1)} %get-tuple-element.79.refs_5_) | copy-start | bytes 6291460
  130.9 19.1 %collective-permute-start.29 = (bf16[128,4224]{1,0:T(8,128)(2,1)S(1)}, bf16[128,4224]{1,0:T(8,128)(2,1)}, u32[]{:S(2)}, u32[]{:S(2)}) collective-permute-start(bf16[128,4224]{1,0:T(8,128)(2,1)S(1)} %get-tuple-element.84.refs_1_), channel_id=1, source_target_pairs={{0,16},{1,3},{2,18},{3,1},{4,20},{5,7},{6,22},{7,5},{8,24},{9,11},... | collective-permute-start | bytes 3244040 | tf_op jit(solution)/shard_map/ppermute | solution.py:358
  137.7 20.5 %collective-permute-start.30 = (bf16[128,3072]{1,0:T(8,128)(2,1)S(1)}, bf16[128,3072]{1,0:T(8,128)(2,1)}, u32[]{:S(2)}, u32[]{:S(2)}) collective-permute-start(bf16[128,3072]{1,0:T(8,128)(2,1)S(1)} %gate_up.15.refs_0_.refs_1_), channel_id=1, source_target_pairs={{0,16},{1,3},{2,18},{3,1},{4,20},{5,7},{6,22},{7,5},{8,24},{9,11},... | collective-permute-start | bytes 2359304 | tf_op jit(solution)/shard_map/ppermute | solution.py:358
  138.8 1.6 copy-start.1
  147.4 20.6 %collective-permute-start.26 = (bf16[32,4096]{1,0:T(8,128)(2,1)S(1)}, bf16[32,4096]{1,0:T(8,128)(2,1)S(1)}, u32[]{:S(2)}, u32[]{:S(2)}) collective-permute-start(bf16[32,4096]{1,0:T(8,128)(2,1)S(1)} %get-tuple-element.81), channel_id=1, source_target_pairs={{0,16},{1,13},{2,18},{3,15},{4,20},{5,1},{6,22},{7,3},{8,24},{9,5}... | collective-permute-start | bytes 786440 | tf_op jit(solution)/shard_map/ppermute | solution.py:358
  149.2 19.2 %collective-permute-start.27 = (bf16[32,4096]{1,0:T(8,128)(2,1)S(1)}, bf16[32,4096]{1,0:T(8,128)(2,1)S(1)}, u32[]{:S(2)}, u32[]{:S(2)}) collective-permute-start(bf16[32,4096]{1,0:T(8,128)(2,1)S(1)} %get-tuple-element.82), channel_id=1, source_target_pairs={{0,16},{1,9},{2,18},{3,11},{4,20},{5,13},{6,22},{7,15},{8,24},{9,1... | collective-permute-start | bytes 786440 | tf_op jit(solution)/shard_map/ppermute | solution.py:358
  149.3 19.1 %collective-permute-start.28 = (bf16[32,4096]{1,0:T(8,128)(2,1)S(1)}, bf16[32,4096]{1,0:T(8,128)(2,1)S(1)}, u32[]{:S(2)}, u32[]{:S(2)}) collective-permute-start(bf16[32,4096]{1,0:T(8,128)(2,1)S(1)} %get-tuple-element.83.refs_0_), channel_id=1, source_target_pairs={{0,16},{1,5},{2,18},{3,7},{4,20},{5,9},{6,22},{7,11},{8,24},{9,13}... | collective-permute-start | bytes 786440 | tf_op jit(solution)/shard_map/ppermute | solution.py:358
  150.0 30.8 %collective-permute-start.34 = (bf16[2,32,4096]{2,1,0:T(8,128)(2,1)S(1)}, bf16[2,32,4096]{2,1,0:T(8,128)(2,1)S(1)}, u32[]{:S(2)}, u32[]{:S(2)}) collective-permute-start(bf16[2,32,4096]{2,1,0:T(8,128)(2,1)S(1)} %pad_maximum_fusion), channel_id=1, source_target_pairs={{0,1},{1,0},{2,3},{3,2},{4,5},{5,4},{6,7},{7,6},{8,9},{9,8},{10,11... | collective-permute-start | bytes 1572872 | tf_op jit(solution)/shard_map/ppermute | solution.py:358
  165.2 6.1 %collective-permute-start.31 = (bf16[32,4096]{1,0:T(8,128)(2,1)S(1)}, bf16[32,4096]{1,0:T(8,128)(2,1)S(1)}, u32[]{:S(2)}, u32[]{:S(2)}) collective-permute-start(bf16[32,4096]{1,0:T(8,128)(2,1)S(1)} %get-tuple-element.88), channel_id=1, source_target_pairs={{0,16},{1,13},{2,18},{3,15},{4,20},{5,1},{6,22},{7,3},{8,24},{9,5}... | collective-permute-start | bytes 786440 | tf_op jit(solution)/shard_map/ppermute | solution.py:358
  167.9 12.6 %collective-permute-start.32 = (bf16[32,4096]{1,0:T(8,128)(2,1)S(1)}, bf16[32,4096]{1,0:T(8,128)(2,1)S(1)}, u32[]{:S(2)}, u32[]{:S(2)}) collective-permute-start(bf16[32,4096]{1,0:T(8,128)(2,1)S(1)} %get-tuple-element.89), channel_id=1, source_target_pairs={{0,16},{1,9},{2,18},{3,11},{4,20},{5,13},{6,22},{7,15},{8,24},{9,1... | collective-permute-start | bytes 786440 | tf_op jit(solution)/shard_map/ppermute | solution.py:358
  168.4 12.2 %collective-permute-start.33 = (bf16[32,4096]{1,0:T(8,128)(2,1)S(1)}, bf16[32,4096]{1,0:T(8,128)(2,1)S(1)}, u32[]{:S(2)}, u32[]{:S(2)}) collective-permute-start(bf16[32,4096]{1,0:T(8,128)(2,1)S(1)} %get-tuple-element.90), channel_id=1, source_target_pairs={{0,16},{1,5},{2,18},{3,7},{4,20},{5,9},{6,22},{7,11},{8,24},{9,13}... | collective-permute-start | bytes 786440 | tf_op jit(solution)/shard_map/ppermute | solution.py:358

commit v4 on v3

--- a/solution.py
+++ b/solution.py
@@ -9,6 +9,7 @@
 MIB = 1 << 20
 LANES = 128
 BUFFERS = 3
+DOWN_BUFFERS = 4
 VMEM_MIB = 12
 PIECES = 8
 PARTS = 2
@@ -82,24 +83,24 @@
         return pairs
 
 
-def streamed(count, parts, copy, body):
+def streamed(count, parts, slots, copy, body):
     def start(q):
         tile, part = (q // parts, q % parts) if isinstance(q, int) else (lax.div(q, parts), lax.rem(q, parts))
-        copy(tile, part, q % BUFFERS if isinstance(q, int) else lax.rem(q, BUFFERS)).start()
-
-    for q in range(min(BUFFERS, count * parts)):
+        copy(tile, part, q % slots if isinstance(q, int) else lax.rem(q, slots)).start()
+
+    for q in range(min(slots, count * parts)):
         start(q)
 
     def step(i, carry):
         def use(part, f):
             q = i * parts + part
-            slot = lax.rem(q, BUFFERS)
+            slot = lax.rem(q, slots)
             copy(i, part, slot).wait()
             value = f(slot)
 
-            @pl.when(q + BUFFERS < count * parts)
+            @pl.when(q + slots < count * parts)
             def _():
-                start(q + BUFFERS)
+                start(q + slots)
 
             return value
 
@@ -230,7 +231,7 @@
                     up = up + use(part, lambda slot: product(part * half, buf[slot]))
                 out[:, pl.ds(pl.multiple_of(size + offset, tile), tile)] = up.astype(bf16)
 
-            run = streamed(size // tile, PARTS, copy, body)
+            run = streamed(size // tile, PARTS, BUFFERS, copy, body)
             scaled = sources[0]
             if opens:
                 scaled = refs[1]
@@ -267,6 +268,7 @@
         opens, last = start == 0, start + size == self.width
         parts = -(-size // WIDEST)
         deep = size // parts
+        slots = DOWN_BUFFERS
         features = self.depth * n_row
         flat = [in_vmem(v) for group in sums for v in group]
         n = len(flat)
@@ -297,7 +299,7 @@
                 else:
                     outs[0][:, place] = total
 
-            run = streamed(columns // tile, parts, copy, body)
+            run = streamed(columns // tile, parts, slots, copy, body)
             for first in range(0, rows, tok):
                 place = slice(first, first + tok)
                 for c, (begin, width) in enumerate(chunks):
@@ -339,8 +341,8 @@
             out_shape,
             [
                 pltpu.VMEM((rows, size), bf16),
-                pltpu.VMEM((BUFFERS, deep, tile), bf16),
-                pltpu.SemaphoreType.DMA((BUFFERS,)),
+                pltpu.VMEM((slots, deep, tile), bf16),
+                pltpu.SemaphoreType.DMA((slots,)),
             ],
             VMEM_MIB,
             2 * rows * size * columns,

time: 182 us -> 179 us (0.984)
  transfers between devices with their start and end apart: 35 -> 35, of which waited for: 10 -> 10; matrix products, arithmetic and copies ran while one was open for 0% -> 0% of each run, Pallas kernels for 38% -> 37%
where the time goes in v4:
time: 179 us
  Pallas kernels  67 us (37%)
  starting transfers between devices  56.1 us (31%)
  waiting for transfers between devices  51.4 us (29%)
  local copies, waits for them, and re-layouts  2.67 us (1%)
    pallas_call x17, Pallas kernels, call(): pl.pallas_call(wrapped, out_shape=out_shape, in_specs=[VMEM_SPEC] * n_kep...  67 us
    ppermute x35, starting transfers between devices, move(): return lax.ppermute(value, AXES, pairs)  56.1 us
    ppermute x35, waiting for transfers between devices, move(): return lax.ppermute(value, AXES, pairs)  51.4 us
  transfers between devices with their start and end apart: 35, of which 10 were waited for; matrix products, arithmetic and copies ran while one was open for 0% of the time, Pallas kernels for 37%

profile of v4, /device:TPU:1, one launch (start us, length us, event | category | flops | bytes accessed | tf_op | source)
XLA Modules:
  0.0 179.1 jit_solution(8851021451087364789)
XLA Ops:
  0.0 1.1 slice_bitcast_fusion
  1.1 2.1 %collective-permute-start = (bf16[32,4096]{1,0:T(8,128)(2,1)S(1)}, bf16[32,4096]{1,0:T(8,128)(2,1)S(1)}, u32[]{:S(2)}, u32[]{:S(2)}) collective-permute-start(bf16[32,4096]{1,0:T(8,128)(2,1)S(1)} %get-tuple-element.92.refs_9_), channel_id=1, source_target_pairs={{0,4},{1,17},{2,6},{3,19},{4,8},{5,21},{6,10},{7,23},{8,12},{9,25}... | collective-permute-start | bytes 786440 | tf_op jit(solution)/shard_map/ppermute | solution.py:360
  3.3 1.4 collective-permute-start.2
  4.7 9.5 %load.1 = (bf16[512,3584]{1,0:T(8,128)(2,1)S(1)}, bf16[512,3584]{1,0:T(8,128)(2,1)S(1)}, bf16[512,3584]{1,0:T(8,128)(2,1)S(1)}, bf16[512,3584]{1,0:T(8,128)(2,1)...) custom-call(bf16[1,4096,3584]{2,1,0:T(8,128)(2,1)} %refs_0_.1), custom_call_target="tpu_custom_call" | custom-call | bytes 29360128 | tf_op jit(solution)/shard_map/load/pallas_call | solution.py:137
  14.3 0.2 collective-permute-start.3
  14.4 1.4 collective-permute-start.4
  15.9 1.4 collective-permute-start.6
  17.3 0.2 collective-permute-start.7
  17.5 2.1 %collective-permute-done.3.refs_10_ = bf16[32,4096]{1,0:T(8,128)(2,1)S(1)} collective-permute-done((bf16[32,4096]{1,0:T(8,128)(2,1)S(1)}, bf16[32,4096]{1,0:T(8,128)(2,1)S(1)}, u32[]{:S(2)}, u32[]{:S(2)}) %collective-permute-start.3) | collective-permute-done | bytes 262176 | tf_op jit(solution)/shard_map/ppermute | solution.py:360
  19.5 2.8 %collective-permute-done.4.refs_11_ = bf16[32,4096]{1,0:T(8,128)(2,1)S(1)} collective-permute-done((bf16[32,4096]{1,0:T(8,128)(2,1)S(1)}, bf16[32,4096]{1,0:T(8,128)(2,1)S(1)}, u32[]{:S(2)}, u32[]{:S(2)}) %collective-permute-start.4) | collective-permute-done | bytes 262176 | tf_op jit(solution)/shard_map/ppermute | solution.py:360
  22.3 2.8 %collective-permute-done.5.refs_12_ = bf16[32,4096]{1,0:T(8,128)(2,1)S(1)} collective-permute-done((bf16[32,4096]{1,0:T(8,128)(2,1)S(1)}, bf16[32,4096]{1,0:T(8,128)(2,1)S(1)}, u32[]{:S(2)}, u32[]{:S(2)}) %collective-permute-start.5) | collective-permute-done | bytes 262176 | tf_op jit(solution)/shard_map/ppermute | solution.py:360
  25.2 0.2 collective-permute-start.12
  25.4 11.7 %collective-permute-done.6.refs_10_ = bf16[128,4224]{1,0:T(8,128)(2,1)S(1)} collective-permute-done((bf16[128,4224]{1,0:T(8,128)(2,1)S(1)}, bf16[128,4224]{1,0:T(8,128)(2,1)S(1)}, u32[]{:S(2)}, u32[]{:S(2)}) %collective-permute-start.6) | collective-permute-done | bytes 1081376 | tf_op jit(solution)/shard_map/ppermute | solution.py:360
  37.1 8.4 %collective-permute-done.7.refs_10_ = bf16[128,3072]{1,0:T(8,128)(2,1)S(1)} collective-permute-done((bf16[128,3072]{1,0:T(8,128)(2,1)S(1)}, bf16[128,3072]{1,0:T(8,128)(2,1)S(1)}, u32[]{:S(2)}, u32[]{:S(2)}) %collective-permute-start.7) | collective-permute-done | bytes 786464 | tf_op jit(solution)/shard_map/ppermute | solution.py:360
  45.5 16.1 %collective-permute-start.10 = (bf16[32,4096]{1,0:T(8,128)(2,1)S(1)}, bf16[32,4096]{1,0:T(8,128)(2,1)S(1)}, u32[]{:S(2)}, u32[]{:S(2)}) collective-permute-start(bf16[32,4096]{1,0:T(8,128)(2,1)S(1)} %get-tuple-element.64), channel_id=1, source_target_pairs={{0,9},{1,0},{2,11},{3,2},{4,13},{5,4},{6,15},{7,6},{8,1},{9,8},{10... | collective-permute-start | bytes 786440 | tf_op jit(solution)/shard_map/ppermute | solution.py:360
  61.7 3.4 %collective-permute-start.8 = (bf16[32,4096]{1,0:T(8,128)(2,1)S(1)}, bf16[32,4096]{1,0:T(8,128)(2,1)S(1)}, u32[]{:S(2)}, u32[]{:S(2)}) collective-permute-start(bf16[32,4096]{1,0:T(8,128)(2,1)S(1)} %get-tuple-element.62), channel_id=1, source_target_pairs={{0,1},{1,0},{2,3},{3,2},{4,5},{5,4},{6,7},{7,6},{8,9},{9,8},{10,11... | collective-permute-start | bytes 786440 | tf_op jit(solution)/shard_map/ppermute | solution.py:360
  65.1 1.3 collective-permute-start.13
  66.5 6.9 %collective-permute-done.10 = bf16[32,4096]{1,0:T(8,128)(2,1)S(1)} collective-permute-done((bf16[32,4096]{1,0:T(8,128)(2,1)S(1)}, bf16[32,4096]{1,0:T(8,128)(2,1)S(1)}, u32[]{:S(2)}, u32[]{:S(2)}) %collective-permute-start.10) | collective-permute-done | bytes 262176 | tf_op jit(solution)/shard_map/ppermute | solution.py:360
  73.4 2.2 %collective-permute-done.9 = bf16[32,4096]{1,0:T(8,128)(2,1)S(1)} collective-permute-done((bf16[32,4096]{1,0:T(8,128)(2,1)S(1)}, bf16[32,4096]{1,0:T(8,128)(2,1)S(1)}, u32[]{:S(2)}, u32[]{:S(2)}) %collective-permute-start.9) | collective-permute-done | bytes 262176 | tf_op jit(solution)/shard_map/ppermute | solution.py:360
  75.7 1.2 collective-permute-start.14
  77.0 2.3 %collective-permute-start.16 = (bf16[32,4096]{1,0:T(8,128)(2,1)S(1)}, bf16[32,4096]{1,0:T(8,128)(2,1)S(1)}, u32[]{:S(2)}, u32[]{:S(2)}) collective-permute-start(bf16[32,4096]{1,0:T(8,128)(2,1)S(1)} %add_convert_fusion.3.refs_9_), channel_id=1, source_target_pairs={{0,16},{1,13},{2,18},{3,15},{4,20},{5,1},{6,22},{7,3},{8,24},{9,5}... | collective-permute-start | bytes 786440 | tf_op jit(solution)/shard_map/ppermute | solution.py:360
  79.3 10.2 %collective-permute-start.18 = (bf16[32,4096]{1,0:T(8,128)(2,1)S(1)}, bf16[32,4096]{1,0:T(8,128)(2,1)S(1)}, u32[]{:S(2)}, u32[]{:S(2)}) collective-permute-start(bf16[32,4096]{1,0:T(8,128)(2,1)S(1)} %get-tuple-element.74), channel_id=1, source_target_pairs={{0,1},{1,0},{2,3},{3,2},{4,5},{5,4},{6,7},{7,6},{8,9},{9,8},{10,11... | collective-permute-start | bytes 786440 | tf_op jit(solution)/shard_map/ppermute | solution.py:360
  89.6 1.7 collective-permute-start.20
  91.4 8.3 %gate_up.12 = (bf16[128,4224]{1,0:T(8,128)(2,1)S(1)}, bf16[128,4096]{1,0:T(8,128)(2,1)S(1)}) custom-call(bf16[512,3584]{1,0:T(8,128)(2,1)S(1)} %get-tuple-element.48.refs_0_, bf16[512,3584]{1,0:T(8,128)(2,1)S(1)} %get-tuple-element.49.refs_1_, bf16[512,3584]{1,0:T(8,128)(2,1)S(1)} %get-tuple-element.50.refs_2_, ...), custom_call_target="tpu_custom_call" | custom-call | flops 1431655808 | bytes 5592405 | tf_op jit(solution)/shard_map/gate_up/pallas_call | solution.py:137
  99.7 0.3 collective-permute-start.17
  100.0 6.3 %gate_up.13.refs_8_.refs_1_ = bf16[128,3072]{1,0:T(8,128)(2,1)S(1)} custom-call(bf16[512,3584]{1,0:T(8,128)(2,1)S(1)} %get-tuple-element.48.refs_0_, bf16[512,3584]{1,0:T(8,128)(2,1)S(1)} %get-tuple-element.49.refs_1_, bf16[512,3584]{1,0:T(8,128)(2,1)S(1)} %get-tuple-element.50.refs_2_, bf16[512,3584]{1,0:T(8,128)(2,1)S(1)} %get-tuple-element.51.refs_3_, ...), custom_call_target="tpu_custom_call" | custom-call | flops 1073741824 | bytes 4194304 | tf_op jit(solution)/shard_map/gate_up/pallas_call | solution.py:137
  106.6 0.6 collective-permute-start.22
  107.1 1.6 collective-permute-start.23
  108.7 1.3 collective-permute-start.24
  110.0 1.2 collective-permute-start.25
  111.2 2.8 %collective-permute-done.17.refs_10_ = bf16[128,4224]{1,0:T(8,128)(2,1)S(1)} collective-permute-done((bf16[128,4224]{1,0:T(8,128)(2,1)S(1)}, bf16[128,4224]{1,0:T(8,128)(2,1)S(1)}, u32[]{:S(2)}, u32[]{:S(2)}) %collective-permute-start.17) | collective-permute-done | bytes 1081376 | tf_op jit(solution)/shard_map/ppermute | solution.py:360
  114.1 6.7 %down.12 = (f32[128,4096]{1,0:T(8,128)S(1)}, f32[128,128]{1,0:T(8,128)S(1)}) custom-call(bf16[512,3584]{1,0:T(8,128)(2,1)S(1)} %get-tuple-element.48.refs_0_, bf16[512,3584]{1,0:T(8,128)(2,1)S(1)} %get-tuple-element.49.refs_1_, bf16[512,3584]{1,0:T(8,128)(2,1)S(1)} %get-tuple-element.50.refs_2_, bf16[512,3584]{1,0:T(8,128)(2,1)S(1)} %get-tuple-element.51.refs_3_, ...), custom_call_target="tpu_custom_call" | custom-call | flops 2147483648 | bytes 16777216 | tf_op jit(solution)/shard_map/down/pallas_call | solution.py:137
  120.8 8.7 %gate_up.14 = (bf16[128,4224]{1,0:T(8,128)(2,1)S(1)}, bf16[128,4096]{1,0:T(8,128)(2,1)S(1)}) custom-call(bf16[512,3584]{1,0:T(8,128)(2,1)S(1)} %get-tuple-element.48.refs_0_, bf16[512,3584]{1,0:T(8,128)(2,1)S(1)} %get-tuple-element.49.refs_1_, bf16[512,3584]{1,0:T(8,128)(2,1)S(1)} %get-tuple-element.50.refs_2_, ...), custom_call_target="tpu_custom_call" | custom-call | flops 4294967296 | bytes 16777216 | tf_op jit(solution)/shard_map/gate_up/pallas_call | solution.py:137
  129.5 0.3 collective-permute-start.29
  129.8 6.3 %gate_up.15.refs_0_.refs_1_ = bf16[128,3072]{1,0:T(8,128)(2,1)S(1)} custom-call(bf16[512,3584]{1,0:T(8,128)(2,1)S(1)} %get-tuple-element.48.refs_0_, bf16[512,3584]{1,0:T(8,128)(2,1)S(1)} %get-tuple-element.49.refs_1_, bf16[512,3584]{1,0:T(8,128)(2,1)S(1)} %get-tuple-element.50.refs_2_, bf16[512,3584]{1,0:T(8,128)(2,1)S(1)} %get-tuple-element.51.refs_3_, ...), custom_call_target="tpu_custom_call" | custom-call | flops 3221225472 | bytes 12582912 | tf_op jit(solution)/shard_map/gate_up/pallas_call | solution.py:137
  136.1 1.3 collective-permute-start.30
  137.4 1.6 copy-done.1
  139.0 6.5 %down.13 = (bf16[32,4096]{1,0:T(8,128)(2,1)S(1)}, bf16[32,4096]{1,0:T(8,128)(2,1)S(1)}, bf16[32,4096]{1,0:T(8,128)(2,1)S(1)}, bf16[32,4096]{1,0:T(8,128)(2,1)S(1)}) custom-call(bf16[128,3072]{1,0:T(8,128)(2,1)S(1)} %gate_up.15.refs_0_.refs_1_, bf16[128,3072]{1,0:T(8,128)(2,1)S(1)} %gate_up.13.refs_8_.refs_1_, ...), custom_call_target="tpu_custom_call" | custom-call | flops 1610612736 | bytes 12582912 | tf_op jit(solution)/shard_map/down/pallas_call | solution.py:137
  145.5 1.9 %collective-permute-start.26 = (bf16[32,4096]{1,0:T(8,128)(2,1)S(1)}, bf16[32,4096]{1,0:T(8,128)(2,1)S(1)}, u32[]{:S(2)}, u32[]{:S(2)}) collective-permute-start(bf16[32,4096]{1,0:T(8,128)(2,1)S(1)} %get-tuple-element.81), channel_id=1, source_target_pairs={{0,16},{1,13},{2,18},{3,15},{4,20},{5,1},{6,22},{7,3},{8,24},{9,5}... | collective-permute-start | bytes 786440 | tf_op jit(solution)/shard_map/ppermute | solution.py:360
  147.4 0.5 collective-permute-start.27
  147.8 0.2 collective-permute-start.28
  148.2 7.9 %down.14 = (f32[128,4096]{1,0:T(8,128)S(1)}, f32[128,128]{1,0:T(8,128)S(1)}) custom-call(bf16[32,4096]{1,0:T(8,128)(2,1)S(1)} %get-tuple-element.83.refs_0_, bf16[128,4224]{1,0:T(8,128)(2,1)S(1)} %get-tuple-element.84.refs_1_, bf16[128,4224]{1,0:T(8,128)(2,1)} %collective-permute-done.29.refs_2_, bf16[1,3584,4096]{2,1,0:T(8,128)(2,1)} %refs_3_.5), custom_call_target="tpu_custom_call" | custom-call | flops 214748368 | bytes 1677721 | tf_op jit(solution)/shard_map/down/pallas_call | solution.py:137
  156.1 6.5 %down.15 = (bf16[32,4096]{1,0:T(8,128)(2,1)S(1)}, bf16[32,4096]{1,0:T(8,128)(2,1)S(1)}, bf16[32,4096]{1,0:T(8,128)(2,1)S(1)}, bf16[32,4096]{1,0:T(8,128)(2,1)S(1)}) custom-call(f32[128,128]{1,0:T(8,128)S(1)} %get-tuple-element.85.refs_0_.refs_4_, bf16[128,3072]{1,0:T(8,128)(2,1)S(1)} %gate_up.15.refs_0_.refs_1_, ...), custom_call_target="tpu_custom_call" | custom-call | flops 161061280 | bytes 1258291 | tf_op jit(solution)/shard_map/down/pallas_call | solution.py:137
  162.7 3.1 %collective-permute-start.31 = (bf16[32,4096]{1,0:T(8,128)(2,1)S(1)}, bf16[32,4096]{1,0:T(8,128)(2,1)S(1)}, u32[]{:S(2)}, u32[]{:S(2)}) collective-permute-start(bf16[32,4096]{1,0:T(8,128)(2,1)S(1)} %get-tuple-element.88), channel_id=1, source_target_pairs={{0,16},{1,13},{2,18},{3,15},{4,20},{5,1},{6,22},{7,3},{8,24},{9,5}... | collective-permute-start | bytes 786440 | tf_op jit(solution)/shard_map/ppermute | solution.py:360
  165.9 0.3 collective-permute-start.33
  166.3 2.8 %collective-permute-done.31 = bf16[32,4096]{1,0:T(8,128)(2,1)S(1)} collective-permute-done((bf16[32,4096]{1,0:T(8,128)(2,1)S(1)}, bf16[32,4096]{1,0:T(8,128)(2,1)S(1)}, u32[]{:S(2)}, u32[]{:S(2)}) %collective-permute-start.31) | collective-permute-done | bytes 262176 | tf_op jit(solution)/shard_map/ppermute | solution.py:360
  169.1 8.9 %collective-permute-done.32 = bf16[32,4096]{1,0:T(8,128)(2,1)S(1)} collective-permute-done((bf16[32,4096]{1,0:T(8,128)(2,1)S(1)}, bf16[32,4096]{1,0:T(8,128)(2,1)S(1)}, u32[]{:S(2)}, u32[]{:S(2)}) %collective-permute-start.32) | collective-permute-done | bytes 262176 | tf_op jit(solution)/shard_map/ppermute | solution.py:360
  178.2 0.9 fusion
  (54 shorter events, 1.7 us)
Async XLA Ops:
  1.1 13.1 %copy-start.2 = (f32[1,4096]{1,0:T(1,128)S(1)}, f32[1,4096]{1,0:T(1,128)}, u32[]{:S(2)}) copy-start(f32[1,4096]{1,0:T(1,128)} %refs_10_.7) | copy-start | bytes 49156
  1.1 13.1 %collective-permute-start = (bf16[32,4096]{1,0:T(8,128)(2,1)S(1)}, bf16[32,4096]{1,0:T(8,128)(2,1)S(1)}, u32[]{:S(2)}, u32[]{:S(2)}) collective-permute-start(bf16[32,4096]{1,0:T(8,128)(2,1)S(1)} %get-tuple-element.92.refs_9_), channel_id=1, source_target_pairs={{0,4},{1,17},{2,6},{3,19},{4,8},{5,21},{6,10},{7,23},{8,12},{9,25}... | collective-permute-start | bytes 786440 | tf_op jit(solution)/shard_map/ppermute | solution.py:360
  3.2 11.0 %collective-permute-start.1 = (bf16[32,4096]{1,0:T(8,128)(2,1)S(1)}, bf16[32,4096]{1,0:T(8,128)(2,1)S(1)}, u32[]{:S(2)}, u32[]{:S(2)}) collective-permute-start(bf16[32,4096]{1,0:T(8,128)(2,1)S(1)} %get-tuple-element.92.refs_9_), channel_id=1, source_target_pairs={{0,8},{1,17},{2,10},{3,19},{4,12},{5,21},{6,14},{7,23},{8,0},{9,25... | collective-permute-start | bytes 786440 | tf_op jit(solution)/shard_map/ppermute | solution.py:360
  3.3 10.9 %collective-permute-start.2 = (bf16[32,4096]{1,0:T(8,128)(2,1)S(1)}, bf16[32,4096]{1,0:T(8,128)(2,1)S(1)}, u32[]{:S(2)}, u32[]{:S(2)}) collective-permute-start(bf16[32,4096]{1,0:T(8,128)(2,1)S(1)} %get-tuple-element.92.refs_9_), channel_id=1, source_target_pairs={{0,12},{1,17},{2,14},{3,19},{4,0},{5,21},{6,2},{7,23},{8,4},{9,25}... | collective-permute-start | bytes 786440 | tf_op jit(solution)/shard_map/ppermute | solution.py:360
  14.3 5.3 %collective-permute-start.3 = (bf16[32,4096]{1,0:T(8,128)(2,1)S(1)}, bf16[32,4096]{1,0:T(8,128)(2,1)S(1)}, u32[]{:S(2)}, u32[]{:S(2)}) collective-permute-start(bf16[32,4096]{1,0:T(8,128)(2,1)S(1)} %get-tuple-element.57.refs_9_), channel_id=1, source_target_pairs={{0,4},{1,17},{2,6},{3,19},{4,8},{5,21},{6,10},{7,23},{8,12},{9,25}... | collective-permute-start | bytes 786440 | tf_op jit(solution)/shard_map/ppermute | solution.py:360
  14.4 7.9 %collective-permute-start.4 = (bf16[32,4096]{1,0:T(8,128)(2,1)S(1)}, bf16[32,4096]{1,0:T(8,128)(2,1)S(1)}, u32[]{:S(2)}, u32[]{:S(2)}) collective-permute-start(bf16[32,4096]{1,0:T(8,128)(2,1)S(1)} %get-tuple-element.57.refs_9_), channel_id=1, source_target_pairs={{0,8},{1,17},{2,10},{3,19},{4,12},{5,21},{6,14},{7,23},{8,0},{9,25... | collective-permute-start | bytes 786440 | tf_op jit(solution)/shard_map/ppermute | solution.py:360
  15.8 9.4 %collective-permute-start.5 = (bf16[32,4096]{1,0:T(8,128)(2,1)S(1)}, bf16[32,4096]{1,0:T(8,128)(2,1)S(1)}, u32[]{:S(2)}, u32[]{:S(2)}) collective-permute-start(bf16[32,4096]{1,0:T(8,128)(2,1)S(1)} %get-tuple-element.57.refs_9_), channel_id=1, source_target_pairs={{0,12},{1,17},{2,14},{3,19},{4,0},{5,21},{6,2},{7,23},{8,4},{9,25}... | collective-permute-start | bytes 786440 | tf_op jit(solution)/shard_map/ppermute | solution.py:360
  15.9 21.1 %collective-permute-start.6 = (bf16[128,4224]{1,0:T(8,128)(2,1)S(1)}, bf16[128,4224]{1,0:T(8,128)(2,1)S(1)}, u32[]{:S(2)}, u32[]{:S(2)}) collective-permute-start(bf16[128,4224]{1,0:T(8,128)(2,1)S(1)} %get-tuple-element.59.refs_9_), channel_id=1, source_target_pairs={{0,2},{1,17},{2,0},{3,19},{4,6},{5,21},{6,4},{7,23},{8,10},{9,25},... | collective-permute-start | bytes 3244040 | tf_op jit(solution)/shard_map/ppermute | solution.py:360
  17.3 28.2 %collective-permute-start.7 = (bf16[128,3072]{1,0:T(8,128)(2,1)S(1)}, bf16[128,3072]{1,0:T(8,128)(2,1)S(1)}, u32[]{:S(2)}, u32[]{:S(2)}) collective-permute-start(bf16[128,3072]{1,0:T(8,128)(2,1)S(1)} %gate_up.9.refs_8_.refs_9_), channel_id=1, source_target_pairs={{0,2},{1,17},{2,0},{3,19},{4,6},{5,21},{6,4},{7,23},{8,10},{9,25},... | collective-permute-start | bytes 2359304 | tf_op jit(solution)/shard_map/ppermute | solution.py:360
  25.2 40.0 %collective-permute-start.12 = (bf16[128,4224]{1,0:T(8,128)(2,1)S(1)}, bf16[128,4224]{1,0:T(8,128)(2,1)S(1)}, u32[]{:S(2)}, u32[]{:S(2)}) collective-permute-start(bf16[128,4224]{1,0:T(8,128)(2,1)S(1)} %get-tuple-element.66.refs_9_), channel_id=1, source_target_pairs={{0,2},{1,17},{2,0},{3,19},{4,6},{5,21},{6,4},{7,23},{8,10},{9,25},... | collective-permute-start | bytes 3244040 | tf_op jit(solution)/shard_map/ppermute | solution.py:360
  45.5 27.8 %collective-permute-start.10 = (bf16[32,4096]{1,0:T(8,128)(2,1)S(1)}, bf16[32,4096]{1,0:T(8,128)(2,1)S(1)}, u32[]{:S(2)}, u32[]{:S(2)}) collective-permute-start(bf16[32,4096]{1,0:T(8,128)(2,1)S(1)} %get-tuple-element.64), channel_id=1, source_target_pairs={{0,9},{1,0},{2,11},{3,2},{4,13},{5,4},{6,15},{7,6},{8,1},{9,8},{10... | collective-permute-start | bytes 786440 | tf_op jit(solution)/shard_map/ppermute | solution.py:360
  61.6 11.7 %collective-permute-start.11 = (bf16[32,4096]{1,0:T(8,128)(2,1)S(1)}, bf16[32,4096]{1,0:T(8,128)(2,1)S(1)}, u32[]{:S(2)}, u32[]{:S(2)}) collective-permute-start(bf16[32,4096]{1,0:T(8,128)(2,1)S(1)} %get-tuple-element.65.refs_8_), channel_id=1, source_target_pairs={{0,5},{1,0},{2,7},{3,2},{4,9},{5,4},{6,11},{7,6},{8,13},{9,8},{10,... | collective-permute-start | bytes 786440 | tf_op jit(solution)/shard_map/ppermute | solution.py:360
  61.7 11.7 %collective-permute-start.8 = (bf16[32,4096]{1,0:T(8,128)(2,1)S(1)}, bf16[32,4096]{1,0:T(8,128)(2,1)S(1)}, u32[]{:S(2)}, u32[]{:S(2)}) collective-permute-start(bf16[32,4096]{1,0:T(8,128)(2,1)S(1)} %get-tuple-element.62), channel_id=1, source_target_pairs={{0,1},{1,0},{2,3},{3,2},{4,5},{5,4},{6,7},{7,6},{8,9},{9,8},{10,11... | collective-permute-start | bytes 786440 | tf_op jit(solution)/shard_map/ppermute | solution.py:360
  65.1 10.5 %collective-permute-start.9 = (bf16[32,4096]{1,0:T(8,128)(2,1)S(1)}, bf16[32,4096]{1,0:T(8,128)(2,1)S(1)}, u32[]{:S(2)}, u32[]{:S(2)}) collective-permute-start(bf16[32,4096]{1,0:T(8,128)(2,1)S(1)} %get-tuple-element.63), channel_id=1, source_target_pairs={{0,13},{1,0},{2,15},{3,2},{4,1},{5,4},{6,3},{7,6},{8,5},{9,8},{10,... | collective-permute-start | bytes 786440 | tf_op jit(solution)/shard_map/ppermute | solution.py:360
  65.1 10.4 %copy-start.3 = (bf16[2,32,4096]{2,1,0:T(8,128)(2,1)S(1)}, bf16[2,32,4096]{2,1,0:T(8,128)(2,1)}, u32[]{:S(2)}) copy-start(bf16[2,32,4096]{2,1,0:T(8,128)(2,1)} %param.5) | copy-start | bytes 1572868
  65.1 14.1 %collective-permute-start.13 = (bf16[128,3072]{1,0:T(8,128)(2,1)S(1)}, bf16[128,3072]{1,0:T(8,128)(2,1)S(1)}, u32[]{:S(2)}, u32[]{:S(2)}) collective-permute-start(bf16[128,3072]{1,0:T(8,128)(2,1)S(1)} %gate_up.11.refs_8_.refs_9_), channel_id=1, source_target_pairs={{0,2},{1,17},{2,0},{3,19},{4,6},{5,21},{6,4},{7,23},{8,10},{9,25},... | collective-permute-start | bytes 2359304 | tf_op jit(solution)/shard_map/ppermute | solution.py:360
  75.7 13.8 %collective-permute-start.14 = (bf16[32,4096]{1,0:T(8,128)(2,1)S(1)}, bf16[32,4096]{1,0:T(8,128)(2,1)S(1)}, u32[]{:S(2)}, u32[]{:S(2)}) collective-permute-start(bf16[32,4096]{1,0:T(8,128)(2,1)S(1)} %add_convert_fusion.3.refs_9_), channel_id=1, source_target_pairs={{0,16},{1,5},{2,18},{3,7},{4,20},{5,9},{6,22},{7,11},{8,24},{9,13}... | collective-permute-start | bytes 786440 | tf_op jit(solution)/shard_map/ppermute | solution.py:360
  76.9 14.4 %collective-permute-start.15 = (bf16[32,4096]{1,0:T(8,128)(2,1)S(1)}, bf16[32,4096]{1,0:T(8,128)(2,1)S(1)}, u32[]{:S(2)}, u32[]{:S(2)}) collective-permute-start(bf16[32,4096]{1,0:T(8,128)(2,1)S(1)} %add_convert_fusion.3.refs_9_), channel_id=1, source_target_pairs={{0,16},{1,9},{2,18},{3,11},{4,20},{5,13},{6,22},{7,15},{8,24},{9,1... | collective-permute-start | bytes 786440 | tf_op jit(solution)/shard_map/ppermute | solution.py:360
  77.0 14.4 %collective-permute-start.16 = (bf16[32,4096]{1,0:T(8,128)(2,1)S(1)}, bf16[32,4096]{1,0:T(8,128)(2,1)S(1)}, u32[]{:S(2)}, u32[]{:S(2)}) collective-permute-start(bf16[32,4096]{1,0:T(8,128)(2,1)S(1)} %add_convert_fusion.3.refs_9_), channel_id=1, source_target_pairs={{0,16},{1,13},{2,18},{3,15},{4,20},{5,1},{6,22},{7,3},{8,24},{9,5}... | collective-permute-start | bytes 786440 | tf_op jit(solution)/shard_map/ppermute | solution.py:360
  79.3 27.0 %collective-permute-start.18 = (bf16[32,4096]{1,0:T(8,128)(2,1)S(1)}, bf16[32,4096]{1,0:T(8,128)(2,1)S(1)}, u32[]{:S(2)}, u32[]{:S(2)}) collective-permute-start(bf16[32,4096]{1,0:T(8,128)(2,1)S(1)} %get-tuple-element.74), channel_id=1, source_target_pairs={{0,1},{1,0},{2,3},{3,2},{4,5},{5,4},{6,7},{7,6},{8,9},{9,8},{10,11... | collective-permute-start | bytes 786440 | tf_op jit(solution)/shard_map/ppermute | solution.py:360
  89.5 16.9 %collective-permute-start.19 = (bf16[32,4096]{1,0:T(8,128)(2,1)S(1)}, bf16[32,4096]{1,0:T(8,128)(2,1)S(1)}, u32[]{:S(2)}, u32[]{:S(2)}) collective-permute-start(bf16[32,4096]{1,0:T(8,128)(2,1)S(1)} %get-tuple-element.75), channel_id=1, source_target_pairs={{0,13},{1,0},{2,15},{3,2},{4,1},{5,4},{6,3},{7,6},{8,5},{9,8},{10,... | collective-permute-start | bytes 786440 | tf_op jit(solution)/shard_map/ppermute | solution.py:360
  89.6 16.8 %collective-permute-start.20 = (bf16[32,4096]{1,0:T(8,128)(2,1)S(1)}, bf16[32,4096]{1,0:T(8,128)(2,1)S(1)}, u32[]{:S(2)}, u32[]{:S(2)}) collective-permute-start(bf16[32,4096]{1,0:T(8,128)(2,1)S(1)} %get-tuple-element.76), channel_id=1, source_target_pairs={{0,9},{1,0},{2,11},{3,2},{4,13},{5,4},{6,15},{7,6},{8,1},{9,8},{10... | collective-permute-start | bytes 786440 | tf_op jit(solution)/shard_map/ppermute | solution.py:360
  91.3 15.1 %collective-permute-start.21 = (bf16[32,4096]{1,0:T(8,128)(2,1)S(1)}, bf16[32,4096]{1,0:T(8,128)(2,1)S(1)}, u32[]{:S(2)}, u32[]{:S(2)}) collective-permute-start(bf16[32,4096]{1,0:T(8,128)(2,1)S(1)} %get-tuple-element.70.refs_8_), channel_id=1, source_target_pairs={{0,5},{1,0},{2,7},{3,2},{4,9},{5,4},{6,11},{7,6},{8,13},{9,8},{10,... | collective-permute-start | bytes 786440 | tf_op jit(solution)/shard_map/ppermute | solution.py:360
  99.7 14.4 %collective-permute-start.17 = (bf16[128,4224]{1,0:T(8,128)(2,1)S(1)}, bf16[128,4224]{1,0:T(8,128)(2,1)S(1)}, u32[]{:S(2)}, u32[]{:S(2)}) collective-permute-start(bf16[128,4224]{1,0:T(8,128)(2,1)S(1)} %get-tuple-element.72.refs_9_), channel_id=1, source_target_pairs={{0,16},{1,3},{2,18},{3,1},{4,20},{5,7},{6,22},{7,5},{8,24},{9,11},... | collective-permute-start | bytes 3244040 | tf_op jit(solution)/shard_map/ppermute | solution.py:360
  106.6 14.2 %collective-permute-start.22 = (bf16[32,4096]{1,0:T(8,128)(2,1)S(1)}, bf16[32,4096]{1,0:T(8,128)(2,1)S(1)}, u32[]{:S(2)}, u32[]{:S(2)}) collective-permute-start(bf16[32,4096]{1,0:T(8,128)(2,1)S(1)} %add_convert_fusion.2.refs_9_), channel_id=1, source_target_pairs={{0,16},{1,5},{2,18},{3,7},{4,20},{5,9},{6,22},{7,11},{8,24},{9,13}... | collective-permute-start | bytes 786440 | tf_op jit(solution)/shard_map/ppermute | solution.py:360
  107.1 13.6 %collective-permute-start.23 = (bf16[32,4096]{1,0:T(8,128)(2,1)S(1)}, bf16[32,4096]{1,0:T(8,128)(2,1)S(1)}, u32[]{:S(2)}, u32[]{:S(2)}) collective-permute-start(bf16[32,4096]{1,0:T(8,128)(2,1)S(1)} %add_convert_fusion.2.refs_9_), channel_id=1, source_target_pairs={{0,16},{1,9},{2,18},{3,11},{4,20},{5,13},{6,22},{7,15},{8,24},{9,1... | collective-permute-start | bytes 786440 | tf_op jit(solution)/shard_map/ppermute | solution.py:360
  108.7 12.1 %collective-permute-start.24 = (bf16[32,4096]{1,0:T(8,128)(2,1)S(1)}, bf16[32,4096]{1,0:T(8,128)(2,1)S(1)}, u32[]{:S(2)}, u32[]{:S(2)}) collective-permute-start(bf16[32,4096]{1,0:T(8,128)(2,1)S(1)} %add_convert_fusion.2.refs_9_), channel_id=1, source_target_pairs={{0,16},{1,13},{2,18},{3,15},{4,20},{5,1},{6,22},{7,3},{8,24},{9,5}... | collective-permute-start | bytes 786440 | tf_op jit(solution)/shard_map/ppermute | solution.py:360
  110.0 27.4 %collective-permute-start.25 = (bf16[128,3072]{1,0:T(8,128)(2,1)S(1)}, bf16[128,3072]{1,0:T(8,128)(2,1)}, u32[]{:S(2)}, u32[]{:S(2)}) collective-permute-start(bf16[128,3072]{1,0:T(8,128)(2,1)S(1)} %gate_up.13.refs_8_.refs_1_), channel_id=1, source_target_pairs={{0,16},{1,3},{2,18},{3,1},{4,20},{5,7},{6,22},{7,5},{8,24},{9,11},... | collective-permute-start | bytes 2359304 | tf_op jit(solution)/shard_map/ppermute | solution.py:360
  120.7 8.7 %copy-start = (f32[128,4096]{1,0:T(8,128)}, f32[128,4096]{1,0:T(8,128)S(1)}, u32[]{:S(2)}) copy-start(f32[128,4096]{1,0:T(8,128)S(1)} %get-tuple-element.79.refs_5_) | copy-start | bytes 6291460
  129.5 18.6 %collective-permute-start.29 = (bf16[128,4224]{1,0:T(8,128)(2,1)S(1)}, bf16[128,4224]{1,0:T(8,128)(2,1)}, u32[]{:S(2)}, u32[]{:S(2)}) collective-permute-start(bf16[128,4224]{1,0:T(8,128)(2,1)S(1)} %get-tuple-element.84.refs_1_), channel_id=1, source_target_pairs={{0,16},{1,3},{2,18},{3,1},{4,20},{5,7},{6,22},{7,5},{8,24},{9,11},... | collective-permute-start | bytes 3244040 | tf_op jit(solution)/shard_map/ppermute | solution.py:360
  136.1 20.0 %collective-permute-start.30 = (bf16[128,3072]{1,0:T(8,128)(2,1)S(1)}, bf16[128,3072]{1,0:T(8,128)(2,1)}, u32[]{:S(2)}, u32[]{:S(2)}) collective-permute-start(bf16[128,3072]{1,0:T(8,128)(2,1)S(1)} %gate_up.15.refs_0_.refs_1_), channel_id=1, source_target_pairs={{0,16},{1,3},{2,18},{3,1},{4,20},{5,7},{6,22},{7,5},{8,24},{9,11},... | collective-permute-start | bytes 2359304 | tf_op jit(solution)/shard_map/ppermute | solution.py:360
  137.4 1.6 copy-start.1
  145.5 20.3 %collective-permute-start.26 = (bf16[32,4096]{1,0:T(8,128)(2,1)S(1)}, bf16[32,4096]{1,0:T(8,128)(2,1)S(1)}, u32[]{:S(2)}, u32[]{:S(2)}) collective-permute-start(bf16[32,4096]{1,0:T(8,128)(2,1)S(1)} %get-tuple-element.81), channel_id=1, source_target_pairs={{0,16},{1,13},{2,18},{3,15},{4,20},{5,1},{6,22},{7,3},{8,24},{9,5}... | collective-permute-start | bytes 786440 | tf_op jit(solution)/shard_map/ppermute | solution.py:360
  147.4 18.5 %collective-permute-start.27 = (bf16[32,4096]{1,0:T(8,128)(2,1)S(1)}, bf16[32,4096]{1,0:T(8,128)(2,1)S(1)}, u32[]{:S(2)}, u32[]{:S(2)}) collective-permute-start(bf16[32,4096]{1,0:T(8,128)(2,1)S(1)} %get-tuple-element.82), channel_id=1, source_target_pairs={{0,16},{1,9},{2,18},{3,11},{4,20},{5,13},{6,22},{7,15},{8,24},{9,1... | collective-permute-start | bytes 786440 | tf_op jit(solution)/shard_map/ppermute | solution.py:360
  147.8 18.3 %collective-permute-start.28 = (bf16[32,4096]{1,0:T(8,128)(2,1)S(1)}, bf16[32,4096]{1,0:T(8,128)(2,1)S(1)}, u32[]{:S(2)}, u32[]{:S(2)}) collective-permute-start(bf16[32,4096]{1,0:T(8,128)(2,1)S(1)} %get-tuple-element.83.refs_0_), channel_id=1, source_target_pairs={{0,16},{1,5},{2,18},{3,7},{4,20},{5,9},{6,22},{7,11},{8,24},{9,13}... | collective-permute-start | bytes 786440 | tf_op jit(solution)/shard_map/ppermute | solution.py:360
  148.1 30.1 %collective-permute-start.34 = (bf16[2,32,4096]{2,1,0:T(8,128)(2,1)S(1)}, bf16[2,32,4096]{2,1,0:T(8,128)(2,1)S(1)}, u32[]{:S(2)}, u32[]{:S(2)}) collective-permute-start(bf16[2,32,4096]{2,1,0:T(8,128)(2,1)S(1)} %pad_maximum_fusion), channel_id=1, source_target_pairs={{0,1},{1,0},{2,3},{3,2},{4,5},{5,4},{6,7},{7,6},{8,9},{9,8},{10,11... | collective-permute-start | bytes 1572872 | tf_op jit(solution)/shard_map/ppermute | solution.py:360
  162.7 6.5 %collective-permute-start.31 = (bf16[32,4096]{1,0:T(8,128)(2,1)S(1)}, bf16[32,4096]{1,0:T(8,128)(2,1)S(1)}, u32[]{:S(2)}, u32[]{:S(2)}) collective-permute-start(bf16[32,4096]{1,0:T(8,128)(2,1)S(1)} %get-tuple-element.88), channel_id=1, source_target_pairs={{0,16},{1,13},{2,18},{3,15},{4,20},{5,1},{6,22},{7,3},{8,24},{9,5}... | collective-permute-start | bytes 786440 | tf_op jit(solution)/shard_map/ppermute | solution.py:360
  165.8 12.3 %collective-permute-start.32 = (bf16[32,4096]{1,0:T(8,128)(2,1)S(1)}, bf16[32,4096]{1,0:T(8,128)(2,1)S(1)}, u32[]{:S(2)}, u32[]{:S(2)}) collective-permute-start(bf16[32,4096]{1,0:T(8,128)(2,1)S(1)} %get-tuple-element.89), channel_id=1, source_target_pairs={{0,16},{1,9},{2,18},{3,11},{4,20},{5,13},{6,22},{7,15},{8,24},{9,1... | collective-permute-start | bytes 786440 | tf_op jit(solution)/shard_map/ppermute | solution.py:360
  165.9 12.2 %collective-permute-start.33 = (bf16[32,4096]{1,0:T(8,128)(2,1)S(1)}, bf16[32,4096]{1,0:T(8,128)(2,1)S(1)}, u32[]{:S(2)}, u32[]{:S(2)}) collective-permute-start(bf16[32,4096]{1,0:T(8,128)(2,1)S(1)} %get-tuple-element.90), channel_id=1, source_target_pairs={{0,16},{1,5},{2,18},{3,7},{4,20},{5,9},{6,22},{7,11},{8,24},{9,13}... | collective-permute-start | bytes 786440 | tf_op jit(solution)/shard_map/ppermute | solution.py:360
